TPU v7x, 768 devices: a whole 4x8x12 slice. The times are simulated.
768 devices in a mesh: blk: 128 (over z_hi, x, y), col: 6 (over z_lo, core).
Axes of the slice: x: 4, y: 8, z: 12 (z_hi: 4, z_lo: 3; z = z_hi * 3 + z_lo), core: 2. Of those that a mesh axis runs over, the one named last changes fastest.
Arguments:
- psi: bfloat16 [256, 384, 384], P('blk', 'col')
- dims: int32 [256], P('blk'), may hold values from 192 to 384, as said below
- pattern: int32 [256, 5], P('blk'), may hold values 0 or 1
- left_env: bfloat16 [256, 12, 384, 384], P('blk', 'col')
- right_env: bfloat16 [12, 384, 384], P('col')
Outputs:
- sigma_first: float32 [256, 384, 384], P('blk', 'col')
- sigma_second: float32 [256, 384, 384], P('blk', 'col')
Inputs may be any that keep to these rules, and one draw needn't show every extreme that they name: dims[s] lies between 192 and 384.
All inputs are finite; a program needn't handle non-finite values. No bound on the sum of `pattern` on one device may be relied on, other than what follows from the above.
Results may differ from a plain program's by a relative error of at most 0.022.
Values may be sent and summed in bfloat16 or wider, within the bound.
No kernel may reach another device: no remote copies, remote signals or barrier semaphores. Data moves between devices by JAX's collectives and lax.ppermute only.
A program may use at most 32 MiB of HBM per device.

v0:
```python
import jax
import jax.numpy as jnp
from jax import lax
from jax.sharding import PartitionSpec as P

W_COL = 2


def with_halo(block, sides, width):
    for axis, dim in sides:
        count = lax.axis_size(axis)
        forward = [(i, i + 1) for i in range(count - 1)]
        backward = [(target, source) for source, target in forward]
        low = lax.ppermute(
            lax.slice_in_dim(block, block.shape[dim] - width, None, axis=dim), axis, forward
        )
        high = lax.ppermute(lax.slice_in_dim(block, 0, width, axis=dim), axis, backward)
        block = jnp.concatenate([low, block, high], axis=dim)
    return block


def combine_blocks(padded, pattern, sectors):
    coeff = pattern.astype(jnp.float32)
    total = jnp.zeros((sectors,) + padded.shape[1:], jnp.float32)
    for offset in range(pattern.shape[1]):
        total = total + coeff[:, offset, None, None] * padded[offset : offset + sectors].astype(
            jnp.float32
        )
    return total.astype(jnp.bfloat16)


def apply_hamiltonian(vector, pattern, left_env, right_env, mask, scale):
    sectors = vector.shape[0]
    full = lax.all_gather(vector, "col", axis=1, tiled=True)
    padded = with_halo(full, (("blk", 0),), 2)
    combined = combine_blocks(padded, pattern, sectors)
    temp = jnp.einsum(
        "swab,sbc->swac", left_env, combined, preferred_element_type=jnp.float32
    ).astype(jnp.bfloat16)
    partial_term = jnp.einsum("swac,wdc->sad", temp, right_env, preferred_element_type=jnp.float32)
    summed = lax.psum_scatter(
        partial_term.astype(jnp.bfloat16), "col", scatter_dimension=1, tiled=True
    ).astype(jnp.float32)
    return jnp.where(mask, summed * scale, jnp.float32(0.0))


def body(psi, dims, pattern, left_env, right_env):
    rows = psi.shape[1]
    width = psi.shape[2]
    row_ids = lax.axis_index("col") * rows + jnp.arange(rows, dtype=jnp.int32)
    col_ids = jnp.arange(width, dtype=jnp.int32)
    mask = (row_ids[None, :, None] < dims[:, None, None]) & (
        col_ids[None, None, :] < dims[:, None, None]
    )
    psi_m = jnp.where(mask, psi, jnp.zeros_like(psi))
    scale = 1.0 / jnp.sqrt(jnp.float32(W_COL * lax.axis_size("col")))
    sigma_first = apply_hamiltonian(psi_m, pattern, left_env, right_env, mask, scale)
    psi_float = psi_m.astype(jnp.float32)
    numerator, denominator = lax.psum(
        (jnp.sum(psi_float * sigma_first), jnp.sum(psi_float * psi_float)), ("blk", "col")
    )
    theta = numerator / denominator
    resid = (sigma_first - theta * psi_float).astype(jnp.bfloat16)
    sigma_second = apply_hamiltonian(resid, pattern, left_env, right_env, mask, scale)
    return (sigma_first, sigma_second)


def solution(mesh):
    return jax.shard_map(
        body,
        mesh=mesh,
        in_specs=(
            P("blk", "col", None),
            P("blk"),
            P("blk", None),
            P("blk", "col", None, None),
            P("col", None, None),
        ),
        out_specs=(P("blk", "col", None), P("blk", "col", None)),
        check_vma=False,
    )
```

profile of v0, /device:TPU:1, one launch (start us, length us, event | category | flops | bytes accessed | tf_op | source)
XLA Modules:
  0.0 331.4 jit_solution(18401237043447781209)
XLA Ops:
  7.2 0.0 copy-start
  7.2 0.0 reduce-scatter.3.cloned.1.call-start
  7.2 0.8 iota_compare_fusion
  8.1 0.7 broadcast_compare_fusion
  8.8 1.0 and_select_fusion.2
  9.8 20.2 %all_gather.6 = bf16[2,384,384]{2,1,0:T(8,128)(2,1)S(1)} all-gather(bf16[2,64,384]{2,1,0:T(8,128)(2,1)S(1)} %and_select_fusion.2), channel_id=1, replica_groups=mesh['blk'=128,'col'=6] {'col'}, dimensions={1}, use_global_device_ids=true | all-gather | bytes 688128 | tf_op jit(solution)/shard_map/all_gather | solution.py:34
  29.9 1.3 collective-permute-start.1
  31.2 4.0 %collective-permute-start = (bf16[2,384,384]{2,1,0:T(8,128)(2,1)S(1)}, bf16[2,384,384]{2,1,0:T(8,128)(2,1)S(1)}, u32[]{:S(2)}, u32[]{:S(2)}) collective-permute-start(bf16[2,384,384]{2,1,0:T(8,128)(2,1)S(1)} %all_gather.6), channel_id=1, source_target_pairs={{0,6},{6,12},{12,18},{18,24},{24,30},{30,36},{36,42},{42,48},{48,5... | collective-permute-start | bytes 1769480 | tf_op jit(solution)/shard_map/ppermute | solution.py:14
  35.3 0.7 convert_element_type.70
  35.9 0.2 slice_reduce_fusion.4
  36.2 10.4 %collective-permute-done.1 = bf16[2,384,384]{2,1,0:T(8,128)(2,1)S(1)} collective-permute-done((bf16[2,384,384]{2,1,0:T(8,128)(2,1)S(1)}, bf16[2,384,384]{2,1,0:T(8,128)(2,1)S(1)}, u32[]{:S(2)}, u32[]{:S(2)}) %collective-permute-start.1) | collective-permute-done | bytes 589856 | tf_op jit(solution)/shard_map/ppermute | solution.py:17
  46.6 0.9 collective-permute-done
  47.5 0.0 copy-done
  47.5 3.8 %fusion.2 = bf16[2,384,384]{2,1,0:T(8,128)(2,1)} fusion(bf16[2,2,384,384]{3,2,1,0:T(8,128)(2,1)S(1)} %copy-done, bf16[2,384,384]{2,1,0:T(8,128)(2,1)} %param.9, bf16[2,384,384]{2,1,0:T(8,128)(2,1)S(1)} %collective-permute-done.1, bf16[2,384,384]{2,1,0:T(8,128)(2,1)S(1)} %all_gather.6, bf16[2,384,384]{2,1,0:T(8,128)(2,1)S(1)} %collective-permute-done, ...), kind=kOutput, calls=%fused_computation.6 | convolution fusion | flops 913047552 | bytes 4128808 | tf_op jit(solution)/shard_map/swac,wdc->sad/dot_general | solution.py:40
  51.3 0.0 reduce-scatter.3.cloned.1.call-update
  51.3 0.0 reduce-scatter.5.cloned.1.call-start
  51.4 63.3 %reduce-scatter.3.cloned.1.call-done = bf16[2,64,384]{2,1,0:T(8,128)(2,1)} async-done(((bf16[2,384,384]{2,1,0:T(8,128)(2,1)}), bf16[2,64,384]{2,1,0:T(8,128)(2,1)}) %reduce-scatter.3.cloned.1.call-update) | async-done | bytes 98320 | tf_op jit(solution)/shard_map/reduce_scatter | solution.py:41
  114.6 0.0 copy-done.1
  114.7 1.7 fusion.27
  116.4 113.2 %all-reduce = (f32[]{:T(128)}, f32[]{:T(128)}) all-reduce(f32[]{:T(128)} %get-tuple-element.3, f32[]{:T(128)} %get-tuple-element.2), channel_id=1, replica_groups=mesh['blk'=128,'col'=6] {'blk','col'}, use_global_device_ids=true, to_apply=%region_2.3 | all-reduce | flops 2 | bytes 16 | tf_op jit(solution)/shard_map/psum | solution.py:59
  230.8 0.1 fusion.29
  231.0 11.2 %all_gather.7 = bf16[2,384,384]{2,1,0:T(8,128)(2,1)S(1)} all-gather(bf16[2,64,384]{2,1,0:T(8,128)(2,1)S(1)} %fusion.29), channel_id=1, replica_groups=mesh['blk'=128,'col'=6] {'col'}, dimensions={1}, use_global_device_ids=true | all-gather | bytes 688128 | tf_op jit(solution)/shard_map/all_gather | solution.py:34
  242.2 1.3 collective-permute-start.3
  243.5 4.8 %collective-permute-start.2 = (bf16[2,384,384]{2,1,0:T(8,128)(2,1)S(1)}, bf16[2,384,384]{2,1,0:T(8,128)(2,1)}, u32[]{:S(2)}, u32[]{:S(2)}) collective-permute-start(bf16[2,384,384]{2,1,0:T(8,128)(2,1)S(1)} %all_gather.7), channel_id=1, source_target_pairs={{0,6},{6,12},{12,18},{18,24},{24,30},{30,36},{36,42},{42,48},{48,5... | collective-permute-start | bytes 1769480 | tf_op jit(solution)/shard_map/ppermute | solution.py:14
  248.3 10.6 %collective-permute-done.3 = bf16[2,384,384]{2,1,0:T(8,128)(2,1)S(1)} collective-permute-done((bf16[2,384,384]{2,1,0:T(8,128)(2,1)S(1)}, bf16[2,384,384]{2,1,0:T(8,128)(2,1)S(1)}, u32[]{:S(2)}, u32[]{:S(2)}) %collective-permute-start.3) | collective-permute-done | bytes 589856 | tf_op jit(solution)/shard_map/ppermute | solution.py:17
  258.8 0.9 collective-permute-done.2
  259.7 0.0 copy-done.3
  259.7 3.9 %fusion.3 = bf16[2,384,384]{2,1,0:T(8,128)(2,1)} fusion(bf16[2,2,384,384]{3,2,1,0:T(8,128)(2,1)S(1)} %copy-done, bf16[2,384,384]{2,1,0:T(8,128)(2,1)S(1)} %copy-done.3, bf16[2,384,384]{2,1,0:T(8,128)(2,1)S(1)} %collective-permute-done.3, bf16[2,384,384]{2,1,0:T(8,128)(2,1)S(1)} %all_gather.7, bf16[2,384,384]{2,1,0:T(8,128)(2,1)} %collective-permute-done.2, ...), kind=kOutput, calls=%fused_computation.7 | convolution fusion | flops 913047552 | bytes 4128808 | tf_op jit(solution)/shard_map/swac,wdc->sad/dot_general | solution.py:40
  263.6 0.0 copy-done.2
  263.6 0.0 reduce-scatter.5.cloned.1.call-update
  263.6 59.3 %reduce-scatter.5.cloned.1.call-done = bf16[2,64,384]{2,1,0:T(8,128)(2,1)} async-done(((bf16[2,384,384]{2,1,0:T(8,128)(2,1)}), bf16[2,64,384]{2,1,0:T(8,128)(2,1)}) %reduce-scatter.5.cloned.1.call-update) | async-done | bytes 98320 | tf_op jit(solution)/shard_map/reduce_scatter | solution.py:41
  322.9 1.7 and_select_fusion
  (4 shorter events, 0.0 us)
Async XLA Ops:
  7.2 40.3 %copy-start = (bf16[2,2,384,384]{3,2,1,0:T(8,128)(2,1)S(1)}, bf16[2,2,384,384]{3,2,1,0:T(8,128)(2,1)}, u32[]{:S(2)}) copy-start(bf16[2,2,384,384]{3,2,1,0:T(8,128)(2,1)} %param.8) | copy-start | bytes 3538948
  7.2 107.5 %reduce-scatter.3.cloned.1.call-start = ((), (), s32[]{:S(2)}) async-start(), calls=%async_computation.2 | async-start | bytes 688128 | tf_op jit(solution)/shard_map/reduce_scatter | solution.py:41
  29.9 16.7 %collective-permute-start.1 = (bf16[2,384,384]{2,1,0:T(8,128)(2,1)S(1)}, bf16[2,384,384]{2,1,0:T(8,128)(2,1)S(1)}, u32[]{:S(2)}, u32[]{:S(2)}) collective-permute-start(bf16[2,384,384]{2,1,0:T(8,128)(2,1)S(1)} %all_gather.6), channel_id=1, source_target_pairs={{6,0},{12,6},{18,12},{24,18},{30,24},{36,30},{42,36},{48,42},{54,4... | collective-permute-start | bytes 1769480 | tf_op jit(solution)/shard_map/ppermute | solution.py:17
  31.2 16.2 %collective-permute-start = (bf16[2,384,384]{2,1,0:T(8,128)(2,1)S(1)}, bf16[2,384,384]{2,1,0:T(8,128)(2,1)S(1)}, u32[]{:S(2)}, u32[]{:S(2)}) collective-permute-start(bf16[2,384,384]{2,1,0:T(8,128)(2,1)S(1)} %all_gather.6), channel_id=1, source_target_pairs={{0,6},{6,12},{12,18},{18,24},{24,30},{30,36},{36,42},{42,48},{48,5... | collective-permute-start | bytes 1769480 | tf_op jit(solution)/shard_map/ppermute | solution.py:14
  47.5 67.2 %copy-start.1 = (bf16[2,64,384]{2,1,0:T(8,128)(2,1)S(1)}, bf16[2,64,384]{2,1,0:T(8,128)(2,1)}, u32[]{:S(2)}) copy-start(bf16[2,64,384]{2,1,0:T(8,128)(2,1)} %param.5) | copy-start | bytes 294916
  51.3 208.4 %copy-start.3 = (bf16[2,384,384]{2,1,0:T(8,128)(2,1)S(1)}, bf16[2,384,384]{2,1,0:T(8,128)(2,1)}, u32[]{:S(2)}) copy-start(bf16[2,384,384]{2,1,0:T(8,128)(2,1)} %param.9) | copy-start | bytes 1769476
  51.3 271.6 %reduce-scatter.5.cloned.1.call-start = ((), (), s32[]{:S(2)}) async-start(), calls=%async_computation.3 | async-start | bytes 688128 | tf_op jit(solution)/shard_map/reduce_scatter | solution.py:41
  116.4 147.2 %copy-start.2 = (f32[2,64,384]{2,1,0:T(8,128)}, f32[2,64,384]{2,1,0:T(8,128)S(1)}, u32[]{:S(2)}) copy-start(f32[2,64,384]{2,1,0:T(8,128)S(1)} %get-tuple-element.11) | copy-start | bytes 589828
  242.2 16.7 %collective-permute-start.3 = (bf16[2,384,384]{2,1,0:T(8,128)(2,1)S(1)}, bf16[2,384,384]{2,1,0:T(8,128)(2,1)S(1)}, u32[]{:S(2)}, u32[]{:S(2)}) collective-permute-start(bf16[2,384,384]{2,1,0:T(8,128)(2,1)S(1)} %all_gather.7), channel_id=1, source_target_pairs={{6,0},{12,6},{18,12},{24,18},{30,24},{36,30},{42,36},{48,42},{54,4... | collective-permute-start | bytes 1769480 | tf_op jit(solution)/shard_map/ppermute | solution.py:17
  243.5 16.2 %collective-permute-start.2 = (bf16[2,384,384]{2,1,0:T(8,128)(2,1)S(1)}, bf16[2,384,384]{2,1,0:T(8,128)(2,1)}, u32[]{:S(2)}, u32[]{:S(2)}) collective-permute-start(bf16[2,384,384]{2,1,0:T(8,128)(2,1)S(1)} %all_gather.7), channel_id=1, source_target_pairs={{0,6},{6,12},{12,18},{18,24},{24,30},{30,36},{36,42},{42,48},{48,5... | collective-permute-start | bytes 1769480 | tf_op jit(solution)/shard_map/ppermute | solution.py:14
Sparse Core Ops, SparseCore 0:
  51.4 63.1 reduce-scatter.2
  263.7 59.1 reduce-scatter.4
where the time goes:
time: 334 us; the launch traced here: 331 us
  blocking collectives  145 us (43%)
  waiting for transfers between devices  145 us (43%)
  between operations  15.4 us (5%)
  starting transfers between devices  11.5 us (3%)
  matrix products  7.7 us (2%)
  other arithmetic  6.7 us (2%)
    reduce_scatter x2, waiting for transfers between devices, apply_hamiltonian(): lax.psum_scatter(partial_term.astype(jnp.bfloat16), 'col', scatter_dimens...  123 us
    psum x1, blocking collectives, body(): lax.psum((jnp.sum(psi_float * sigma_first), jnp.sum(psi_float * psi_float...  113 us
    all_gather x2, blocking collectives, apply_hamiltonian(): full = lax.all_gather(vector, 'col', axis=1, tiled=True)  31.4 us
    ppermute x2, waiting for transfers between devices, with_halo(): lax.ppermute(lax.slice_in_dim(block, 0, width, axis=dim), axis, backward)  21 us
    ppermute x2, starting transfers between devices, with_halo(): lax.ppermute(lax.slice_in_dim(block, block.shape[dim] - width, None, axis...  8.83 us
    dot_general x2, matrix products, apply_hamiltonian(): jnp.einsum('swac,wdc->sad', temp, right_env, preferred_element_type=jnp.f...  7.7 us
  transfers between devices with their start and end apart: 6, of which 6 were waited for; matrix products, arithmetic and copies ran while one was open for 0% of the time, Pallas kernels for 0%

commit v1 on v0

v1 whole, which is shorter than its diff:
```python
import jax
import jax.numpy as jnp
from jax import lax
from jax.sharding import PartitionSpec as P

CORES = 2


def combine_rows(vector, pattern):
    count = lax.axis_size("blk")
    forward = [(i, i + 1) for i in range(count - 1)]
    backward = [(target, source) for source, target in forward]
    low = lax.ppermute(vector, "blk", forward)
    high = lax.ppermute(vector, "blk", backward)
    padded = jnp.concatenate([low, vector, high], axis=0).astype(jnp.float32)
    coeff = pattern.astype(jnp.float32)
    sectors = vector.shape[0]
    total = jnp.zeros(vector.shape, jnp.float32)
    for offset in range(pattern.shape[1]):
        total = total + coeff[:, offset, None, None] * padded[offset : offset + sectors]
    return total.astype(jnp.bfloat16)


def exchange_sum(values, axis):
    copies = jnp.broadcast_to(values[None, :, None], (lax.axis_size(axis), values.shape[0], 128))
    return jnp.sum(lax.all_to_all(copies, axis, 0, 0, tiled=True)[:, :, 0], axis=0)


def apply_hamiltonian(vector, pattern, envs, mask, scale):
    sectors, rows, width = vector.shape
    count = lax.axis_size("col")
    rows_of_z = combine_rows(vector, pattern)
    outgoing = jnp.tile(rows_of_z, (count // CORES, 1, 1))
    combined = lax.all_to_all(outgoing, "col", 0, 0, tiled=True).reshape(count * rows, width)
    part = jnp.zeros((count * rows, width), jnp.float32)
    for left, right in envs:
        temp = jnp.einsum("wab,bc->wac", left, combined, preferred_element_type=jnp.float32)
        part = part + jnp.einsum(
            "wac,wdc->ad", temp.astype(jnp.bfloat16), right, preferred_element_type=jnp.float32
        )
    part = part.astype(jnp.bfloat16).reshape(count, rows, width)
    mine = lax.all_to_all(part, "col", 0, 0, tiled=True).astype(jnp.float32)
    summed = jnp.sum(mine.reshape(count // CORES, sectors, rows, width), axis=0)
    return jnp.where(mask, summed * scale, jnp.float32(0.0))


def body(psi, dims, pattern, left_env, right_env):
    rows = psi.shape[1]
    width = psi.shape[2]
    count = lax.axis_size("col")
    core = lax.rem(lax.axis_index("col"), CORES)
    swap = [(i, i ^ 1) for i in range(count)]
    left_mine = lax.dynamic_index_in_dim(left_env, core, 0, keepdims=False)
    left_sent = lax.dynamic_index_in_dim(left_env, 1 - core, 0, keepdims=False)
    row_ids = lax.axis_index("col") * rows + jnp.arange(rows, dtype=jnp.int32)
    col_ids = jnp.arange(width, dtype=jnp.int32)
    mask = (row_ids[None, :, None] < dims[:, None, None]) & (
        col_ids[None, None, :] < dims[:, None, None]
    )
    psi_m = jnp.where(mask, psi, jnp.zeros_like(psi))
    envs = (
        (left_mine, right_env),
        (lax.ppermute(left_sent, "col", swap), lax.ppermute(right_env, "col", swap)),
    )
    scale = 1.0 / jnp.sqrt(jnp.float32(right_env.shape[0] * count))
    sigma_first = apply_hamiltonian(psi_m, pattern, envs, mask, scale)
    psi_float = psi_m.astype(jnp.float32)
    products = jnp.stack([jnp.sum(psi_float * sigma_first), jnp.sum(psi_float * psi_float)])
    sums = exchange_sum(exchange_sum(products, "blk"), "col")
    theta = sums[0] / sums[1]
    applied = apply_hamiltonian(sigma_first.astype(jnp.bfloat16), pattern, envs, mask, scale)
    return (sigma_first, applied - theta * sigma_first)


def solution(mesh):
    return jax.shard_map(
        body,
        mesh=mesh,
        in_specs=(
            P("blk", "col", None),
            P("blk"),
            P("blk", None),
            P("blk", "col", None, None),
            P("col", None, None),
        ),
        out_specs=(P("blk", "col", None), P("blk", "col", None)),
        check_vma=False,
    )
```

time: 334 us -> 140 us (0.42)
  blocking collectives: 145 us -> 10.6 us
  waiting for transfers between devices: 145 us -> 32 us
  starting transfers between devices: 11.5 us -> 76.7 us
  between operations: 15.4 us -> 2.1 us
  local copies, waits for them, and re-layouts: 0.24 us -> 3.78 us
    reduce_scatter x2 -> x0, waiting for transfers between devices: 123 us -> none  [apply_hamiltonian(): lax.psum_scatter(partial_term.astype(jnp.bfloat16), 'col', scatter_dimens...]
    psum x1 -> x0, blocking collectives: 113 us -> none  [body(): lax.psum((jnp.sum(psi_float * sigma_first), jnp.sum(psi_float * psi_float...]
    all_to_all x0 -> x5, starting transfers between devices: none -> 60.5 us  [the longest x2 35.7 us: exchange_sum(): lax.all_to_all(copies, axis, 0, 0, tiled=True)[:, :, 0]]
    all_gather x2 -> x0, blocking collectives: 31.4 us -> none  [apply_hamiltonian(): full = lax.all_gather(vector, 'col', axis=1, tiled=True)]
    all_to_all x0 -> x5, waiting for transfers between devices: none -> 31.2 us  [the longest x2 15.4 us: exchange_sum(): lax.all_to_all(copies, axis, 0, 0, tiled=True)[:, :, 0]]
    ppermute x4 -> x6, waiting for transfers between devices: 22.7 us -> 0.72 us  [the longest x2 0.71 us: combine_rows(): low = lax.ppermute(vector, 'blk', forward)]
    all_to_all x0 -> x1, blocking collectives: none -> 10.6 us  [apply_hamiltonian(): mine = lax.all_to_all(part, 'col', 0, 0, tiled=True).astype(jnp.float32)]
    ppermute x4 -> x6, starting transfers between devices: 11.4 us -> 16.2 us  [the longest x2 9.33 us: combine_rows(): low = lax.ppermute(vector, 'blk', forward)]
  transfers between devices with their start and end apart: 6 -> 11, of which waited for: 6 -> 6; matrix products, arithmetic and copies ran while one was open for 0% -> 7% of each run, Pallas kernels for 0% -> 0%
where the time goes in v1:
time: 140 us; the launch traced here: 139 us
  starting transfers between devices  76.7 us (55%)
  waiting for transfers between devices  32 us (23%)
  blocking collectives  10.6 us (8%)
  matrix products  7.12 us (5%)
  other arithmetic  6.86 us (5%)
  local copies, waits for them, and re-layouts  3.78 us (3%)
  between operations  2.1 us (2%)
    all_to_all x2, starting transfers between devices, exchange_sum(): lax.all_to_all(copies, axis, 0, 0, tiled=True)[:, :, 0]  35.7 us
    all_to_all x2, starting transfers between devices, apply_hamiltonian(): lax.all_to_all(outgoing, 'col', 0, 0, tiled=True)  20.7 us
    all_to_all x2, waiting for transfers between devices, exchange_sum(): lax.all_to_all(copies, axis, 0, 0, tiled=True)[:, :, 0]  15.4 us
    all_to_all x1, blocking collectives, apply_hamiltonian(): mine = lax.all_to_all(part, 'col', 0, 0, tiled=True).astype(jnp.float32)  10.6 us
    all_to_all x2, waiting for transfers between devices, apply_hamiltonian(): lax.all_to_all(outgoing, 'col', 0, 0, tiled=True)  10.3 us
    ppermute x2, starting transfers between devices, combine_rows(): low = lax.ppermute(vector, 'blk', forward)  9.33 us
    dot_general x4, matrix products, apply_hamiltonian(): jnp.einsum('wac,wdc->ad', temp.astype(jnp.bfloat16), right, preferred_ele...  7.12 us
    all_to_all x1, waiting for transfers between devices, apply_hamiltonian(): mine = lax.all_to_all(part, 'col', 0, 0, tiled=True).astype(jnp.float32)  5.52 us
  transfers between devices with their start and end apart: 11, of which 6 were waited for; matrix products, arithmetic and copies ran while one was open for 7% of the time, Pallas kernels for 0%

profile of v1, /device:TPU:1, one launch (start us, length us, event | category | flops | bytes accessed | tf_op | source)
XLA Modules:
  0.0 139.1 jit_solution(12905958815103653706)
XLA Ops:
  0.7 0.8 iota_compare_fusion
  1.5 0.7 broadcast_compare_fusion
  2.2 1.0 and_select_fusion.2
  3.2 1.3 collective-permute-start.1
  4.5 4.7 %collective-permute-start = (bf16[2,64,384]{2,1,0:T(8,128)(2,1)S(1)}, bf16[2,64,384]{2,1,0:T(8,128)(2,1)S(1)}, u32[]{:S(2)}, u32[]{:S(2)}) collective-permute-start(bf16[2,64,384]{2,1,0:T(8,128)(2,1)S(1)} %and_select_fusion.2), channel_id=1, source_target_pairs={{0,6},{6,12},{12,18},{18,24},{24,30},{30,36},{36,42},{42,48},{48,5... | collective-permute-start | bytes 294920 | tf_op jit(solution)/shard_map/ppermute | solution.py:13
  9.2 0.7 convert_element_type.42
  10.1 0.7 collective-permute-done
  11.0 0.7 tile.8
  11.7 14.4 %all-to-all-start = ((bf16[6,64,384]{2,1,0:T(8,128)(2,1)}), bf16[6,64,384]{2,1,0:T(8,128)(2,1)S(1)}, u32[]{:S(2)}, u32[]{:S(2)}) async-start(bf16[6,64,384]{2,1,0:T(8,128)(2,1)} %bitcast.1), calls=%async_computation | async-start | bytes 589824 | tf_op jit(solution)/shard_map/all_to_all | solution.py:34
  26.2 2.0 %collective-permute-start.2 = (bf16[2,384,384]{2,1,0:T(8,128)(2,1)S(1)}, bf16[2,384,384]{2,1,0:T(8,128)(2,1)S(1)}, u32[]{:S(2)}, u32[]{:S(2)}) collective-permute-start(bf16[2,384,384]{2,1,0:T(8,128)(2,1)S(1)} %dynamic-slice_bitcast_fusion), channel_id=1, source_target_pairs={{0,1},{1,0},{2,3},{3,2},{4,5},{5,4},{6,7},{7,6},{8,9},{9,8},{10,11... | collective-permute-start | bytes 1769480 | tf_op jit(solution)/shard_map/ppermute | solution.py:63
  28.2 2.3 %collective-permute-start.3 = (bf16[2,384,384]{2,1,0:T(8,128)(2,1)S(1)}, bf16[2,384,384]{2,1,0:T(8,128)(2,1)}, u32[]{:S(2)}, u32[]{:S(2)}) collective-permute-start(bf16[2,384,384]{2,1,0:T(8,128)(2,1)S(1)} %copy-done.3), channel_id=1, source_target_pairs={{0,1},{1,0},{2,3},{3,2},{4,5},{5,4},{6,7},{7,6},{8,9},{9,8},{10,11... | collective-permute-start | bytes 1769480 | tf_op jit(solution)/shard_map/ppermute | solution.py:63
  30.5 3.1 %all-to-all-done = bf16[6,64,384]{2,1,0:T(8,128)(2,1)S(1)} async-done(((bf16[6,64,384]{2,1,0:T(8,128)(2,1)}), bf16[6,64,384]{2,1,0:T(8,128)(2,1)S(1)}, u32[]{:S(2)}, u32[]{:S(2)}) %all-to-all-start) | async-done | bytes 294944 | tf_op jit(solution)/shard_map/all_to_all | solution.py:34
  33.6 1.6 %fusion.7 = f32[384,384]{1,0:T(8,128)} fusion(bf16[2,384,384]{2,1,0:T(8,128)(2,1)S(1)} %copy-done.3, bf16[384,384,1]{1,0,2:T(8,128)(2,1)S(1)} %bitcast.54, bf16[2,2,384,384]{3,2,1,0:T(8,128)(2,1)S(1)} %copy-done, s32[]{:T(128)S(6)} %select_n.18), kind=kOutput, calls=%fused_computation.11 | convolution fusion | flops 453279744 | bytes 2064388 | tf_op jit(solution)/shard_map/wac,wdc->ad/dot_general | solution.py:38
  35.2 2.1 %fusion.11 = bf16[384,384]{1,0:T(8,128)(2,1)S(1)} fusion(f32[384,384]{1,0:T(8,128)} %fusion.7, bf16[2,384,384]{2,1,0:T(8,128)(2,1)} %collective-permute-done.3, bf16[2,384,384]{2,1,0:T(8,128)(2,1)S(1)} %collective-permute-done.2, bf16[384,384,1]{1,0,2:T(8,128)(2,1)S(1)} %bitcast.55), kind=kOutput, calls=%fused_computation.15 | convolution fusion | flops 453574656 | bytes 2359296 | tf_op jit(solution)/shard_map/wac,wdc->ad/dot_general | solution.py:38
  37.3 10.6 %all_to_all.30 = bf16[6,64,384]{2,1,0:T(8,128)(2,1)S(1)} all-to-all(bf16[6,64,384]{2,1,0:T(8,128)(2,1)S(1)} %bitcast.58), channel_id=1, replica_groups=mesh['blk'=128,'col'=6] {'col'}, dimensions={0} | all-to-all | bytes 589824 | tf_op jit(solution)/shard_map/all_to_all | solution.py:42
  47.9 0.8 fusion.20
  48.7 1.3 collective-permute-start.5
  50.0 4.7 %collective-permute-start.4 = (bf16[2,64,384]{2,1,0:T(8,128)(2,1)S(1)}, bf16[2,64,384]{2,1,0:T(8,128)(2,1)S(1)}, u32[]{:S(2)}, u32[]{:S(2)}) collective-permute-start(bf16[2,64,384]{2,1,0:T(8,128)(2,1)S(1)} %convert_element_type.48), channel_id=1, source_target_pairs={{0,6},{6,12},{12,18},{18,24},{24,30},{30,36},{36,42},{42,48},{48,5... | collective-permute-start | bytes 294920 | tf_op jit(solution)/shard_map/ppermute | solution.py:13
  54.7 1.3 pad_maximum_fusion
  55.9 0.8 broadcast_in_dim.13
  56.7 31.6 %all-to-all-start.4 = ((f32[128,2,128]{2,1,0:T(2,128)}), f32[128,2,128]{2,1,0:T(2,128)S(1)}, u32[]{:S(2)}, u32[]{:S(2)}) async-start(f32[128,2,128]{2,1,0:T(2,128)} %broadcast_in_dim.13), calls=%async_computation.4 | async-start | bytes 262144 | tf_op jit(solution)/shard_map/all_to_all | solution.py:26
  88.5 14.8 %all-to-all-done.4 = f32[128,2,128]{2,1,0:T(2,128)S(1)} async-done(((f32[128,2,128]{2,1,0:T(2,128)}), f32[128,2,128]{2,1,0:T(2,128)S(1)}, u32[]{:S(2)}, u32[]{:S(2)}) %all-to-all-start.4) | async-done | bytes 131104 | tf_op jit(solution)/shard_map/all_to_all | solution.py:26
  103.3 0.7 tile.20
  104.1 6.3 %all-to-all-start.2 = ((bf16[6,64,384]{2,1,0:T(8,128)(2,1)}), bf16[6,64,384]{2,1,0:T(8,128)(2,1)S(1)}, u32[]{:S(2)}, u32[]{:S(2)}) async-start(bf16[6,64,384]{2,1,0:T(8,128)(2,1)} %bitcast.10), calls=%async_computation.2 | async-start | bytes 589824 | tf_op jit(solution)/shard_map/all_to_all | solution.py:34
  110.7 7.2 %all-to-all-done.2 = bf16[6,64,384]{2,1,0:T(8,128)(2,1)S(1)} async-done(((bf16[6,64,384]{2,1,0:T(8,128)(2,1)}), bf16[6,64,384]{2,1,0:T(8,128)(2,1)S(1)}, u32[]{:S(2)}, u32[]{:S(2)}) %all-to-all-start.2) | async-done | bytes 294944 | tf_op jit(solution)/shard_map/all_to_all | solution.py:34
  117.9 0.7 broadcast_in_dim.14
  118.6 4.1 %all-to-all-start.5 = ((f32[6,2,128]{2,1,0:T(2,128)}), f32[6,2,128]{2,1,0:T(2,128)S(1)}, u32[]{:S(2)}, u32[]{:S(2)}) async-start(f32[6,2,128]{2,1,0:T(2,128)} %broadcast_in_dim.14), calls=%async_computation.5 | async-start | bytes 12288 | tf_op jit(solution)/shard_map/all_to_all | solution.py:26
  122.7 0.8 fusion.5
  123.5 2.6 %fusion.10 = bf16[384,384]{1,0:T(8,128)(2,1)} fusion(f32[384,384]{1,0:T(8,128)S(1)} %fusion.5, bf16[2,384,384]{2,1,0:T(8,128)(2,1)} %collective-permute-done.3, bf16[2,384,384]{2,1,0:T(8,128)(2,1)S(1)} %collective-permute-done.2, bf16[384,384,1]{1,0,2:T(8,128)(2,1)S(1)} %bitcast.57), kind=kOutput, calls=%fused_computation.14 | convolution fusion | flops 453574656 | bytes 2359296 | tf_op jit(solution)/shard_map/wac,wdc->ad/dot_general | solution.py:38
  126.7 4.1 %all-to-all-start.3 = ((bf16[6,64,384]{2,1,0:T(8,128)(2,1)}), bf16[6,64,384]{2,1,0:T(8,128)(2,1)S(1)}, u32[]{:S(2)}, u32[]{:S(2)}) async-start(bf16[6,64,384]{2,1,0:T(8,128)(2,1)} %bitcast.16), calls=%async_computation.3 | async-start | bytes 589824 | tf_op jit(solution)/shard_map/all_to_all | solution.py:42
  132.7 5.5 %all-to-all-done.3 = bf16[6,64,384]{2,1,0:T(8,128)(2,1)S(1)} async-done(((bf16[6,64,384]{2,1,0:T(8,128)(2,1)}), bf16[6,64,384]{2,1,0:T(8,128)(2,1)S(1)}, u32[]{:S(2)}, u32[]{:S(2)}) %all-to-all-start.3) | async-done | bytes 294944 | tf_op jit(solution)/shard_map/all_to_all | solution.py:42
  138.3 0.8 fusion.22
  (27 shorter events, 2.3 us)
Async XLA Ops:
  0.6 25.5 %copy-start = (bf16[2,2,384,384]{3,2,1,0:T(8,128)(2,1)S(1)}, bf16[2,2,384,384]{3,2,1,0:T(8,128)(2,1)}, u32[]{:S(2)}) copy-start(bf16[2,2,384,384]{3,2,1,0:T(8,128)(2,1)} %param.8) | copy-start | bytes 3538948
  3.2 6.9 %collective-permute-start.1 = (bf16[2,64,384]{2,1,0:T(8,128)(2,1)S(1)}, bf16[2,64,384]{2,1,0:T(8,128)(2,1)S(1)}, u32[]{:S(2)}, u32[]{:S(2)}) collective-permute-start(bf16[2,64,384]{2,1,0:T(8,128)(2,1)S(1)} %and_select_fusion.2), channel_id=1, source_target_pairs={{6,0},{12,6},{18,12},{24,18},{30,24},{36,30},{42,36},{48,42},{54,4... | collective-permute-start | bytes 294920 | tf_op jit(solution)/shard_map/ppermute | solution.py:14
  4.5 6.3 %collective-permute-start = (bf16[2,64,384]{2,1,0:T(8,128)(2,1)S(1)}, bf16[2,64,384]{2,1,0:T(8,128)(2,1)S(1)}, u32[]{:S(2)}, u32[]{:S(2)}) collective-permute-start(bf16[2,64,384]{2,1,0:T(8,128)(2,1)S(1)} %and_select_fusion.2), channel_id=1, source_target_pairs={{0,6},{6,12},{12,18},{18,24},{24,30},{30,36},{36,42},{42,48},{48,5... | collective-permute-start | bytes 294920 | tf_op jit(solution)/shard_map/ppermute | solution.py:13
  11.0 17.2 %copy-start.3 = (bf16[2,384,384]{2,1,0:T(8,128)(2,1)S(1)}, bf16[2,384,384]{2,1,0:T(8,128)(2,1)}, u32[]{:S(2)}) copy-start(bf16[2,384,384]{2,1,0:T(8,128)(2,1)} %param.9) | copy-start | bytes 1769476
  11.7 21.8 %all-to-all-start = ((bf16[6,64,384]{2,1,0:T(8,128)(2,1)}), bf16[6,64,384]{2,1,0:T(8,128)(2,1)S(1)}, u32[]{:S(2)}, u32[]{:S(2)}) async-start(bf16[6,64,384]{2,1,0:T(8,128)(2,1)} %bitcast.1), calls=%async_computation | async-start | bytes 589824 | tf_op jit(solution)/shard_map/all_to_all | solution.py:34
  26.2 9.0 %collective-permute-start.2 = (bf16[2,384,384]{2,1,0:T(8,128)(2,1)S(1)}, bf16[2,384,384]{2,1,0:T(8,128)(2,1)S(1)}, u32[]{:S(2)}, u32[]{:S(2)}) collective-permute-start(bf16[2,384,384]{2,1,0:T(8,128)(2,1)S(1)} %dynamic-slice_bitcast_fusion), channel_id=1, source_target_pairs={{0,1},{1,0},{2,3},{3,2},{4,5},{5,4},{6,7},{7,6},{8,9},{9,8},{10,11... | collective-permute-start | bytes 1769480 | tf_op jit(solution)/shard_map/ppermute | solution.py:63
  28.2 7.0 %collective-permute-start.3 = (bf16[2,384,384]{2,1,0:T(8,128)(2,1)S(1)}, bf16[2,384,384]{2,1,0:T(8,128)(2,1)}, u32[]{:S(2)}, u32[]{:S(2)}) collective-permute-start(bf16[2,384,384]{2,1,0:T(8,128)(2,1)S(1)} %copy-done.3), channel_id=1, source_target_pairs={{0,1},{1,0},{2,3},{3,2},{4,5},{5,4},{6,7},{7,6},{8,9},{9,8},{10,11... | collective-permute-start | bytes 1769480 | tf_op jit(solution)/shard_map/ppermute | solution.py:63
  35.2 12.7 %copy-start.2 = (bf16[2,64,384]{2,1,0:T(8,128)(2,1)S(1)}, bf16[2,64,384]{2,1,0:T(8,128)(2,1)}, u32[]{:S(2)}) copy-start(bf16[2,64,384]{2,1,0:T(8,128)(2,1)} %param.5) | copy-start | bytes 294916
  48.7 89.6 %copy-start.1 = (f32[2,64,384]{2,1,0:T(8,128)}, f32[2,64,384]{2,1,0:T(8,128)S(1)}, u32[]{:S(2)}) copy-start(f32[2,64,384]{2,1,0:T(8,128)S(1)} %get-tuple-element.9) | copy-start | bytes 589828
  48.7 39.6 %collective-permute-start.5 = (bf16[2,64,384]{2,1,0:T(8,128)(2,1)S(1)}, bf16[2,64,384]{2,1,0:T(8,128)(2,1)S(1)}, u32[]{:S(2)}, u32[]{:S(2)}) collective-permute-start(bf16[2,64,384]{2,1,0:T(8,128)(2,1)S(1)} %convert_element_type.48), channel_id=1, source_target_pairs={{6,0},{12,6},{18,12},{24,18},{30,24},{36,30},{42,36},{48,42},{54,4... | collective-permute-start | bytes 294920 | tf_op jit(solution)/shard_map/ppermute | solution.py:14
  50.0 38.3 %collective-permute-start.4 = (bf16[2,64,384]{2,1,0:T(8,128)(2,1)S(1)}, bf16[2,64,384]{2,1,0:T(8,128)(2,1)S(1)}, u32[]{:S(2)}, u32[]{:S(2)}) collective-permute-start(bf16[2,64,384]{2,1,0:T(8,128)(2,1)S(1)} %convert_element_type.48), channel_id=1, source_target_pairs={{0,6},{6,12},{12,18},{18,24},{24,30},{30,36},{36,42},{42,48},{48,5... | collective-permute-start | bytes 294920 | tf_op jit(solution)/shard_map/ppermute | solution.py:13
  56.7 46.6 %all-to-all-start.4 = ((f32[128,2,128]{2,1,0:T(2,128)}), f32[128,2,128]{2,1,0:T(2,128)S(1)}, u32[]{:S(2)}, u32[]{:S(2)}) async-start(f32[128,2,128]{2,1,0:T(2,128)} %broadcast_in_dim.13), calls=%async_computation.4 | async-start | bytes 262144 | tf_op jit(solution)/shard_map/all_to_all | solution.py:26
  104.1 13.8 %all-to-all-start.2 = ((bf16[6,64,384]{2,1,0:T(8,128)(2,1)}), bf16[6,64,384]{2,1,0:T(8,128)(2,1)S(1)}, u32[]{:S(2)}, u32[]{:S(2)}) async-start(bf16[6,64,384]{2,1,0:T(8,128)(2,1)} %bitcast.10), calls=%async_computation.2 | async-start | bytes 589824 | tf_op jit(solution)/shard_map/all_to_all | solution.py:34
  118.6 8.1 %all-to-all-start.5 = ((f32[6,2,128]{2,1,0:T(2,128)}), f32[6,2,128]{2,1,0:T(2,128)S(1)}, u32[]{:S(2)}, u32[]{:S(2)}) async-start(f32[6,2,128]{2,1,0:T(2,128)} %broadcast_in_dim.14), calls=%async_computation.5 | async-start | bytes 12288 | tf_op jit(solution)/shard_map/all_to_all | solution.py:26
  126.7 11.6 %all-to-all-start.3 = ((bf16[6,64,384]{2,1,0:T(8,128)(2,1)}), bf16[6,64,384]{2,1,0:T(8,128)(2,1)S(1)}, u32[]{:S(2)}, u32[]{:S(2)}) async-start(bf16[6,64,384]{2,1,0:T(8,128)(2,1)} %bitcast.16), calls=%async_computation.3 | async-start | bytes 589824 | tf_op jit(solution)/shard_map/all_to_all | solution.py:42

commit v2 on v1

v2 whole, which is shorter than its diff:
```python
import jax
import jax.numpy as jnp
from jax import lax
from jax.sharding import Mesh, PartitionSpec as P

CORES = 2
LANES = 128
SPLIT = {"z_hi": 4, "x": 4, "y": 8, "z_lo": 3, "core": 2}
BLK = ("z_hi", "x", "y")
COL = ("z_lo", "core")
NEAR = ("x", "y")
FAR = ("z_hi", "z_lo", "core")
F32 = jnp.float32
BF16 = jnp.bfloat16


def exchange(blocks, axes):
    return lax.all_to_all(blocks, axes, 0, 0, tiled=True)


def masked(value, dims):
    _, rows, width = value.shape
    dims = lax.optimization_barrier(dims)[:, None, None]
    row = lax.broadcasted_iota(jnp.int32, value.shape, 1) + lax.axis_index(COL) * rows
    column = lax.broadcasted_iota(jnp.int32, value.shape, 2)
    return jnp.where((row < dims) & (column < dims), value, jnp.zeros_like(value))


def combine(vector, coeff):
    count = lax.axis_size(BLK)
    forward = [(i, i + 1) for i in range(count - 1)]
    backward = [(target, source) for source, target in forward]
    low = lax.ppermute(vector, BLK, forward)
    high = lax.ppermute(vector, BLK, backward)
    padded = jnp.concatenate([low, vector, high], axis=0).astype(F32)
    sectors, rows, width = vector.shape
    total = jnp.zeros(coeff.shape[:2] + (rows, width), F32)
    for offset in range(coeff.shape[2]):
        total = total + coeff[:, :, offset, None, None] * padded[None, offset : offset + sectors]
    return total.astype(BF16).reshape(-1, rows, width)


def product(z, left, right):
    count, rows, width = z.shape
    z = z.reshape(count * rows, width)
    temp = jnp.einsum("wab,bc->wac", left, z, preferred_element_type=F32).astype(BF16)
    part = jnp.einsum("wac,wdc->ad", temp, right, preferred_element_type=F32)
    return part.astype(BF16).reshape(count, rows, width)


def reduced(parts, sectors, scale):
    count, rows, width = parts.shape
    parts = parts.astype(F32).reshape(count // sectors, sectors, rows, width)
    return jnp.sum(parts, axis=0) * scale


def gathered(values, axes):
    return exchange(jnp.broadcast_to(values[None, None, :], (lax.axis_size(axes), 1, LANES)), axes)


def body(psi, dims, pattern, left_env, right_env):
    sectors = psi.shape[0]
    count = lax.axis_size(COL)
    core = lax.axis_index("core")
    swap = [(0, 1), (1, 0)]
    scale = 1.0 / jnp.sqrt(F32(right_env.shape[0] * count))
    coeff = jnp.broadcast_to(pattern.astype(F32)[None], (count // CORES,) + pattern.shape)
    coeff = lax.optimization_barrier(coeff)

    psi_m = masked(psi, dims)
    outgoing = combine(psi_m, coeff)
    left_mine = lax.dynamic_index_in_dim(left_env, core, 0, keepdims=False)
    left_sent = lax.dynamic_index_in_dim(left_env, 1 - core, 0, keepdims=False)
    left = jnp.concatenate([left_mine, lax.ppermute(left_sent, "core", swap)], axis=0)
    right = jnp.concatenate([right_env, lax.ppermute(right_env, "core", swap)], axis=0)
    left, right = lax.optimization_barrier((left, right))
    parts = exchange(product(exchange(outgoing, COL), left, right), COL)
    sigma = masked(reduced(parts, sectors, scale), dims)
    vector = psi_m.astype(F32)
    products = jnp.where(
        jnp.arange(LANES) < LANES // 2, jnp.sum(vector * sigma), jnp.sum(vector * vector)
    )
    sums = jnp.sum(gathered(products, NEAR), axis=(0, 1))
    z = exchange(combine(sigma.astype(BF16), coeff), COL)
    z, sums = lax.optimization_barrier((z, sums))
    sums = jnp.sum(gathered(sums, FAR), axis=(0, 1))
    parts = exchange(product(z, left, right), COL)
    theta = sums[0] / sums[LANES // 2]
    second = masked(reduced(parts, sectors, scale), dims) - theta * sigma
    return (sigma, second)


def solution(mesh):
    split = Mesh(mesh.devices.reshape(tuple(SPLIT.values())), tuple(SPLIT))
    return jax.shard_map(
        body,
        mesh=split,
        in_specs=(
            P(BLK, COL, None),
            P(BLK),
            P(BLK, None),
            P(BLK, COL, None, None),
            P(COL, None, None),
        ),
        out_specs=(P(BLK, COL, None), P(BLK, COL, None)),
        check_vma=False,
    )
```

time: 140 us -> 132 us (0.943)
  starting transfers between devices: 76.7 us -> 72.9 us
  matrix products: 7.12 us -> 3.66 us
    all_to_all x5, starting transfers between devices: 60.5 us -> 47.3 us  [exchange(): return lax.all_to_all(blocks, axes, 0, 0, tiled=True)]
    ppermute x6, starting transfers between devices: 16.2 us -> 25.6 us  [the longest x1 12.3 us: body(): lax.ppermute(right_env, 'core', swap)]
    dot_general x4 -> x2, matrix products: 7.12 us -> 3.66 us  [product(): part = jnp.einsum('wac,wdc->ad', temp, right, preferred_element_type=F32)]
    convert_element_type x6, other arithmetic: 1.06 us -> 2.76 us  [the longest x2 1.96 us: combine(): return total.astype(BF16).reshape(-1, rows, width)]
    lt x2 -> x0, other arithmetic: 1.55 us -> none  [the longest x1 0.82 us: body(): col_ids[None, None, :] < dims[:, None, None]]
    another operation x2 -> x0, local copies, waits for them, and re-layouts: 1.47 us -> none  [apply_hamiltonian(): outgoing = jnp.tile(rows_of_z, (count // CORES, 1, 1))]
  transfers between devices with their start and end apart: 11 -> 11, of which waited for: 6 -> 6; matrix products, arithmetic and copies ran while one was open for 7% -> 6% of each run, Pallas kernels for 0% -> 0%
where the time goes in v2:
time: 132 us
  starting transfers between devices  72.9 us (55%)
  waiting for transfers between devices  32.4 us (25%)
  blocking collectives  10.6 us (8%)
  other arithmetic  6.99 us (5%)
  matrix products  3.66 us (3%)
  local copies, waits for them, and re-layouts  2.64 us (2%)
  between operations  2.28 us (2%)
    all_to_all x5, starting transfers between devices, exchange(): return lax.all_to_all(blocks, axes, 0, 0, tiled=True)  47.3 us
    all_to_all x5, waiting for transfers between devices, exchange(): return lax.all_to_all(blocks, axes, 0, 0, tiled=True)  30.6 us
    ppermute x1, starting transfers between devices, body(): lax.ppermute(right_env, 'core', swap)  12.3 us
    all_to_all x1, blocking collectives, exchange(): return lax.all_to_all(blocks, axes, 0, 0, tiled=True)  10.6 us
    ppermute x2, starting transfers between devices, combine(): low = lax.ppermute(vector, BLK, forward)  8.66 us
    dot_general x2, matrix products, product(): part = jnp.einsum('wac,wdc->ad', temp, right, preferred_element_type=F32)  3.66 us
  transfers between devices with their start and end apart: 11, of which 6 were waited for; matrix products, arithmetic and copies ran while one was open for 6% of the time, Pallas kernels for 0%

profile of v2, /device:TPU:1, one launch (start us, length us, event | category | flops | bytes accessed | tf_op | source)
XLA Modules:
  0.0 131.5 jit_solution(15260403105157286617)
XLA Ops:
  0.7 1.0 fusion.19
  1.6 1.3 collective-permute-start.3
  2.9 4.7 %collective-permute-start.2 = (bf16[2,64,384]{2,1,0:T(8,128)(2,1)S(1)}, bf16[2,64,384]{2,1,0:T(8,128)(2,1)S(1)}, u32[]{:S(2)}, u32[]{:S(2)}) collective-permute-start(bf16[2,64,384]{2,1,0:T(8,128)(2,1)S(1)} %fusion.19), channel_id=1, source_target_pairs={{0,6},{6,12},{12,18},{18,24},{24,30},{30,36},{36,42},{42,48},{48,5... | collective-permute-start | bytes 294920 | tf_op jit(solution)/shard_map/ppermute | solution.py:33
  7.6 12.3 %collective-permute-start.1 = (bf16[2,384,384]{2,1,0:T(8,128)(2,1)}, bf16[2,384,384]{2,1,0:T(8,128)(2,1)S(1)}, u32[]{:S(2)}, u32[]{:S(2)}) collective-permute-start(bf16[2,384,384]{2,1,0:T(8,128)(2,1)} %param.9), channel_id=1, source_target_pairs={{0,1},{1,0},{2,3},{3,2},{4,5},{5,4},{6,7},{7,6},{8,9},{9,8},{10,11... | collective-permute-start | bytes 1769480 | tf_op jit(solution)/shard_map/ppermute | solution.py:75
  19.9 0.7 convert_element_type.37
  21.3 1.0 fusion.12
  22.3 3.4 %all-to-all-start = ((bf16[6,64,384]{2,1,0:T(8,128)(2,1)}), bf16[6,64,384]{2,1,0:T(8,128)(2,1)S(1)}, u32[]{:S(2)}, u32[]{:S(2)}) async-start(bf16[6,64,384]{2,1,0:T(8,128)(2,1)} %fusion.12), calls=%async_computation | async-start | bytes 589824 | tf_op jit(solution)/shard_map/all_to_all | solution.py:18
  25.9 2.1 %collective-permute-start = (bf16[2,384,384]{2,1,0:T(8,128)(2,1)S(1)}, bf16[2,384,384]{2,1,0:T(8,128)(2,1)S(1)}, u32[]{:S(2)}, u32[]{:S(2)}) collective-permute-start(bf16[2,384,384]{2,1,0:T(8,128)(2,1)S(1)} %get-tuple-element.14), channel_id=1, source_target_pairs={{0,1},{1,0},{2,3},{3,2},{4,5},{5,4},{6,7},{7,6},{8,9},{9,8},{10,11... | collective-permute-start | bytes 1769480 | tf_op jit(solution)/shard_map/ppermute | solution.py:74
  28.0 0.1 pad_maximum_fusion.1
  28.1 1.8 %collective-permute-done = bf16[2,384,384]{2,1,0:T(8,128)(2,1)S(1)} collective-permute-done((bf16[2,384,384]{2,1,0:T(8,128)(2,1)S(1)}, bf16[2,384,384]{2,1,0:T(8,128)(2,1)S(1)}, u32[]{:S(2)}, u32[]{:S(2)}) %collective-permute-start) | collective-permute-done | bytes 589856 | tf_op jit(solution)/shard_map/ppermute | solution.py:74
  29.9 0.1 pad_maximum_fusion
  30.0 3.1 %all-to-all-done = bf16[6,64,384]{2,1,0:T(8,128)(2,1)S(1)} async-done(((bf16[6,64,384]{2,1,0:T(8,128)(2,1)}), bf16[6,64,384]{2,1,0:T(8,128)(2,1)S(1)}, u32[]{:S(2)}, u32[]{:S(2)}) %all-to-all-start) | async-done | bytes 294944 | tf_op jit(solution)/shard_map/all_to_all | solution.py:18
  33.2 1.5 %fusion.4 = bf16[384,384]{1,0:T(8,128)(2,1)S(1)} fusion(bf16[4,384,384]{2,1,0:T(8,128)(2,1)S(1)} %pad_maximum_fusion.1, bf16[4,384,384]{2,1,0:T(8,128)(2,1)S(1)} %pad_maximum_fusion, bf16[384,384,1]{1,0,2:T(8,128)(2,1)S(1)} %bitcast.101), kind=kOutput, calls=%fused_computation.6 | convolution fusion | flops 906706944 | bytes 2949120 | tf_op jit(solution)/shard_map/wac,wdc->ad/dot_general | solution.py:47
  34.6 10.6 %all_to_all.30 = bf16[6,64,384]{2,1,0:T(8,128)(2,1)S(1)} all-to-all(bf16[6,64,384]{2,1,0:T(8,128)(2,1)S(1)} %bitcast.103), channel_id=1, replica_groups=mesh['z_hi'=4,'x'=4,'y'=8,'z_lo'=3,'core'=2] {'z_lo','core'}, dimensions={0} | all-to-all | bytes 589824 | tf_op jit(solution)/shard_map/all_to_all | solution.py:18
  45.3 0.8 fusion.16
  46.1 1.3 collective-permute-start.5
  47.4 4.0 %collective-permute-start.4 = (bf16[2,64,384]{2,1,0:T(8,128)(2,1)S(1)}, bf16[2,64,384]{2,1,0:T(8,128)(2,1)S(1)}, u32[]{:S(2)}, u32[]{:S(2)}) collective-permute-start(bf16[2,64,384]{2,1,0:T(8,128)(2,1)S(1)} %convert_element_type.42), channel_id=1, source_target_pairs={{0,6},{6,12},{12,18},{18,24},{24,30},{30,36},{36,42},{42,48},{48,5... | collective-permute-start | bytes 294920 | tf_op jit(solution)/shard_map/ppermute | solution.py:33
  51.4 1.3 compare_select_fusion
  52.7 0.6 broadcast_in_dim.20
  53.3 18.1 %all-to-all-start.3 = ((f32[32,1,128]{2,1,0:T(1,128)}), f32[32,1,128]{2,1,0:T(1,128)S(1)}, u32[]{:S(2)}, u32[]{:S(2)}) async-start(f32[32,1,128]{2,1,0:T(1,128)} %broadcast_in_dim.20), calls=%async_computation.3 | async-start | bytes 32768 | tf_op jit(solution)/shard_map/all_to_all | solution.py:18
  71.5 1.0 fusion.7
  72.5 7.4 %all-to-all-done.3 = f32[32,1,128]{2,1,0:T(1,128)S(1)} async-done(((f32[32,1,128]{2,1,0:T(1,128)}), f32[32,1,128]{2,1,0:T(1,128)S(1)}, u32[]{:S(2)}, u32[]{:S(2)}) %all-to-all-start.3) | async-done | bytes 16416 | tf_op jit(solution)/shard_map/all_to_all | solution.py:18
  79.9 6.1 %all-to-all-start.2 = ((bf16[6,64,384]{2,1,0:T(8,128)(2,1)}), bf16[6,64,384]{2,1,0:T(8,128)(2,1)S(1)}, u32[]{:S(2)}, u32[]{:S(2)}) async-start(bf16[6,64,384]{2,1,0:T(8,128)(2,1)} %fusion.7), calls=%async_computation.2 | async-start | bytes 589824 | tf_op jit(solution)/shard_map/all_to_all | solution.py:18
  86.1 7.5 %all-to-all-done.2 = bf16[6,64,384]{2,1,0:T(8,128)(2,1)S(1)} async-done(((bf16[6,64,384]{2,1,0:T(8,128)(2,1)}), bf16[6,64,384]{2,1,0:T(8,128)(2,1)S(1)}, u32[]{:S(2)}, u32[]{:S(2)}) %all-to-all-start.2) | async-done | bytes 294944 | tf_op jit(solution)/shard_map/all_to_all | solution.py:18
  93.5 0.6 broadcast_in_dim.21
  94.2 15.7 %all-to-all-start.5 = ((f32[24,1,128]{2,1,0:T(1,128)}), f32[24,1,128]{2,1,0:T(1,128)S(1)}, u32[]{:S(2)}, u32[]{:S(2)}) async-start(f32[24,1,128]{2,1,0:T(1,128)} %broadcast_in_dim.21), calls=%async_computation.5 | async-start | bytes 24576 | tf_op jit(solution)/shard_map/all_to_all | solution.py:18
  109.8 2.2 %fusion.5 = bf16[384,384]{1,0:T(8,128)(2,1)} fusion(bf16[4,384,384]{2,1,0:T(8,128)(2,1)S(1)} %pad_maximum_fusion.1, bf16[4,384,384]{2,1,0:T(8,128)(2,1)S(1)} %pad_maximum_fusion, bf16[384,384,1]{1,0,2:T(8,128)(2,1)S(1)} %bitcast.102), kind=kOutput, calls=%fused_computation.7 | convolution fusion | flops 906706944 | bytes 2949120 | tf_op jit(solution)/shard_map/wac,wdc->ad/dot_general | solution.py:47
  112.0 7.2 %all-to-all-done.5 = f32[24,1,128]{2,1,0:T(1,128)S(1)} async-done(((f32[24,1,128]{2,1,0:T(1,128)}), f32[24,1,128]{2,1,0:T(1,128)S(1)}, u32[]{:S(2)}, u32[]{:S(2)}) %all-to-all-start.5) | async-done | bytes 12320 | tf_op jit(solution)/shard_map/all_to_all | solution.py:18
  119.2 4.0 %all-to-all-start.4 = ((bf16[6,64,384]{2,1,0:T(8,128)(2,1)}), bf16[6,64,384]{2,1,0:T(8,128)(2,1)S(1)}, u32[]{:S(2)}, u32[]{:S(2)}) async-start(bf16[6,64,384]{2,1,0:T(8,128)(2,1)} %bitcast.21), calls=%async_computation.4 | async-start | bytes 589824 | tf_op jit(solution)/shard_map/all_to_all | solution.py:18
  123.2 0.6 fusion.23
  125.2 5.5 %all-to-all-done.4 = bf16[6,64,384]{2,1,0:T(8,128)(2,1)S(1)} async-done(((bf16[6,64,384]{2,1,0:T(8,128)(2,1)}), bf16[6,64,384]{2,1,0:T(8,128)(2,1)S(1)}, u32[]{:S(2)}, u32[]{:S(2)}) %all-to-all-start.4) | async-done | bytes 294944 | tf_op jit(solution)/shard_map/all_to_all | solution.py:18
  130.7 0.8 multiply_subtract_fusion
  (34 shorter events, 1.1 us)
Async XLA Ops:
  1.6 19.5 %collective-permute-start.3 = (bf16[2,64,384]{2,1,0:T(8,128)(2,1)S(1)}, bf16[2,64,384]{2,1,0:T(8,128)(2,1)S(1)}, u32[]{:S(2)}, u32[]{:S(2)}) collective-permute-start(bf16[2,64,384]{2,1,0:T(8,128)(2,1)S(1)} %fusion.19), channel_id=1, source_target_pairs={{6,0},{12,6},{18,12},{24,18},{30,24},{36,30},{42,36},{48,42},{54,4... | collective-permute-start | bytes 294920 | tf_op jit(solution)/shard_map/ppermute | solution.py:34
  2.9 18.2 %collective-permute-start.2 = (bf16[2,64,384]{2,1,0:T(8,128)(2,1)S(1)}, bf16[2,64,384]{2,1,0:T(8,128)(2,1)S(1)}, u32[]{:S(2)}, u32[]{:S(2)}) collective-permute-start(bf16[2,64,384]{2,1,0:T(8,128)(2,1)S(1)} %fusion.19), channel_id=1, source_target_pairs={{0,6},{6,12},{12,18},{18,24},{24,30},{30,36},{36,42},{42,48},{48,5... | collective-permute-start | bytes 294920 | tf_op jit(solution)/shard_map/ppermute | solution.py:33
  7.6 20.3 %collective-permute-start.1 = (bf16[2,384,384]{2,1,0:T(8,128)(2,1)}, bf16[2,384,384]{2,1,0:T(8,128)(2,1)S(1)}, u32[]{:S(2)}, u32[]{:S(2)}) collective-permute-start(bf16[2,384,384]{2,1,0:T(8,128)(2,1)} %param.9), channel_id=1, source_target_pairs={{0,1},{1,0},{2,3},{3,2},{4,5},{5,4},{6,7},{7,6},{8,9},{9,8},{10,11... | collective-permute-start | bytes 1769480 | tf_op jit(solution)/shard_map/ppermute | solution.py:75
  21.3 4.4 %copy-start.1 = (bf16[2,2,384,384]{3,2,1,0:T(8,128)(2,1)S(1)}, bf16[2,2,384,384]{3,2,1,0:T(8,128)(2,1)}, u32[]{:S(2)}) copy-start(bf16[2,2,384,384]{3,2,1,0:T(8,128)(2,1)} %param.8) | copy-start | bytes 3538948
  22.3 10.9 %all-to-all-start = ((bf16[6,64,384]{2,1,0:T(8,128)(2,1)}), bf16[6,64,384]{2,1,0:T(8,128)(2,1)S(1)}, u32[]{:S(2)}, u32[]{:S(2)}) async-start(bf16[6,64,384]{2,1,0:T(8,128)(2,1)} %fusion.12), calls=%async_computation | async-start | bytes 589824 | tf_op jit(solution)/shard_map/all_to_all | solution.py:18
  25.7 2.2 %copy-start.2 = (bf16[2,384,384]{2,1,0:T(8,128)(2,1)S(1)}, bf16[2,384,384]{2,1,0:T(8,128)(2,1)}, u32[]{:S(2)}) copy-start(bf16[2,384,384]{2,1,0:T(8,128)(2,1)} %param.9) | copy-start | bytes 1769476
  25.9 4.0 %collective-permute-start = (bf16[2,384,384]{2,1,0:T(8,128)(2,1)S(1)}, bf16[2,384,384]{2,1,0:T(8,128)(2,1)S(1)}, u32[]{:S(2)}, u32[]{:S(2)}) collective-permute-start(bf16[2,384,384]{2,1,0:T(8,128)(2,1)S(1)} %get-tuple-element.14), channel_id=1, source_target_pairs={{0,1},{1,0},{2,3},{3,2},{4,5},{5,4},{6,7},{7,6},{8,9},{9,8},{10,11... | collective-permute-start | bytes 1769480 | tf_op jit(solution)/shard_map/ppermute | solution.py:74
  33.2 12.1 %copy-start.3 = (bf16[2,64,384]{2,1,0:T(8,128)(2,1)S(1)}, bf16[2,64,384]{2,1,0:T(8,128)(2,1)}, u32[]{:S(2)}) copy-start(bf16[2,64,384]{2,1,0:T(8,128)(2,1)} %param.5) | copy-start | bytes 294916
  33.2 12.1 %copy-start.4 = (s32[2]{0:T(128)S(1)}, s32[2]{0:T(128)}, u32[]{:S(2)}) copy-start(s32[2]{0:T(128)} %param.6) | copy-start | bytes 28
  46.1 84.7 %copy-start = (f32[2,64,384]{2,1,0:T(8,128)}, f32[2,64,384]{2,1,0:T(8,128)S(1)}, u32[]{:S(2)}) copy-start(f32[2,64,384]{2,1,0:T(8,128)S(1)} %get-tuple-element.12) | copy-start | bytes 589828
  46.1 25.3 %collective-permute-start.5 = (bf16[2,64,384]{2,1,0:T(8,128)(2,1)S(1)}, bf16[2,64,384]{2,1,0:T(8,128)(2,1)S(1)}, u32[]{:S(2)}, u32[]{:S(2)}) collective-permute-start(bf16[2,64,384]{2,1,0:T(8,128)(2,1)S(1)} %convert_element_type.42), channel_id=1, source_target_pairs={{6,0},{12,6},{18,12},{24,18},{30,24},{36,30},{42,36},{48,42},{54,4... | collective-permute-start | bytes 294920 | tf_op jit(solution)/shard_map/ppermute | solution.py:34
  47.4 24.0 %collective-permute-start.4 = (bf16[2,64,384]{2,1,0:T(8,128)(2,1)S(1)}, bf16[2,64,384]{2,1,0:T(8,128)(2,1)S(1)}, u32[]{:S(2)}, u32[]{:S(2)}) collective-permute-start(bf16[2,64,384]{2,1,0:T(8,128)(2,1)S(1)} %convert_element_type.42), channel_id=1, source_target_pairs={{0,6},{6,12},{12,18},{18,24},{24,30},{30,36},{36,42},{42,48},{48,5... | collective-permute-start | bytes 294920 | tf_op jit(solution)/shard_map/ppermute | solution.py:33
  53.3 26.6 %all-to-all-start.3 = ((f32[32,1,128]{2,1,0:T(1,128)}), f32[32,1,128]{2,1,0:T(1,128)S(1)}, u32[]{:S(2)}, u32[]{:S(2)}) async-start(f32[32,1,128]{2,1,0:T(1,128)} %broadcast_in_dim.20), calls=%async_computation.3 | async-start | bytes 32768 | tf_op jit(solution)/shard_map/all_to_all | solution.py:18
  79.9 13.6 %all-to-all-start.2 = ((bf16[6,64,384]{2,1,0:T(8,128)(2,1)}), bf16[6,64,384]{2,1,0:T(8,128)(2,1)S(1)}, u32[]{:S(2)}, u32[]{:S(2)}) async-start(bf16[6,64,384]{2,1,0:T(8,128)(2,1)} %fusion.7), calls=%async_computation.2 | async-start | bytes 589824 | tf_op jit(solution)/shard_map/all_to_all | solution.py:18
  94.2 25.0 %all-to-all-start.5 = ((f32[24,1,128]{2,1,0:T(1,128)}), f32[24,1,128]{2,1,0:T(1,128)S(1)}, u32[]{:S(2)}, u32[]{:S(2)}) async-start(f32[24,1,128]{2,1,0:T(1,128)} %broadcast_in_dim.21), calls=%async_computation.5 | async-start | bytes 24576 | tf_op jit(solution)/shard_map/all_to_all | solution.py:18
  119.2 11.5 %all-to-all-start.4 = ((bf16[6,64,384]{2,1,0:T(8,128)(2,1)}), bf16[6,64,384]{2,1,0:T(8,128)(2,1)S(1)}, u32[]{:S(2)}, u32[]{:S(2)}) async-start(bf16[6,64,384]{2,1,0:T(8,128)(2,1)} %bitcast.21), calls=%async_computation.4 | async-start | bytes 589824 | tf_op jit(solution)/shard_map/all_to_all | solution.py:18

commit v3 on v2

--- a/solution.py
+++ b/solution.py
@@ -8,8 +8,7 @@
 SPLIT = {"z_hi": 4, "x": 4, "y": 8, "z_lo": 3, "core": 2}
 BLK = ("z_hi", "x", "y")
 COL = ("z_lo", "core")
-NEAR = ("x", "y")
-FAR = ("z_hi", "z_lo", "core")
+NEAR = ("x", "y", "core")
 F32 = jnp.float32
 BF16 = jnp.bfloat16
 
@@ -28,10 +27,12 @@
 
 def combine(vector, coeff):
     count = lax.axis_size(BLK)
-    forward = [(i, i + 1) for i in range(count - 1)]
-    backward = [(target, source) for source, target in forward]
-    low = lax.ppermute(vector, BLK, forward)
-    high = lax.ppermute(vector, BLK, backward)
+    near = [(i, i ^ 1) for i in range(count)]
+    across = [(i, i + 1 if i % 2 else i - 1) for i in range(1, count - 1)]
+    other = lax.ppermute(vector, BLK, across)
+    partner = lax.ppermute(vector, BLK, near)
+    odd = lax.rem(lax.axis_index(BLK), 2) == 1
+    low, high = jnp.where(odd, partner, other), jnp.where(odd, other, partner)
     padded = jnp.concatenate([low, vector, high], axis=0).astype(F32)
     sectors, rows, width = vector.shape
     total = jnp.zeros(coeff.shape[:2] + (rows, width), F32)
@@ -54,8 +55,17 @@
     return jnp.sum(parts, axis=0) * scale
 
 
-def gathered(values, axes):
-    return exchange(jnp.broadcast_to(values[None, None, :], (lax.axis_size(axes), 1, LANES)), axes)
+def sum_by_exchange(values, axes):
+    copies = jnp.broadcast_to(values[None], (lax.axis_size(axes), 1, LANES))
+    return jnp.sum(exchange(copies, axes), axis=0)
+
+
+def sum_by_permutes(values, axis, distances):
+    count = lax.axis_size(axis)
+    total = values
+    for distance in distances:
+        total = total + lax.ppermute(values, axis, [(i, (i + distance) % count) for i in range(count)])
+    return total
 
 
 def body(psi, dims, pattern, left_env, right_env):
@@ -77,15 +87,18 @@
     parts = exchange(product(exchange(outgoing, COL), left, right), COL)
     sigma = masked(reduced(parts, sectors, scale), dims)
     vector = psi_m.astype(F32)
-    products = jnp.where(
-        jnp.arange(LANES) < LANES // 2, jnp.sum(vector * sigma), jnp.sum(vector * vector)
-    )
-    sums = jnp.sum(gathered(products, NEAR), axis=(0, 1))
-    z = exchange(combine(sigma.astype(BF16), coeff), COL)
-    z, sums = lax.optimization_barrier((z, sums))
-    sums = jnp.sum(gathered(sums, FAR), axis=(0, 1))
-    parts = exchange(product(z, left, right), COL)
-    theta = sums[0] / sums[LANES // 2]
+    lane = lax.broadcasted_iota(jnp.int32, (1, LANES), 1)
+    products = jnp.where(lane < LANES // 2, jnp.sum(vector * sigma), jnp.sum(vector * vector))
+    outgoing = combine(sigma.astype(BF16), coeff)
+    sums = sum_by_exchange(products, NEAR)
+    outgoing, sums = lax.optimization_barrier((outgoing, sums))
+    sums = sum_by_permutes(sums, "z_hi", (2,))
+    part = product(exchange(outgoing, COL), left, right)
+    part, sums = lax.optimization_barrier((part, sums))
+    sums = sum_by_permutes(sums, "z_lo", (1, 2))
+    sums = sum_by_permutes(sums, "z_hi", (1,))
+    parts = exchange(part, COL)
+    theta = sums[0, 0] / sums[0, LANES // 2]
     second = masked(reduced(parts, sectors, scale), dims) - theta * sigma
     return (sigma, second)
 

time: 132 us -> 126 us (0.955)
  blocking collectives: 10.6 us -> 39.1 us
  waiting for transfers between devices: 32.4 us -> 12.1 us
  starting transfers between devices: 72.9 us -> 59.6 us
    all_to_all x5 -> x3, starting transfers between devices: 47.3 us -> 13.1 us  [exchange(): return lax.all_to_all(blocks, axes, 0, 0, tiled=True)]
    all_to_all x1 -> x2, blocking collectives: 10.6 us -> 39.1 us  [exchange(): return lax.all_to_all(blocks, axes, 0, 0, tiled=True)]
    all_to_all x5 -> x3, waiting for transfers between devices: 30.6 us -> 3.19 us  [exchange(): return lax.all_to_all(blocks, axes, 0, 0, tiled=True)]
    ppermute x4 -> x8, starting transfers between devices: 11.2 us -> 36.6 us  [the longest x4 25.2 us: sum_by_permutes(): lax.ppermute(values, axis, [(i, (i + distance) % count) for i in range(co...]
    ppermute x4 -> x8, waiting for transfers between devices: 0.01 us -> 7.2 us  [the longest x4 7.19 us: sum_by_permutes(): lax.ppermute(values, axis, [(i, (i + distance) % count) for i in range(co...]
    ppermute x1, starting transfers between devices: 12.3 us -> 7.78 us  [body(): lax.ppermute(right_env, 'core', swap)]
  transfers between devices with their start and end apart: 11 -> 13, of which waited for: 6 -> 5; matrix products, arithmetic and copies ran while one was open for 6% -> 4% of each run, Pallas kernels for 0% -> 0%
where the time goes in v3:
time: 126 us; the launch traced here: 125 us
  starting transfers between devices  59.6 us (47%)
  blocking collectives  39.1 us (31%)
  waiting for transfers between devices  12.1 us (10%)
  other arithmetic  7 us (6%)
  matrix products  3.65 us (3%)
  between operations  2.25 us (2%)
  local copies, waits for them, and re-layouts  1.42 us (1%)
    all_to_all x2, blocking collectives, exchange(): return lax.all_to_all(blocks, axes, 0, 0, tiled=True)  39.1 us
    ppermute x4, starting transfers between devices, sum_by_permutes(): lax.ppermute(values, axis, [(i, (i + distance) % count) for i in range(co...  25.2 us
    all_to_all x3, starting transfers between devices, exchange(): return lax.all_to_all(blocks, axes, 0, 0, tiled=True)  13.1 us
    ppermute x2, starting transfers between devices, combine(): partner = lax.ppermute(vector, BLK, near)  10 us
    ppermute x1, starting transfers between devices, body(): lax.ppermute(right_env, 'core', swap)  7.78 us
    ppermute x4, waiting for transfers between devices, sum_by_permutes(): lax.ppermute(values, axis, [(i, (i + distance) % count) for i in range(co...  7.19 us
    dot_general x2, matrix products, product(): part = jnp.einsum('wac,wdc->ad', temp, right, preferred_element_type=F32)  3.65 us
    all_to_all x3, waiting for transfers between devices, exchange(): return lax.all_to_all(blocks, axes, 0, 0, tiled=True)  3.19 us
  transfers between devices with their start and end apart: 13, of which 5 were waited for; matrix products, arithmetic and copies ran while one was open for 4% of the time, Pallas kernels for 0%

profile of v3, /device:TPU:1, one launch (start us, length us, event | category | flops | bytes accessed | tf_op | source)
XLA Modules:
  0.0 125.1 jit_solution(5133393936664128178)
XLA Ops:
  0.7 1.0 fusion.19
  1.6 0.7 collective-permute-start.3
  2.3 6.6 %collective-permute-start.2 = (bf16[2,64,384]{2,1,0:T(8,128)(2,1)S(1)}, bf16[2,64,384]{2,1,0:T(8,128)(2,1)S(1)}, u32[]{:S(2)}, u32[]{:S(2)}) collective-permute-start(bf16[2,64,384]{2,1,0:T(8,128)(2,1)S(1)} %fusion.19), channel_id=1, source_target_pairs={{0,6},{6,0},{12,18},{18,12},{24,30},{30,24},{36,42},{42,36},{48,54... | collective-permute-start | bytes 294920 | tf_op jit(solution)/shard_map/ppermute | solution.py:33
  8.9 7.8 %collective-permute-start.1 = (bf16[2,384,384]{2,1,0:T(8,128)(2,1)}, bf16[2,384,384]{2,1,0:T(8,128)(2,1)S(1)}, u32[]{:S(2)}, u32[]{:S(2)}) collective-permute-start(bf16[2,384,384]{2,1,0:T(8,128)(2,1)} %param.9), channel_id=1, source_target_pairs={{0,1},{1,0},{2,3},{3,2},{4,5},{5,4},{6,7},{7,6},{8,9},{9,8},{10,11... | collective-permute-start | bytes 1769480 | tf_op jit(solution)/shard_map/ppermute | solution.py:85
  16.7 0.7 convert_element_type.37
  18.1 1.0 fusion.12
  19.1 4.8 %all-to-all-start = ((bf16[6,64,384]{2,1,0:T(8,128)(2,1)}), bf16[6,64,384]{2,1,0:T(8,128)(2,1)S(1)}, u32[]{:S(2)}, u32[]{:S(2)}) async-start(bf16[6,64,384]{2,1,0:T(8,128)(2,1)} %fusion.12), calls=%async_computation | async-start | bytes 589824 | tf_op jit(solution)/shard_map/all_to_all | solution.py:17
  24.0 2.1 %collective-permute-start = (bf16[2,384,384]{2,1,0:T(8,128)(2,1)S(1)}, bf16[2,384,384]{2,1,0:T(8,128)(2,1)S(1)}, u32[]{:S(2)}, u32[]{:S(2)}) collective-permute-start(bf16[2,384,384]{2,1,0:T(8,128)(2,1)S(1)} %get-tuple-element.18), channel_id=1, source_target_pairs={{0,1},{1,0},{2,3},{3,2},{4,5},{5,4},{6,7},{7,6},{8,9},{9,8},{10,11... | collective-permute-start | bytes 1769480 | tf_op jit(solution)/shard_map/ppermute | solution.py:84
  26.2 0.1 pad_maximum_fusion.1
  26.3 1.7 %collective-permute-done = bf16[2,384,384]{2,1,0:T(8,128)(2,1)S(1)} collective-permute-done((bf16[2,384,384]{2,1,0:T(8,128)(2,1)S(1)}, bf16[2,384,384]{2,1,0:T(8,128)(2,1)S(1)}, u32[]{:S(2)}, u32[]{:S(2)}) %collective-permute-start) | collective-permute-done | bytes 589856 | tf_op jit(solution)/shard_map/ppermute | solution.py:84
  28.0 0.1 pad_maximum_fusion
  28.2 3.2 %all-to-all-done = bf16[6,64,384]{2,1,0:T(8,128)(2,1)S(1)} async-done(((bf16[6,64,384]{2,1,0:T(8,128)(2,1)}), bf16[6,64,384]{2,1,0:T(8,128)(2,1)S(1)}, u32[]{:S(2)}, u32[]{:S(2)}) %all-to-all-start) | async-done | bytes 294944 | tf_op jit(solution)/shard_map/all_to_all | solution.py:17
  31.4 1.5 %fusion.4 = bf16[384,384]{1,0:T(8,128)(2,1)S(1)} fusion(bf16[4,384,384]{2,1,0:T(8,128)(2,1)S(1)} %pad_maximum_fusion.1, bf16[4,384,384]{2,1,0:T(8,128)(2,1)S(1)} %pad_maximum_fusion, bf16[384,384,1]{1,0,2:T(8,128)(2,1)S(1)} %bitcast.101), kind=kOutput, calls=%fused_computation.6 | convolution fusion | flops 906706944 | bytes 2949120 | tf_op jit(solution)/shard_map/wac,wdc->ad/dot_general | solution.py:48
  32.8 10.6 %all_to_all.25 = bf16[6,64,384]{2,1,0:T(8,128)(2,1)S(1)} all-to-all(bf16[6,64,384]{2,1,0:T(8,128)(2,1)S(1)} %bitcast.103), channel_id=1, replica_groups=mesh['z_hi'=4,'x'=4,'y'=8,'z_lo'=3,'core'=2] {'z_lo','core'}, dimensions={0} | all-to-all | bytes 589824 | tf_op jit(solution)/shard_map/all_to_all | solution.py:17
  43.5 0.8 fusion.16
  44.3 0.7 collective-permute-start.5
  45.0 3.5 %collective-permute-start.4 = (bf16[2,64,384]{2,1,0:T(8,128)(2,1)S(1)}, bf16[2,64,384]{2,1,0:T(8,128)(2,1)S(1)}, u32[]{:S(2)}, u32[]{:S(2)}) collective-permute-start(bf16[2,64,384]{2,1,0:T(8,128)(2,1)S(1)} %convert_element_type.42), channel_id=1, source_target_pairs={{0,6},{6,0},{12,18},{18,12},{24,30},{30,24},{36,42},{42,36},{48,54... | collective-permute-start | bytes 294920 | tf_op jit(solution)/shard_map/ppermute | solution.py:33
  48.4 1.3 %compare_select_fusion = f32[128]{0:T(128)S(1)} fusion(f32[]{:T(128)} %get-tuple-element.15, f32[]{:T(128)} %get-tuple-element.14), kind=kLoop, calls=%fused_computation.49 | loop fusion | flops 256 | bytes 520 | tf_op jit(solution)/shard_map/jit(_where)/select_n | solution.py:91
  49.7 28.5 %all_to_all.26 = f32[64,1,128]{2,1,0:T(1,128)S(1)} all-to-all(f32[64,1,128]{2,1,0:T(1,128)S(1)} %broadcast_in_dim.18), channel_id=1, replica_groups=mesh['z_hi'=4,'x'=4,'y'=8,'z_lo'=3,'core'=2] {'x','y','core'}, dimensions={0} | all-to-all | bytes 65536 | tf_op jit(solution)/shard_map/all_to_all | solution.py:17
  78.5 1.0 fusion.7
  79.4 4.0 %all-to-all-start.3 = ((bf16[6,64,384]{2,1,0:T(8,128)(2,1)}), bf16[6,64,384]{2,1,0:T(8,128)(2,1)S(1)}, u32[]{:S(2)}, u32[]{:S(2)}) async-start(bf16[6,64,384]{2,1,0:T(8,128)(2,1)} %fusion.7), calls=%async_computation.3 | async-start | bytes 589824 | tf_op jit(solution)/shard_map/all_to_all | solution.py:17
  83.5 9.3 %collective-permute-start.6 = (f32[1,128]{1,0:T(1,128)S(1)}, f32[1,128]{1,0:T(1,128)S(1)}, u32[]{:S(2)}, u32[]{:S(2)}) collective-permute-start(f32[1,128]{1,0:T(1,128)S(1)} %bitcast.105), channel_id=1, source_target_pairs={{0,384},{192,576},{384,0},{576,192},{1,385},{193,577},{385,1},{577... | collective-permute-start | bytes 1544 | tf_op jit(solution)/shard_map/ppermute | solution.py:67
  92.8 3.2 %collective-permute-done.6 = f32[1,128]{1,0:T(1,128)S(1)} collective-permute-done((f32[1,128]{1,0:T(1,128)S(1)}, f32[1,128]{1,0:T(1,128)S(1)}, u32[]{:S(2)}, u32[]{:S(2)}) %collective-permute-start.6) | collective-permute-done | bytes 544 | tf_op jit(solution)/shard_map/ppermute | solution.py:67
  96.0 2.2 %fusion.5 = bf16[384,384]{1,0:T(8,128)(2,1)} fusion(bf16[4,384,384]{2,1,0:T(8,128)(2,1)S(1)} %pad_maximum_fusion.1, bf16[4,384,384]{2,1,0:T(8,128)(2,1)S(1)} %pad_maximum_fusion, bf16[384,384,1]{1,0,2:T(8,128)(2,1)S(1)} %bitcast.102), kind=kOutput, calls=%fused_computation.7 | convolution fusion | flops 906706944 | bytes 2949120 | tf_op jit(solution)/shard_map/wac,wdc->ad/dot_general | solution.py:48
  98.2 4.3 %all-to-all-start.4 = ((bf16[6,64,384]{2,1,0:T(8,128)(2,1)}), bf16[6,64,384]{2,1,0:T(8,128)(2,1)S(1)}, u32[]{:S(2)}, u32[]{:S(2)}) async-start(bf16[6,64,384]{2,1,0:T(8,128)(2,1)} %bitcast.22), calls=%async_computation.4 | async-start | bytes 589824 | tf_op jit(solution)/shard_map/all_to_all | solution.py:17
  102.5 4.2 %collective-permute-start.8 = (f32[1,128]{1,0:T(1,128)S(1)}, f32[1,128]{1,0:T(1,128)S(1)}, u32[]{:S(2)}, u32[]{:S(2)}) collective-permute-start(f32[1,128]{1,0:T(1,128)S(1)} %add.91), channel_id=1, source_target_pairs={{0,4},{2,0},{4,2},{1,5},{3,1},{5,3},{6,10},{8,6},{10,8},{7,11},{9,... | collective-permute-start | bytes 1544 | tf_op jit(solution)/shard_map/ppermute | solution.py:67
  106.7 1.9 %collective-permute-start.7 = (f32[1,128]{1,0:T(1,128)S(1)}, f32[1,128]{1,0:T(1,128)S(1)}, u32[]{:S(2)}, u32[]{:S(2)}) collective-permute-start(f32[1,128]{1,0:T(1,128)S(1)} %add.91), channel_id=1, source_target_pairs={{0,2},{2,4},{4,0},{1,3},{3,5},{5,1},{6,8},{8,10},{10,6},{7,9},{9,1... | collective-permute-start | bytes 1544 | tf_op jit(solution)/shard_map/ppermute | solution.py:67
  108.6 3.2 %collective-permute-done.7 = f32[1,128]{1,0:T(1,128)S(1)} collective-permute-done((f32[1,128]{1,0:T(1,128)S(1)}, f32[1,128]{1,0:T(1,128)S(1)}, u32[]{:S(2)}, u32[]{:S(2)}) %collective-permute-start.7) | collective-permute-done | bytes 544 | tf_op jit(solution)/shard_map/ppermute | solution.py:67
  111.9 9.8 %collective-permute-start.9 = (f32[1,128]{1,0:T(1,128)S(1)}, f32[1,128]{1,0:T(1,128)S(1)}, u32[]{:S(2)}, u32[]{:S(2)}) collective-permute-start(f32[1,128]{1,0:T(1,128)S(1)} %add_add_fusion), channel_id=1, source_target_pairs={{0,192},{192,384},{384,576},{576,0},{1,193},{193,385},{385,577},{5... | collective-permute-start | bytes 1544 | tf_op jit(solution)/shard_map/ppermute | solution.py:67
  121.7 0.7 collective-permute-done.9
  122.4 0.6 fusion.23
  124.3 0.8 multiply_subtract_fusion
  (42 shorter events, 1.1 us)
Async XLA Ops:
  1.6 16.2 %collective-permute-start.3 = (bf16[2,64,384]{2,1,0:T(8,128)(2,1)S(1)}, bf16[2,64,384]{2,1,0:T(8,128)(2,1)S(1)}, u32[]{:S(2)}, u32[]{:S(2)}) collective-permute-start(bf16[2,64,384]{2,1,0:T(8,128)(2,1)S(1)} %fusion.19), channel_id=1, source_target_pairs={{6,12},{12,6},{18,24},{24,18},{30,36},{36,30},{42,48},{48,42},{54,... | collective-permute-start | bytes 294920 | tf_op jit(solution)/shard_map/ppermute | solution.py:32
  2.3 15.6 %collective-permute-start.2 = (bf16[2,64,384]{2,1,0:T(8,128)(2,1)S(1)}, bf16[2,64,384]{2,1,0:T(8,128)(2,1)S(1)}, u32[]{:S(2)}, u32[]{:S(2)}) collective-permute-start(bf16[2,64,384]{2,1,0:T(8,128)(2,1)S(1)} %fusion.19), channel_id=1, source_target_pairs={{0,6},{6,0},{12,18},{18,12},{24,30},{30,24},{36,42},{42,36},{48,54... | collective-permute-start | bytes 294920 | tf_op jit(solution)/shard_map/ppermute | solution.py:33
  8.9 17.2 %collective-permute-start.1 = (bf16[2,384,384]{2,1,0:T(8,128)(2,1)}, bf16[2,384,384]{2,1,0:T(8,128)(2,1)S(1)}, u32[]{:S(2)}, u32[]{:S(2)}) collective-permute-start(bf16[2,384,384]{2,1,0:T(8,128)(2,1)} %param.9), channel_id=1, source_target_pairs={{0,1},{1,0},{2,3},{3,2},{4,5},{5,4},{6,7},{7,6},{8,9},{9,8},{10,11... | collective-permute-start | bytes 1769480 | tf_op jit(solution)/shard_map/ppermute | solution.py:85
  18.1 5.8 %copy-start.1 = (bf16[2,2,384,384]{3,2,1,0:T(8,128)(2,1)S(1)}, bf16[2,2,384,384]{3,2,1,0:T(8,128)(2,1)}, u32[]{:S(2)}) copy-start(bf16[2,2,384,384]{3,2,1,0:T(8,128)(2,1)} %param.8) | copy-start | bytes 3538948
  19.1 12.3 %all-to-all-start = ((bf16[6,64,384]{2,1,0:T(8,128)(2,1)}), bf16[6,64,384]{2,1,0:T(8,128)(2,1)S(1)}, u32[]{:S(2)}, u32[]{:S(2)}) async-start(bf16[6,64,384]{2,1,0:T(8,128)(2,1)} %fusion.12), calls=%async_computation | async-start | bytes 589824 | tf_op jit(solution)/shard_map/all_to_all | solution.py:17
  23.9 2.3 %copy-start.2 = (bf16[2,384,384]{2,1,0:T(8,128)(2,1)S(1)}, bf16[2,384,384]{2,1,0:T(8,128)(2,1)}, u32[]{:S(2)}) copy-start(bf16[2,384,384]{2,1,0:T(8,128)(2,1)} %param.9) | copy-start | bytes 1769476
  24.0 4.0 %collective-permute-start = (bf16[2,384,384]{2,1,0:T(8,128)(2,1)S(1)}, bf16[2,384,384]{2,1,0:T(8,128)(2,1)S(1)}, u32[]{:S(2)}, u32[]{:S(2)}) collective-permute-start(bf16[2,384,384]{2,1,0:T(8,128)(2,1)S(1)} %get-tuple-element.18), channel_id=1, source_target_pairs={{0,1},{1,0},{2,3},{3,2},{4,5},{5,4},{6,7},{7,6},{8,9},{9,8},{10,11... | collective-permute-start | bytes 1769480 | tf_op jit(solution)/shard_map/ppermute | solution.py:84
  31.4 12.1 %copy-start.3 = (bf16[2,64,384]{2,1,0:T(8,128)(2,1)S(1)}, bf16[2,64,384]{2,1,0:T(8,128)(2,1)}, u32[]{:S(2)}) copy-start(bf16[2,64,384]{2,1,0:T(8,128)(2,1)} %param.5) | copy-start | bytes 294916
  31.4 12.1 %copy-start.4 = (s32[2]{0:T(128)S(1)}, s32[2]{0:T(128)}, u32[]{:S(2)}) copy-start(s32[2]{0:T(128)} %param.6) | copy-start | bytes 28
  44.3 80.1 %copy-start = (f32[2,64,384]{2,1,0:T(8,128)}, f32[2,64,384]{2,1,0:T(8,128)S(1)}, u32[]{:S(2)}) copy-start(f32[2,64,384]{2,1,0:T(8,128)S(1)} %get-tuple-element.16) | copy-start | bytes 589828
  44.3 34.0 %collective-permute-start.5 = (bf16[2,64,384]{2,1,0:T(8,128)(2,1)S(1)}, bf16[2,64,384]{2,1,0:T(8,128)(2,1)S(1)}, u32[]{:S(2)}, u32[]{:S(2)}) collective-permute-start(bf16[2,64,384]{2,1,0:T(8,128)(2,1)S(1)} %convert_element_type.42), channel_id=1, source_target_pairs={{6,12},{12,6},{18,24},{24,18},{30,36},{36,30},{42,48},{48,42},{54,... | collective-permute-start | bytes 294920 | tf_op jit(solution)/shard_map/ppermute | solution.py:32
  45.0 33.3 %collective-permute-start.4 = (bf16[2,64,384]{2,1,0:T(8,128)(2,1)S(1)}, bf16[2,64,384]{2,1,0:T(8,128)(2,1)S(1)}, u32[]{:S(2)}, u32[]{:S(2)}) collective-permute-start(bf16[2,64,384]{2,1,0:T(8,128)(2,1)S(1)} %convert_element_type.42), channel_id=1, source_target_pairs={{0,6},{6,0},{12,18},{18,12},{24,30},{30,24},{36,42},{42,36},{48,54... | collective-permute-start | bytes 294920 | tf_op jit(solution)/shard_map/ppermute | solution.py:33
  79.4 16.6 %all-to-all-start.3 = ((bf16[6,64,384]{2,1,0:T(8,128)(2,1)}), bf16[6,64,384]{2,1,0:T(8,128)(2,1)S(1)}, u32[]{:S(2)}, u32[]{:S(2)}) async-start(bf16[6,64,384]{2,1,0:T(8,128)(2,1)} %fusion.7), calls=%async_computation.3 | async-start | bytes 589824 | tf_op jit(solution)/shard_map/all_to_all | solution.py:17
  83.5 12.5 %collective-permute-start.6 = (f32[1,128]{1,0:T(1,128)S(1)}, f32[1,128]{1,0:T(1,128)S(1)}, u32[]{:S(2)}, u32[]{:S(2)}) collective-permute-start(f32[1,128]{1,0:T(1,128)S(1)} %bitcast.105), channel_id=1, source_target_pairs={{0,384},{192,576},{384,0},{576,192},{1,385},{193,577},{385,1},{577... | collective-permute-start | bytes 1544 | tf_op jit(solution)/shard_map/ppermute | solution.py:67
  98.2 26.1 %all-to-all-start.4 = ((bf16[6,64,384]{2,1,0:T(8,128)(2,1)}), bf16[6,64,384]{2,1,0:T(8,128)(2,1)S(1)}, u32[]{:S(2)}, u32[]{:S(2)}) async-start(bf16[6,64,384]{2,1,0:T(8,128)(2,1)} %bitcast.22), calls=%async_computation.4 | async-start | bytes 589824 | tf_op jit(solution)/shard_map/all_to_all | solution.py:17
  102.5 6.1 %collective-permute-start.8 = (f32[1,128]{1,0:T(1,128)S(1)}, f32[1,128]{1,0:T(1,128)S(1)}, u32[]{:S(2)}, u32[]{:S(2)}) collective-permute-start(f32[1,128]{1,0:T(1,128)S(1)} %add.91), channel_id=1, source_target_pairs={{0,4},{2,0},{4,2},{1,5},{3,1},{5,3},{6,10},{8,6},{10,8},{7,11},{9,... | collective-permute-start | bytes 1544 | tf_op jit(solution)/shard_map/ppermute | solution.py:67
  106.7 5.2 %collective-permute-start.7 = (f32[1,128]{1,0:T(1,128)S(1)}, f32[1,128]{1,0:T(1,128)S(1)}, u32[]{:S(2)}, u32[]{:S(2)}) collective-permute-start(f32[1,128]{1,0:T(1,128)S(1)} %add.91), channel_id=1, source_target_pairs={{0,2},{2,4},{4,0},{1,3},{3,5},{5,1},{6,8},{8,10},{10,6},{7,9},{9,1... | collective-permute-start | bytes 1544 | tf_op jit(solution)/shard_map/ppermute | solution.py:67
  111.9 10.5 %collective-permute-start.9 = (f32[1,128]{1,0:T(1,128)S(1)}, f32[1,128]{1,0:T(1,128)S(1)}, u32[]{:S(2)}, u32[]{:S(2)}) collective-permute-start(f32[1,128]{1,0:T(1,128)S(1)} %add_add_fusion), channel_id=1, source_target_pairs={{0,192},{192,384},{384,576},{576,0},{1,193},{193,385},{385,577},{5... | collective-permute-start | bytes 1544 | tf_op jit(solution)/shard_map/ppermute | solution.py:67

commit v4 on v3

--- a/solution.py
+++ b/solution.py
@@ -56,16 +56,27 @@
 
 
 def sum_by_exchange(values, axes):
-    copies = jnp.broadcast_to(values[None], (lax.axis_size(axes), 1, LANES))
+    copies = jnp.broadcast_to(values[None], (lax.axis_size(axes),) + values.shape)
     return jnp.sum(exchange(copies, axes), axis=0)
 
 
-def sum_by_permutes(values, axis, distances):
-    count = lax.axis_size(axis)
-    total = values
-    for distance in distances:
-        total = total + lax.ppermute(values, axis, [(i, (i + distance) % count) for i in range(count)])
-    return total
+def own_share(values):
+    count = lax.axis_size("z_hi")
+    steps = [(h, (h + d) % count) for d in (1, 2, 3) for h in range(count)]
+    place = {d: [(CORES * h, CORES * t) for h, t in steps if (t - h) % count == d] for d in (1, 3)}
+    place[2] = [(CORES * h + 1, CORES * t + 1) for h, t in steps if (t - h) % count == 2]
+    first = lax.ppermute(values, ("z_hi", "core"), place[1] + place[2])
+    last = lax.ppermute(values, ("z_hi", "core"), place[3])
+    own = jnp.where(lax.axis_index("core") == 0, values, jnp.zeros_like(values))
+    return own + first + last
+
+
+def in_thirds(values, shape):
+    high = lax.reduce_precision(values, 8, 7)
+    middle = lax.reduce_precision(values - high, 8, 7)
+    low = values - high - middle
+    rows = jnp.stack([high, middle, low, jnp.zeros_like(low)], axis=1).astype(BF16)
+    return jnp.broadcast_to(rows.reshape(1, -1, shape[2]), (shape[0], 8, shape[2]))
 
 
 def body(psi, dims, pattern, left_env, right_env):
@@ -87,19 +98,18 @@
     parts = exchange(product(exchange(outgoing, COL), left, right), COL)
     sigma = masked(reduced(parts, sectors, scale), dims)
     vector = psi_m.astype(F32)
-    lane = lax.broadcasted_iota(jnp.int32, (1, LANES), 1)
-    products = jnp.where(lane < LANES // 2, jnp.sum(vector * sigma), jnp.sum(vector * vector))
+    products = jnp.stack([jnp.sum(vector * sigma, axis=(0, 1)), jnp.sum(vector * vector, axis=(0, 1))])
+    sums = sum_by_exchange(products, NEAR)
     outgoing = combine(sigma.astype(BF16), coeff)
-    sums = sum_by_exchange(products, NEAR)
     outgoing, sums = lax.optimization_barrier((outgoing, sums))
-    sums = sum_by_permutes(sums, "z_hi", (2,))
+    share = own_share(sums)
     part = product(exchange(outgoing, COL), left, right)
-    part, sums = lax.optimization_barrier((part, sums))
-    sums = sum_by_permutes(sums, "z_lo", (1, 2))
-    sums = sum_by_permutes(sums, "z_hi", (1,))
-    parts = exchange(part, COL)
-    theta = sums[0, 0] / sums[0, LANES // 2]
-    second = masked(reduced(parts, sectors, scale), dims) - theta * sigma
+    sent = jnp.concatenate([part, in_thirds(share, part.shape)], axis=1)
+    parts = exchange(sent, COL)
+    rows = part.shape[1]
+    sums = jnp.sum(parts[:, rows:].astype(F32).reshape(count, 2, 4, -1), axis=(0, 2, 3))
+    theta = sums[0] / sums[1]
+    second = masked(reduced(parts[:, :rows], sectors, scale), dims) - theta * sigma
     return (sigma, second)
 
 

time: 126 us -> 119 us (0.944)
  blocking collectives: 39.1 us -> 24.1 us
  waiting for transfers between devices: 12.1 us -> 17.2 us
  starting transfers between devices: 59.6 us -> 63.5 us
  other arithmetic: 7 us -> 5.56 us
    all_to_all x2, blocking collectives: 39.1 us -> 24.1 us  [exchange(): return lax.all_to_all(blocks, axes, 0, 0, tiled=True)]
    all_to_all x3, starting transfers between devices: 13.1 us -> 27.7 us  [exchange(): return lax.all_to_all(blocks, axes, 0, 0, tiled=True)]
    ppermute x4 -> x2, starting transfers between devices: 25.2 us -> 12.4 us  [the longest x1 11.8 us: own_share(): first = lax.ppermute(values, ('z_hi', 'core'), place[1] + place[2])]
    all_to_all x3, waiting for transfers between devices: 3.19 us -> 12.9 us  [exchange(): return lax.all_to_all(blocks, axes, 0, 0, tiled=True)]
    ppermute x4 -> x2, waiting for transfers between devices: 7.19 us -> 2.57 us  [the longest x1 2.57 us: own_share(): first = lax.ppermute(values, ('z_hi', 'core'), place[1] + place[2])]
    ppermute x1, starting transfers between devices: 7.78 us -> 10.3 us  [body(): lax.ppermute(right_env, 'core', swap)]
    select_n x1 -> x0, other arithmetic: 1.28 us -> none  [body(): jnp.where(lane < LANES // 2, jnp.sum(vector * sigma), jnp.sum(vector * ve...]
  transfers between devices with their start and end apart: 13 -> 11, of which waited for: 5 -> 4; matrix products, arithmetic and copies ran while one was open for 4% -> 4% of each run, Pallas kernels for 0% -> 0%
where the time goes in v4:
time: 119 us; the launch traced here: 118 us
  starting transfers between devices  63.5 us (53%)
  blocking collectives  24.1 us (20%)
  waiting for transfers between devices  17.2 us (14%)
  other arithmetic  5.56 us (5%)
  matrix products  2.94 us (2%)
  local copies, waits for them, and re-layouts  2.36 us (2%)
  between operations  2.34 us (2%)
    all_to_all x3, starting transfers between devices, exchange(): return lax.all_to_all(blocks, axes, 0, 0, tiled=True)  27.7 us
    all_to_all x2, blocking collectives, exchange(): return lax.all_to_all(blocks, axes, 0, 0, tiled=True)  24.1 us
    all_to_all x3, waiting for transfers between devices, exchange(): return lax.all_to_all(blocks, axes, 0, 0, tiled=True)  12.9 us
    ppermute x1, starting transfers between devices, own_share(): first = lax.ppermute(values, ('z_hi', 'core'), place[1] + place[2])  11.8 us
    ppermute x1, starting transfers between devices, body(): lax.ppermute(right_env, 'core', swap)  10.3 us
    ppermute x2, starting transfers between devices, combine(): partner = lax.ppermute(vector, BLK, near)  9.6 us
    dot_general x2, matrix products, product(): part = jnp.einsum('wac,wdc->ad', temp, right, preferred_element_type=F32)  2.94 us
    ppermute x1, waiting for transfers between devices, own_share(): first = lax.ppermute(values, ('z_hi', 'core'), place[1] + place[2])  2.57 us
  transfers between devices with their start and end apart: 11, of which 4 were waited for; matrix products, arithmetic and copies ran while one was open for 4% of the time, Pallas kernels for 0%

profile of v4, /device:TPU:1, one launch (start us, length us, event | category | flops | bytes accessed | tf_op | source)
XLA Modules:
  0.0 118.1 jit_solution(4670874408541784677)
XLA Ops:
  0.7 1.0 fusion.19
  1.6 4.0 %collective-permute-start.2 = (bf16[2,64,384]{2,1,0:T(8,128)(2,1)S(1)}, bf16[2,64,384]{2,1,0:T(8,128)(2,1)S(1)}, u32[]{:S(2)}, u32[]{:S(2)}) collective-permute-start(bf16[2,64,384]{2,1,0:T(8,128)(2,1)S(1)} %fusion.19), channel_id=1, source_target_pairs={{0,6},{6,0},{12,18},{18,12},{24,30},{30,24},{36,42},{42,36},{48,54... | collective-permute-start | bytes 294920 | tf_op jit(solution)/shard_map/ppermute | solution.py:33
  5.7 0.7 collective-permute-start.3
  6.4 10.3 %collective-permute-start.1 = (bf16[2,384,384]{2,1,0:T(8,128)(2,1)}, bf16[2,384,384]{2,1,0:T(8,128)(2,1)S(1)}, u32[]{:S(2)}, u32[]{:S(2)}) collective-permute-start(bf16[2,384,384]{2,1,0:T(8,128)(2,1)} %param.9), channel_id=1, source_target_pairs={{0,1},{1,0},{2,3},{3,2},{4,5},{5,4},{6,7},{7,6},{8,9},{9,8},{10,11... | collective-permute-start | bytes 1769480 | tf_op jit(solution)/shard_map/ppermute | solution.py:96
  16.7 0.7 convert_element_type.48
  18.1 1.0 fusion.12
  19.1 4.1 %all-to-all-start = ((bf16[6,64,384]{2,1,0:T(8,128)(2,1)}), bf16[6,64,384]{2,1,0:T(8,128)(2,1)S(1)}, u32[]{:S(2)}, u32[]{:S(2)}) async-start(bf16[6,64,384]{2,1,0:T(8,128)(2,1)} %fusion.12), calls=%async_computation | async-start | bytes 589824 | tf_op jit(solution)/shard_map/all_to_all | solution.py:17
  23.2 0.1 dynamic-slice_bitcast_fusion.1
  23.4 2.1 %collective-permute-start = (bf16[2,384,384]{2,1,0:T(8,128)(2,1)S(1)}, bf16[2,384,384]{2,1,0:T(8,128)(2,1)S(1)}, u32[]{:S(2)}, u32[]{:S(2)}) collective-permute-start(bf16[2,384,384]{2,1,0:T(8,128)(2,1)S(1)} %get-tuple-element.16), channel_id=1, source_target_pairs={{0,1},{1,0},{2,3},{3,2},{4,5},{5,4},{6,7},{7,6},{8,9},{9,8},{10,11... | collective-permute-start | bytes 1769480 | tf_op jit(solution)/shard_map/ppermute | solution.py:95
  25.5 0.1 pad_maximum_fusion.1
  25.7 1.7 %collective-permute-done = bf16[2,384,384]{2,1,0:T(8,128)(2,1)S(1)} collective-permute-done((bf16[2,384,384]{2,1,0:T(8,128)(2,1)S(1)}, bf16[2,384,384]{2,1,0:T(8,128)(2,1)S(1)}, u32[]{:S(2)}, u32[]{:S(2)}) %collective-permute-start) | collective-permute-done | bytes 589856 | tf_op jit(solution)/shard_map/ppermute | solution.py:95
  27.4 0.1 pad_maximum_fusion
  27.5 3.2 %all-to-all-done = bf16[6,64,384]{2,1,0:T(8,128)(2,1)S(1)} async-done(((bf16[6,64,384]{2,1,0:T(8,128)(2,1)}), bf16[6,64,384]{2,1,0:T(8,128)(2,1)S(1)}, u32[]{:S(2)}, u32[]{:S(2)}) %all-to-all-start) | async-done | bytes 294944 | tf_op jit(solution)/shard_map/all_to_all | solution.py:17
  30.7 1.5 %fusion.4 = bf16[384,384]{1,0:T(8,128)(2,1)S(1)} fusion(bf16[4,384,384]{2,1,0:T(8,128)(2,1)S(1)} %pad_maximum_fusion.1, bf16[4,384,384]{2,1,0:T(8,128)(2,1)S(1)} %pad_maximum_fusion, bf16[384,384,1]{1,0,2:T(8,128)(2,1)S(1)} %bitcast.107), kind=kOutput, calls=%fused_computation.6 | convolution fusion | flops 906706944 | bytes 2949120 | tf_op jit(solution)/shard_map/wac,wdc->ad/dot_general | solution.py:48
  32.2 10.6 %all_to_all.25 = bf16[6,64,384]{2,1,0:T(8,128)(2,1)S(1)} all-to-all(bf16[6,64,384]{2,1,0:T(8,128)(2,1)S(1)} %bitcast.108), channel_id=1, replica_groups=mesh['z_hi'=4,'x'=4,'y'=8,'z_lo'=3,'core'=2] {'z_lo','core'}, dimensions={0} | all-to-all | bytes 589824 | tf_op jit(solution)/shard_map/all_to_all | solution.py:17
  42.8 0.1 fusion.16
  43.0 5.6 %collective-permute-start.4 = (bf16[2,64,384]{2,1,0:T(8,128)(2,1)S(1)}, bf16[2,64,384]{2,1,0:T(8,128)(2,1)S(1)}, u32[]{:S(2)}, u32[]{:S(2)}) collective-permute-start(bf16[2,64,384]{2,1,0:T(8,128)(2,1)S(1)} %convert_element_type.53), channel_id=1, source_target_pairs={{0,6},{6,0},{12,18},{18,12},{24,30},{30,24},{36,42},{42,36},{48,54... | collective-permute-start | bytes 294920 | tf_op jit(solution)/shard_map/ppermute | solution.py:33
  48.6 0.7 collective-permute-start.5
  49.3 0.7 broadcast_in_dim.12
  50.0 20.0 %all-to-all-start.2 = ((f32[64,2,384]{2,1,0:T(2,128)}), f32[64,2,384]{2,1,0:T(2,128)S(1)}, u32[]{:S(2)}, u32[]{:S(2)}) async-start(f32[64,2,384]{2,1,0:T(2,128)} %broadcast_in_dim.12), calls=%async_computation.2 | async-start | bytes 393216 | tf_op jit(solution)/shard_map/all_to_all | solution.py:17
  70.2 1.0 fusion.7
  71.2 9.8 %all-to-all-done.2 = f32[64,2,384]{2,1,0:T(2,128)S(1)} async-done(((f32[64,2,384]{2,1,0:T(2,128)}), f32[64,2,384]{2,1,0:T(2,128)S(1)}, u32[]{:S(2)}, u32[]{:S(2)}) %all-to-all-start.2) | async-done | bytes 196640 | tf_op jit(solution)/shard_map/all_to_all | solution.py:17
  81.1 3.5 %all-to-all-start.3 = ((bf16[6,64,384]{2,1,0:T(8,128)(2,1)}), bf16[6,64,384]{2,1,0:T(8,128)(2,1)S(1)}, u32[]{:S(2)}, u32[]{:S(2)}) async-start(bf16[6,64,384]{2,1,0:T(8,128)(2,1)} %fusion.7), calls=%async_computation.3 | async-start | bytes 589824 | tf_op jit(solution)/shard_map/all_to_all | solution.py:17
  84.6 11.8 %collective-permute-start.6 = (f32[2,384]{1,0:T(2,128)S(1)}, f32[2,384]{1,0:T(2,128)S(1)}, u32[]{:S(2)}, u32[]{:S(2)}) collective-permute-start(f32[2,384]{1,0:T(2,128)S(1)} %reduce_sum.64), channel_id=1, source_target_pairs={{0,192},{192,384},{384,576},{576,0},{1,385},{193,577},{385,1},{577... | collective-permute-start | bytes 9224 | tf_op jit(solution)/shard_map/ppermute | solution.py:68
  96.4 0.7 collective-permute-start.7
  97.1 2.6 %collective-permute-done.6 = f32[2,384]{1,0:T(2,128)S(1)} collective-permute-done((f32[2,384]{1,0:T(2,128)S(1)}, f32[2,384]{1,0:T(2,128)S(1)}, u32[]{:S(2)}, u32[]{:S(2)}) %collective-permute-start.6) | collective-permute-done | bytes 3104 | tf_op jit(solution)/shard_map/ppermute | solution.py:68
  99.8 1.5 %fusion.5 = bf16[384,384]{1,0:T(8,128)(2,1)S(1)} fusion(bf16[4,384,384]{2,1,0:T(8,128)(2,1)S(1)} %pad_maximum_fusion.1, bf16[4,384,384]{2,1,0:T(8,128)(2,1)S(1)} %pad_maximum_fusion, bf16[384,384,1]{1,0,2:T(8,128)(2,1)S(1)} %bitcast.106), kind=kOutput, calls=%fused_computation.7 | convolution fusion | flops 906706944 | bytes 2949120 | tf_op jit(solution)/shard_map/wac,wdc->ad/dot_general | solution.py:48
  101.4 13.5 %all_to_all.26 = bf16[6,72,384]{2,1,0:T(8,128)(2,1)S(1)} all-to-all(bf16[6,72,384]{2,1,0:T(8,128)(2,1)S(1)} %pad_maximum_fusion.2), channel_id=1, replica_groups=mesh['z_hi'=4,'x'=4,'y'=8,'z_lo'=3,'core'=2] {'z_lo','core'}, dimensions={0} | all-to-all | bytes 663552 | tf_op jit(solution)/shard_map/all_to_all | solution.py:17
  114.9 0.1 convert_reduce_fusion.2
  115.1 0.1 reduce_sum.68
  115.2 0.6 fusion.27
  117.3 0.8 multiply_subtract_fusion
  (49 shorter events, 1.4 us)
Async XLA Ops:
  1.6 16.2 %collective-permute-start.2 = (bf16[2,64,384]{2,1,0:T(8,128)(2,1)S(1)}, bf16[2,64,384]{2,1,0:T(8,128)(2,1)S(1)}, u32[]{:S(2)}, u32[]{:S(2)}) collective-permute-start(bf16[2,64,384]{2,1,0:T(8,128)(2,1)S(1)} %fusion.19), channel_id=1, source_target_pairs={{0,6},{6,0},{12,18},{18,12},{24,30},{30,24},{36,42},{42,36},{48,54... | collective-permute-start | bytes 294920 | tf_op jit(solution)/shard_map/ppermute | solution.py:33
  5.7 12.2 %collective-permute-start.3 = (bf16[2,64,384]{2,1,0:T(8,128)(2,1)S(1)}, bf16[2,64,384]{2,1,0:T(8,128)(2,1)S(1)}, u32[]{:S(2)}, u32[]{:S(2)}) collective-permute-start(bf16[2,64,384]{2,1,0:T(8,128)(2,1)S(1)} %fusion.19), channel_id=1, source_target_pairs={{6,12},{12,6},{18,24},{24,18},{30,36},{36,30},{42,48},{48,42},{54,... | collective-permute-start | bytes 294920 | tf_op jit(solution)/shard_map/ppermute | solution.py:32
  6.4 19.1 %collective-permute-start.1 = (bf16[2,384,384]{2,1,0:T(8,128)(2,1)}, bf16[2,384,384]{2,1,0:T(8,128)(2,1)S(1)}, u32[]{:S(2)}, u32[]{:S(2)}) collective-permute-start(bf16[2,384,384]{2,1,0:T(8,128)(2,1)} %param.9), channel_id=1, source_target_pairs={{0,1},{1,0},{2,3},{3,2},{4,5},{5,4},{6,7},{7,6},{8,9},{9,8},{10,11... | collective-permute-start | bytes 1769480 | tf_op jit(solution)/shard_map/ppermute | solution.py:96
  18.1 5.1 %copy-start.1 = (bf16[2,2,384,384]{3,2,1,0:T(8,128)(2,1)S(1)}, bf16[2,2,384,384]{3,2,1,0:T(8,128)(2,1)}, u32[]{:S(2)}) copy-start(bf16[2,2,384,384]{3,2,1,0:T(8,128)(2,1)} %param.8) | copy-start | bytes 3538948
  19.1 11.6 %all-to-all-start = ((bf16[6,64,384]{2,1,0:T(8,128)(2,1)}), bf16[6,64,384]{2,1,0:T(8,128)(2,1)S(1)}, u32[]{:S(2)}, u32[]{:S(2)}) async-start(bf16[6,64,384]{2,1,0:T(8,128)(2,1)} %fusion.12), calls=%async_computation | async-start | bytes 589824 | tf_op jit(solution)/shard_map/all_to_all | solution.py:17
  23.2 2.3 %copy-start.2 = (bf16[2,384,384]{2,1,0:T(8,128)(2,1)S(1)}, bf16[2,384,384]{2,1,0:T(8,128)(2,1)}, u32[]{:S(2)}) copy-start(bf16[2,384,384]{2,1,0:T(8,128)(2,1)} %param.9) | copy-start | bytes 1769476
  23.4 4.0 %collective-permute-start = (bf16[2,384,384]{2,1,0:T(8,128)(2,1)S(1)}, bf16[2,384,384]{2,1,0:T(8,128)(2,1)S(1)}, u32[]{:S(2)}, u32[]{:S(2)}) collective-permute-start(bf16[2,384,384]{2,1,0:T(8,128)(2,1)S(1)} %get-tuple-element.16), channel_id=1, source_target_pairs={{0,1},{1,0},{2,3},{3,2},{4,5},{5,4},{6,7},{7,6},{8,9},{9,8},{10,11... | collective-permute-start | bytes 1769480 | tf_op jit(solution)/shard_map/ppermute | solution.py:95
  30.7 12.1 %copy-start.3 = (bf16[2,64,384]{2,1,0:T(8,128)(2,1)S(1)}, bf16[2,64,384]{2,1,0:T(8,128)(2,1)}, u32[]{:S(2)}) copy-start(bf16[2,64,384]{2,1,0:T(8,128)(2,1)} %param.5) | copy-start | bytes 294916
  30.7 12.1 %copy-start.4 = (s32[2]{0:T(128)S(1)}, s32[2]{0:T(128)}, u32[]{:S(2)}) copy-start(s32[2]{0:T(128)} %param.6) | copy-start | bytes 28
  43.0 74.3 %copy-start = (f32[2,64,384]{2,1,0:T(8,128)}, f32[2,64,384]{2,1,0:T(8,128)S(1)}, u32[]{:S(2)}) copy-start(f32[2,64,384]{2,1,0:T(8,128)S(1)} %get-tuple-element.14) | copy-start | bytes 589828
  43.0 27.0 %collective-permute-start.4 = (bf16[2,64,384]{2,1,0:T(8,128)(2,1)S(1)}, bf16[2,64,384]{2,1,0:T(8,128)(2,1)S(1)}, u32[]{:S(2)}, u32[]{:S(2)}) collective-permute-start(bf16[2,64,384]{2,1,0:T(8,128)(2,1)S(1)} %convert_element_type.53), channel_id=1, source_target_pairs={{0,6},{6,0},{12,18},{18,12},{24,30},{30,24},{36,42},{42,36},{48,54... | collective-permute-start | bytes 294920 | tf_op jit(solution)/shard_map/ppermute | solution.py:33
  48.6 21.5 %collective-permute-start.5 = (bf16[2,64,384]{2,1,0:T(8,128)(2,1)S(1)}, bf16[2,64,384]{2,1,0:T(8,128)(2,1)S(1)}, u32[]{:S(2)}, u32[]{:S(2)}) collective-permute-start(bf16[2,64,384]{2,1,0:T(8,128)(2,1)S(1)} %convert_element_type.53), channel_id=1, source_target_pairs={{6,12},{12,6},{18,24},{24,18},{30,36},{36,30},{42,48},{48,42},{54,... | collective-permute-start | bytes 294920 | tf_op jit(solution)/shard_map/ppermute | solution.py:32
  50.0 31.0 %all-to-all-start.2 = ((f32[64,2,384]{2,1,0:T(2,128)}), f32[64,2,384]{2,1,0:T(2,128)S(1)}, u32[]{:S(2)}, u32[]{:S(2)}) async-start(f32[64,2,384]{2,1,0:T(2,128)} %broadcast_in_dim.12), calls=%async_computation.2 | async-start | bytes 393216 | tf_op jit(solution)/shard_map/all_to_all | solution.py:17
  81.1 18.8 %all-to-all-start.3 = ((bf16[6,64,384]{2,1,0:T(8,128)(2,1)}), bf16[6,64,384]{2,1,0:T(8,128)(2,1)S(1)}, u32[]{:S(2)}, u32[]{:S(2)}) async-start(bf16[6,64,384]{2,1,0:T(8,128)(2,1)} %fusion.7), calls=%async_computation.3 | async-start | bytes 589824 | tf_op jit(solution)/shard_map/all_to_all | solution.py:17
  84.6 15.1 %collective-permute-start.6 = (f32[2,384]{1,0:T(2,128)S(1)}, f32[2,384]{1,0:T(2,128)S(1)}, u32[]{:S(2)}, u32[]{:S(2)}) collective-permute-start(f32[2,384]{1,0:T(2,128)S(1)} %reduce_sum.64), channel_id=1, source_target_pairs={{0,192},{192,384},{384,576},{576,0},{1,385},{193,577},{385,1},{577... | collective-permute-start | bytes 9224 | tf_op jit(solution)/shard_map/ppermute | solution.py:68
  96.4 3.3 %collective-permute-start.7 = (f32[2,384]{1,0:T(2,128)S(1)}, f32[2,384]{1,0:T(2,128)S(1)}, u32[]{:S(2)}, u32[]{:S(2)}) collective-permute-start(f32[2,384]{1,0:T(2,128)S(1)} %reduce_sum.64), channel_id=1, source_target_pairs={{0,576},{192,0},{384,192},{576,384},{2,578},{194,2},{386,194},{578... | collective-permute-start | bytes 9224 | tf_op jit(solution)/shard_map/ppermute | solution.py:69

commit v5 on v4

--- a/solution.py
+++ b/solution.py
@@ -31,8 +31,8 @@
     across = [(i, i + 1 if i % 2 else i - 1) for i in range(1, count - 1)]
     other = lax.ppermute(vector, BLK, across)
     partner = lax.ppermute(vector, BLK, near)
-    odd = lax.rem(lax.axis_index(BLK), 2) == 1
-    low, high = jnp.where(odd, partner, other), jnp.where(odd, other, partner)
+    even = lax.rem(lax.axis_index(BLK), 2) == 0
+    low, high = jnp.where(even, other, partner), jnp.where(even, partner, other)
     padded = jnp.concatenate([low, vector, high], axis=0).astype(F32)
     sectors, rows, width = vector.shape
     total = jnp.zeros(coeff.shape[:2] + (rows, width), F32)
@@ -107,7 +107,9 @@
     sent = jnp.concatenate([part, in_thirds(share, part.shape)], axis=1)
     parts = exchange(sent, COL)
     rows = part.shape[1]
-    sums = jnp.sum(parts[:, rows:].astype(F32).reshape(count, 2, 4, -1), axis=(0, 2, 3))
+    sums = jnp.sum(parts[:, rows:].astype(F32).reshape(count, 2, 4, -1), axis=(0, 2))
+    sums = jnp.broadcast_to(jnp.sum(sums, axis=1, keepdims=True), sums.shape)
+    sums = lax.optimization_barrier(sums)
     theta = sums[0] / sums[1]
     second = masked(reduced(parts[:, :rows], sectors, scale), dims) - theta * sigma
     return (sigma, second)

time: 119 us -> 115 us (0.966)
  starting transfers between devices: 63.5 us -> 59 us
  blocking collectives: 24.1 us -> 26.7 us
  between operations: 2.34 us -> 0.97 us
    all_to_all x2, blocking collectives: 24.1 us -> 26.7 us  [exchange(): return lax.all_to_all(blocks, axes, 0, 0, tiled=True)]
    ppermute x1, starting transfers between devices: 10.3 us -> 7.78 us  [body(): lax.ppermute(right_env, 'core', swap)]
    ppermute x1, starting transfers between devices: 11.8 us -> 9.3 us  [own_share(): first = lax.ppermute(values, ('z_hi', 'core'), place[1] + place[2])]
where the time goes in v5:
time: 115 us; the launch traced here: 114 us
  starting transfers between devices  59 us (51%)
  blocking collectives  26.7 us (23%)
  waiting for transfers between devices  17.3 us (15%)
  other arithmetic  5.57 us (5%)
  matrix products  2.94 us (3%)
  local copies, waits for them, and re-layouts  1.84 us (2%)
    all_to_all x3, starting transfers between devices, exchange(): return lax.all_to_all(blocks, axes, 0, 0, tiled=True)  27.8 us
    all_to_all x2, blocking collectives, exchange(): return lax.all_to_all(blocks, axes, 0, 0, tiled=True)  26.7 us
    all_to_all x3, waiting for transfers between devices, exchange(): return lax.all_to_all(blocks, axes, 0, 0, tiled=True)  12.9 us
    ppermute x2, starting transfers between devices, combine(): partner = lax.ppermute(vector, BLK, near)  10 us
    ppermute x1, starting transfers between devices, own_share(): first = lax.ppermute(values, ('z_hi', 'core'), place[1] + place[2])  9.3 us
    ppermute x1, starting transfers between devices, body(): lax.ppermute(right_env, 'core', swap)  7.78 us
    dot_general x2, matrix products, product(): part = jnp.einsum('wac,wdc->ad', temp, right, preferred_element_type=F32)  2.94 us
    ppermute x1, waiting for transfers between devices, own_share(): first = lax.ppermute(values, ('z_hi', 'core'), place[1] + place[2])  2.58 us
  transfers between devices with their start and end apart: 11, of which 4 were waited for; matrix products, arithmetic and copies ran while one was open for 4% of the time, Pallas kernels for 0%

profile of v5, /device:TPU:1, one launch (start us, length us, event | category | flops | bytes accessed | tf_op | source)
XLA Modules:
  0.0 114.3 jit_solution(17648681708516728598)
XLA Ops:
  0.7 1.0 fusion.19
  1.6 0.7 collective-permute-start.2
  2.3 6.6 %collective-permute-start.3 = (bf16[2,64,384]{2,1,0:T(8,128)(2,1)S(1)}, bf16[2,64,384]{2,1,0:T(8,128)(2,1)S(1)}, u32[]{:S(2)}, u32[]{:S(2)}) collective-permute-start(bf16[2,64,384]{2,1,0:T(8,128)(2,1)S(1)} %fusion.19), channel_id=1, source_target_pairs={{0,6},{6,0},{12,18},{18,12},{24,30},{30,24},{36,42},{42,36},{48,54... | collective-permute-start | bytes 294920 | tf_op jit(solution)/shard_map/ppermute | solution.py:33
  8.9 7.8 %collective-permute-start.1 = (bf16[2,384,384]{2,1,0:T(8,128)(2,1)}, bf16[2,384,384]{2,1,0:T(8,128)(2,1)S(1)}, u32[]{:S(2)}, u32[]{:S(2)}) collective-permute-start(bf16[2,384,384]{2,1,0:T(8,128)(2,1)} %param.9), channel_id=1, source_target_pairs={{0,1},{1,0},{2,3},{3,2},{4,5},{5,4},{6,7},{7,6},{8,9},{9,8},{10,11... | collective-permute-start | bytes 1769480 | tf_op jit(solution)/shard_map/ppermute | solution.py:96
  16.7 0.7 convert_element_type.48
  17.4 0.1 copy.15
  18.1 1.0 fusion.12
  19.1 4.8 %all-to-all-start = ((bf16[6,64,384]{2,1,0:T(8,128)(2,1)}), bf16[6,64,384]{2,1,0:T(8,128)(2,1)S(1)}, u32[]{:S(2)}, u32[]{:S(2)}) async-start(bf16[6,64,384]{2,1,0:T(8,128)(2,1)} %fusion.12), calls=%async_computation | async-start | bytes 589824 | tf_op jit(solution)/shard_map/all_to_all | solution.py:17
  23.9 0.1 dynamic-slice_bitcast_fusion.1
  24.0 2.1 %collective-permute-start = (bf16[2,384,384]{2,1,0:T(8,128)(2,1)S(1)}, bf16[2,384,384]{2,1,0:T(8,128)(2,1)S(1)}, u32[]{:S(2)}, u32[]{:S(2)}) collective-permute-start(bf16[2,384,384]{2,1,0:T(8,128)(2,1)S(1)} %get-tuple-element.16), channel_id=1, source_target_pairs={{0,1},{1,0},{2,3},{3,2},{4,5},{5,4},{6,7},{7,6},{8,9},{9,8},{10,11... | collective-permute-start | bytes 1769480 | tf_op jit(solution)/shard_map/ppermute | solution.py:95
  26.2 0.1 pad_maximum_fusion.1
  26.3 1.7 %collective-permute-done = bf16[2,384,384]{2,1,0:T(8,128)(2,1)S(1)} collective-permute-done((bf16[2,384,384]{2,1,0:T(8,128)(2,1)S(1)}, bf16[2,384,384]{2,1,0:T(8,128)(2,1)S(1)}, u32[]{:S(2)}, u32[]{:S(2)}) %collective-permute-start) | collective-permute-done | bytes 589856 | tf_op jit(solution)/shard_map/ppermute | solution.py:95
  28.0 0.1 pad_maximum_fusion
  28.2 3.2 %all-to-all-done = bf16[6,64,384]{2,1,0:T(8,128)(2,1)S(1)} async-done(((bf16[6,64,384]{2,1,0:T(8,128)(2,1)}), bf16[6,64,384]{2,1,0:T(8,128)(2,1)S(1)}, u32[]{:S(2)}, u32[]{:S(2)}) %all-to-all-start) | async-done | bytes 294944 | tf_op jit(solution)/shard_map/all_to_all | solution.py:17
  31.4 1.5 %fusion.4 = bf16[384,384]{1,0:T(8,128)(2,1)S(1)} fusion(bf16[4,384,384]{2,1,0:T(8,128)(2,1)S(1)} %pad_maximum_fusion.1, bf16[4,384,384]{2,1,0:T(8,128)(2,1)S(1)} %pad_maximum_fusion, bf16[384,384,1]{1,0,2:T(8,128)(2,1)S(1)} %bitcast.106), kind=kOutput, calls=%fused_computation.6 | convolution fusion | flops 906706944 | bytes 2949120 | tf_op jit(solution)/shard_map/wac,wdc->ad/dot_general | solution.py:48
  32.8 10.6 %all_to_all.25 = bf16[6,64,384]{2,1,0:T(8,128)(2,1)S(1)} all-to-all(bf16[6,64,384]{2,1,0:T(8,128)(2,1)S(1)} %bitcast.107), channel_id=1, replica_groups=mesh['z_hi'=4,'x'=4,'y'=8,'z_lo'=3,'core'=2] {'z_lo','core'}, dimensions={0} | all-to-all | bytes 589824 | tf_op jit(solution)/shard_map/all_to_all | solution.py:17
  43.5 0.1 fusion.16
  43.7 0.7 collective-permute-start.4
  44.3 3.5 %collective-permute-start.5 = (bf16[2,64,384]{2,1,0:T(8,128)(2,1)S(1)}, bf16[2,64,384]{2,1,0:T(8,128)(2,1)S(1)}, u32[]{:S(2)}, u32[]{:S(2)}) collective-permute-start(bf16[2,64,384]{2,1,0:T(8,128)(2,1)S(1)} %convert_element_type.53), channel_id=1, source_target_pairs={{0,6},{6,0},{12,18},{18,12},{24,30},{30,24},{36,42},{42,36},{48,54... | collective-permute-start | bytes 294920 | tf_op jit(solution)/shard_map/ppermute | solution.py:33
  47.8 0.7 broadcast_in_dim.14
  48.6 19.4 %all-to-all-start.2 = ((f32[64,2,384]{2,1,0:T(2,128)}), f32[64,2,384]{2,1,0:T(2,128)S(1)}, u32[]{:S(2)}, u32[]{:S(2)}) async-start(f32[64,2,384]{2,1,0:T(2,128)} %broadcast_in_dim.14), calls=%async_computation.2 | async-start | bytes 393216 | tf_op jit(solution)/shard_map/all_to_all | solution.py:17
  68.2 1.0 fusion.7
  69.2 9.8 %all-to-all-done.2 = f32[64,2,384]{2,1,0:T(2,128)S(1)} async-done(((f32[64,2,384]{2,1,0:T(2,128)}), f32[64,2,384]{2,1,0:T(2,128)S(1)}, u32[]{:S(2)}, u32[]{:S(2)}) %all-to-all-start.2) | async-done | bytes 196640 | tf_op jit(solution)/shard_map/all_to_all | solution.py:17
  79.0 3.5 %all-to-all-start.3 = ((bf16[6,64,384]{2,1,0:T(8,128)(2,1)}), bf16[6,64,384]{2,1,0:T(8,128)(2,1)S(1)}, u32[]{:S(2)}, u32[]{:S(2)}) async-start(bf16[6,64,384]{2,1,0:T(8,128)(2,1)} %fusion.7), calls=%async_computation.3 | async-start | bytes 589824 | tf_op jit(solution)/shard_map/all_to_all | solution.py:17
  82.6 9.3 %collective-permute-start.6 = (f32[2,384]{1,0:T(2,128)S(1)}, f32[2,384]{1,0:T(2,128)S(1)}, u32[]{:S(2)}, u32[]{:S(2)}) collective-permute-start(f32[2,384]{1,0:T(2,128)S(1)} %reduce_sum.68), channel_id=1, source_target_pairs={{0,192},{192,384},{384,576},{576,0},{1,385},{193,577},{385,1},{577... | collective-permute-start | bytes 9224 | tf_op jit(solution)/shard_map/ppermute | solution.py:68
  91.9 0.7 collective-permute-start.7
  92.6 2.6 %collective-permute-done.6 = f32[2,384]{1,0:T(2,128)S(1)} collective-permute-done((f32[2,384]{1,0:T(2,128)S(1)}, f32[2,384]{1,0:T(2,128)S(1)}, u32[]{:S(2)}, u32[]{:S(2)}) %collective-permute-start.6) | collective-permute-done | bytes 3104 | tf_op jit(solution)/shard_map/ppermute | solution.py:68
  95.3 1.5 %fusion.5 = bf16[384,384]{1,0:T(8,128)(2,1)S(1)} fusion(bf16[4,384,384]{2,1,0:T(8,128)(2,1)S(1)} %pad_maximum_fusion.1, bf16[4,384,384]{2,1,0:T(8,128)(2,1)S(1)} %pad_maximum_fusion, bf16[384,384,1]{1,0,2:T(8,128)(2,1)S(1)} %bitcast.105), kind=kOutput, calls=%fused_computation.7 | convolution fusion | flops 906706944 | bytes 2949120 | tf_op jit(solution)/shard_map/wac,wdc->ad/dot_general | solution.py:48
  96.9 16.1 %all_to_all.26 = bf16[6,72,384]{2,1,0:T(8,128)(2,1)S(1)} all-to-all(bf16[6,72,384]{2,1,0:T(8,128)(2,1)S(1)} %pad_maximum_fusion.2), channel_id=1, replica_groups=mesh['z_hi'=4,'x'=4,'y'=8,'z_lo'=3,'core'=2] {'z_lo','core'}, dimensions={0} | all-to-all | bytes 663552 | tf_op jit(solution)/shard_map/all_to_all | solution.py:17
  113.0 0.1 convert_reduce_fusion.2
  113.3 0.1 reduce_sum.72
  113.5 0.8 multiply_subtract_fusion
  (50 shorter events, 1.4 us)
Async XLA Ops:
  1.6 16.2 %collective-permute-start.2 = (bf16[2,64,384]{2,1,0:T(8,128)(2,1)S(1)}, bf16[2,64,384]{2,1,0:T(8,128)(2,1)S(1)}, u32[]{:S(2)}, u32[]{:S(2)}) collective-permute-start(bf16[2,64,384]{2,1,0:T(8,128)(2,1)S(1)} %fusion.19), channel_id=1, source_target_pairs={{6,12},{12,6},{18,24},{24,18},{30,36},{36,30},{42,48},{48,42},{54,... | collective-permute-start | bytes 294920 | tf_op jit(solution)/shard_map/ppermute | solution.py:32
  2.3 15.6 %collective-permute-start.3 = (bf16[2,64,384]{2,1,0:T(8,128)(2,1)S(1)}, bf16[2,64,384]{2,1,0:T(8,128)(2,1)S(1)}, u32[]{:S(2)}, u32[]{:S(2)}) collective-permute-start(bf16[2,64,384]{2,1,0:T(8,128)(2,1)S(1)} %fusion.19), channel_id=1, source_target_pairs={{0,6},{6,0},{12,18},{18,12},{24,30},{30,24},{36,42},{42,36},{48,54... | collective-permute-start | bytes 294920 | tf_op jit(solution)/shard_map/ppermute | solution.py:33
  8.9 17.3 %collective-permute-start.1 = (bf16[2,384,384]{2,1,0:T(8,128)(2,1)}, bf16[2,384,384]{2,1,0:T(8,128)(2,1)S(1)}, u32[]{:S(2)}, u32[]{:S(2)}) collective-permute-start(bf16[2,384,384]{2,1,0:T(8,128)(2,1)} %param.9), channel_id=1, source_target_pairs={{0,1},{1,0},{2,3},{3,2},{4,5},{5,4},{6,7},{7,6},{8,9},{9,8},{10,11... | collective-permute-start | bytes 1769480 | tf_op jit(solution)/shard_map/ppermute | solution.py:96
  18.1 5.8 %copy-start.1 = (bf16[2,2,384,384]{3,2,1,0:T(8,128)(2,1)S(1)}, bf16[2,2,384,384]{3,2,1,0:T(8,128)(2,1)}, u32[]{:S(2)}) copy-start(bf16[2,2,384,384]{3,2,1,0:T(8,128)(2,1)} %param.8) | copy-start | bytes 3538948
  19.1 12.3 %all-to-all-start = ((bf16[6,64,384]{2,1,0:T(8,128)(2,1)}), bf16[6,64,384]{2,1,0:T(8,128)(2,1)S(1)}, u32[]{:S(2)}, u32[]{:S(2)}) async-start(bf16[6,64,384]{2,1,0:T(8,128)(2,1)} %fusion.12), calls=%async_computation | async-start | bytes 589824 | tf_op jit(solution)/shard_map/all_to_all | solution.py:17
  23.9 2.3 %copy-start.2 = (bf16[2,384,384]{2,1,0:T(8,128)(2,1)S(1)}, bf16[2,384,384]{2,1,0:T(8,128)(2,1)}, u32[]{:S(2)}) copy-start(bf16[2,384,384]{2,1,0:T(8,128)(2,1)} %param.9) | copy-start | bytes 1769476
  24.0 4.0 %collective-permute-start = (bf16[2,384,384]{2,1,0:T(8,128)(2,1)S(1)}, bf16[2,384,384]{2,1,0:T(8,128)(2,1)S(1)}, u32[]{:S(2)}, u32[]{:S(2)}) collective-permute-start(bf16[2,384,384]{2,1,0:T(8,128)(2,1)S(1)} %get-tuple-element.16), channel_id=1, source_target_pairs={{0,1},{1,0},{2,3},{3,2},{4,5},{5,4},{6,7},{7,6},{8,9},{9,8},{10,11... | collective-permute-start | bytes 1769480 | tf_op jit(solution)/shard_map/ppermute | solution.py:95
  31.4 12.1 %copy-start.3 = (bf16[2,64,384]{2,1,0:T(8,128)(2,1)S(1)}, bf16[2,64,384]{2,1,0:T(8,128)(2,1)}, u32[]{:S(2)}) copy-start(bf16[2,64,384]{2,1,0:T(8,128)(2,1)} %param.5) | copy-start | bytes 294916
  31.4 12.1 %copy-start.4 = (s32[2]{0:T(128)S(1)}, s32[2]{0:T(128)}, u32[]{:S(2)}) copy-start(s32[2]{0:T(128)} %param.6) | copy-start | bytes 28
  43.6 69.9 %copy-start = (f32[2,64,384]{2,1,0:T(8,128)}, f32[2,64,384]{2,1,0:T(8,128)S(1)}, u32[]{:S(2)}) copy-start(f32[2,64,384]{2,1,0:T(8,128)S(1)} %get-tuple-element.14) | copy-start | bytes 589828
  43.7 24.3 %collective-permute-start.4 = (bf16[2,64,384]{2,1,0:T(8,128)(2,1)S(1)}, bf16[2,64,384]{2,1,0:T(8,128)(2,1)S(1)}, u32[]{:S(2)}, u32[]{:S(2)}) collective-permute-start(bf16[2,64,384]{2,1,0:T(8,128)(2,1)S(1)} %convert_element_type.53), channel_id=1, source_target_pairs={{6,12},{12,6},{18,24},{24,18},{30,36},{36,30},{42,48},{48,42},{54,... | collective-permute-start | bytes 294920 | tf_op jit(solution)/shard_map/ppermute | solution.py:32
  44.3 23.7 %collective-permute-start.5 = (bf16[2,64,384]{2,1,0:T(8,128)(2,1)S(1)}, bf16[2,64,384]{2,1,0:T(8,128)(2,1)S(1)}, u32[]{:S(2)}, u32[]{:S(2)}) collective-permute-start(bf16[2,64,384]{2,1,0:T(8,128)(2,1)S(1)} %convert_element_type.53), channel_id=1, source_target_pairs={{0,6},{6,0},{12,18},{18,12},{24,30},{30,24},{36,42},{42,36},{48,54... | collective-permute-start | bytes 294920 | tf_op jit(solution)/shard_map/ppermute | solution.py:33
  48.6 30.4 %all-to-all-start.2 = ((f32[64,2,384]{2,1,0:T(2,128)}), f32[64,2,384]{2,1,0:T(2,128)S(1)}, u32[]{:S(2)}, u32[]{:S(2)}) async-start(f32[64,2,384]{2,1,0:T(2,128)} %broadcast_in_dim.14), calls=%async_computation.2 | async-start | bytes 393216 | tf_op jit(solution)/shard_map/all_to_all | solution.py:17
  79.0 16.3 %all-to-all-start.3 = ((bf16[6,64,384]{2,1,0:T(8,128)(2,1)}), bf16[6,64,384]{2,1,0:T(8,128)(2,1)S(1)}, u32[]{:S(2)}, u32[]{:S(2)}) async-start(bf16[6,64,384]{2,1,0:T(8,128)(2,1)} %fusion.7), calls=%async_computation.3 | async-start | bytes 589824 | tf_op jit(solution)/shard_map/all_to_all | solution.py:17
  82.6 12.6 %collective-permute-start.6 = (f32[2,384]{1,0:T(2,128)S(1)}, f32[2,384]{1,0:T(2,128)S(1)}, u32[]{:S(2)}, u32[]{:S(2)}) collective-permute-start(f32[2,384]{1,0:T(2,128)S(1)} %reduce_sum.68), channel_id=1, source_target_pairs={{0,192},{192,384},{384,576},{576,0},{1,385},{193,577},{385,1},{577... | collective-permute-start | bytes 9224 | tf_op jit(solution)/shard_map/ppermute | solution.py:68
  91.9 3.3 %collective-permute-start.7 = (f32[2,384]{1,0:T(2,128)S(1)}, f32[2,384]{1,0:T(2,128)S(1)}, u32[]{:S(2)}, u32[]{:S(2)}) collective-permute-start(f32[2,384]{1,0:T(2,128)S(1)} %reduce_sum.68), channel_id=1, source_target_pairs={{0,576},{192,0},{384,192},{576,384},{2,578},{194,2},{386,194},{578... | collective-permute-start | bytes 9224 | tf_op jit(solution)/shard_map/ppermute | solution.py:69

commit v6 on v5

--- a/solution.py
+++ b/solution.py
@@ -68,7 +68,7 @@
     first = lax.ppermute(values, ("z_hi", "core"), place[1] + place[2])
     last = lax.ppermute(values, ("z_hi", "core"), place[3])
     own = jnp.where(lax.axis_index("core") == 0, values, jnp.zeros_like(values))
-    return own + first + last
+    return own, first, last
 
 
 def in_thirds(values, shape):
@@ -99,11 +99,13 @@
     sigma = masked(reduced(parts, sectors, scale), dims)
     vector = psi_m.astype(F32)
     products = jnp.stack([jnp.sum(vector * sigma, axis=(0, 1)), jnp.sum(vector * vector, axis=(0, 1))])
-    sums = sum_by_exchange(products, NEAR)
+    sums = sum_by_exchange(jnp.sum(products.reshape(2, -1, LANES), axis=1), NEAR)
     outgoing = combine(sigma.astype(BF16), coeff)
     outgoing, sums = lax.optimization_barrier((outgoing, sums))
-    share = own_share(sums)
+    shares = own_share(sums)
     part = product(exchange(outgoing, COL), left, right)
+    part, shares = lax.optimization_barrier((part, shares))
+    share = jnp.pad(sum(shares), ((0, 0), (0, part.shape[2] - LANES)))
     sent = jnp.concatenate([part, in_thirds(share, part.shape)], axis=1)
     parts = exchange(sent, COL)
     rows = part.shape[1]

time: 115 us -> 113 us (0.983)
  waiting for transfers between devices: 17.3 us -> 14.6 us
    ppermute x1, waiting for transfers between devices: 2.58 us -> 1.03 us  [own_share(): first = lax.ppermute(values, ('z_hi', 'core'), place[1] + place[2])]
  transfers between devices with their start and end apart: 11 -> 11, of which waited for: 4 -> 4; matrix products, arithmetic and copies ran while one was open for 4% -> 5% of each run, Pallas kernels for 0% -> 0%
where the time goes in v6:
time: 113 us; the launch traced here: 112 us
  starting transfers between devices  59.3 us (52%)
  blocking collectives  26.8 us (24%)
  waiting for transfers between devices  14.6 us (13%)
  other arithmetic  5.56 us (5%)
  matrix products  2.94 us (3%)
  local copies, waits for them, and re-layouts  1.79 us (2%)
    all_to_all x3, starting transfers between devices, exchange(): return lax.all_to_all(blocks, axes, 0, 0, tiled=True)  28 us
    all_to_all x2, blocking collectives, exchange(): return lax.all_to_all(blocks, axes, 0, 0, tiled=True)  26.8 us
    all_to_all x3, waiting for transfers between devices, exchange(): return lax.all_to_all(blocks, axes, 0, 0, tiled=True)  11.8 us
    ppermute x2, starting transfers between devices, combine(): partner = lax.ppermute(vector, BLK, near)  10 us
    ppermute x1, starting transfers between devices, own_share(): first = lax.ppermute(values, ('z_hi', 'core'), place[1] + place[2])  9.3 us
    ppermute x1, starting transfers between devices, body(): lax.ppermute(right_env, 'core', swap)  7.78 us
    dot_general x2, matrix products, product(): part = jnp.einsum('wac,wdc->ad', temp, right, preferred_element_type=F32)  2.94 us
  transfers between devices with their start and end apart: 11, of which 4 were waited for; matrix products, arithmetic and copies ran while one was open for 5% of the time, Pallas kernels for 0%

profile of v6, /device:TPU:1, one launch (start us, length us, event | category | flops | bytes accessed | tf_op | source)
XLA Modules:
  0.0 111.8 jit_solution(16050883724425838658)
XLA Ops:
  0.7 1.0 fusion.19
  1.6 0.7 collective-permute-start.2
  2.3 6.6 %collective-permute-start.3 = (bf16[2,64,384]{2,1,0:T(8,128)(2,1)S(1)}, bf16[2,64,384]{2,1,0:T(8,128)(2,1)S(1)}, u32[]{:S(2)}, u32[]{:S(2)}) collective-permute-start(bf16[2,64,384]{2,1,0:T(8,128)(2,1)S(1)} %fusion.19), channel_id=1, source_target_pairs={{0,6},{6,0},{12,18},{18,12},{24,30},{30,24},{36,42},{42,36},{48,54... | collective-permute-start | bytes 294920 | tf_op jit(solution)/shard_map/ppermute | solution.py:33
  8.9 7.8 %collective-permute-start.1 = (bf16[2,384,384]{2,1,0:T(8,128)(2,1)}, bf16[2,384,384]{2,1,0:T(8,128)(2,1)S(1)}, u32[]{:S(2)}, u32[]{:S(2)}) collective-permute-start(bf16[2,384,384]{2,1,0:T(8,128)(2,1)} %param.9), channel_id=1, source_target_pairs={{0,1},{1,0},{2,3},{3,2},{4,5},{5,4},{6,7},{7,6},{8,9},{9,8},{10,11... | collective-permute-start | bytes 1769480 | tf_op jit(solution)/shard_map/ppermute | solution.py:96
  16.7 0.7 convert_element_type.50
  17.4 0.1 copy.15
  18.1 1.0 fusion.12
  19.1 4.8 %all-to-all-start = ((bf16[6,64,384]{2,1,0:T(8,128)(2,1)}), bf16[6,64,384]{2,1,0:T(8,128)(2,1)S(1)}, u32[]{:S(2)}, u32[]{:S(2)}) async-start(bf16[6,64,384]{2,1,0:T(8,128)(2,1)} %fusion.12), calls=%async_computation | async-start | bytes 589824 | tf_op jit(solution)/shard_map/all_to_all | solution.py:17
  23.9 0.1 dynamic-slice_bitcast_fusion.1
  24.0 2.1 %collective-permute-start = (bf16[2,384,384]{2,1,0:T(8,128)(2,1)S(1)}, bf16[2,384,384]{2,1,0:T(8,128)(2,1)S(1)}, u32[]{:S(2)}, u32[]{:S(2)}) collective-permute-start(bf16[2,384,384]{2,1,0:T(8,128)(2,1)S(1)} %get-tuple-element.22), channel_id=1, source_target_pairs={{0,1},{1,0},{2,3},{3,2},{4,5},{5,4},{6,7},{7,6},{8,9},{9,8},{10,11... | collective-permute-start | bytes 1769480 | tf_op jit(solution)/shard_map/ppermute | solution.py:95
  26.2 0.1 pad_maximum_fusion.1
  26.3 1.7 %collective-permute-done = bf16[2,384,384]{2,1,0:T(8,128)(2,1)S(1)} collective-permute-done((bf16[2,384,384]{2,1,0:T(8,128)(2,1)S(1)}, bf16[2,384,384]{2,1,0:T(8,128)(2,1)S(1)}, u32[]{:S(2)}, u32[]{:S(2)}) %collective-permute-start) | collective-permute-done | bytes 589856 | tf_op jit(solution)/shard_map/ppermute | solution.py:95
  28.0 0.1 pad_maximum_fusion
  28.2 3.2 %all-to-all-done = bf16[6,64,384]{2,1,0:T(8,128)(2,1)S(1)} async-done(((bf16[6,64,384]{2,1,0:T(8,128)(2,1)}), bf16[6,64,384]{2,1,0:T(8,128)(2,1)S(1)}, u32[]{:S(2)}, u32[]{:S(2)}) %all-to-all-start) | async-done | bytes 294944 | tf_op jit(solution)/shard_map/all_to_all | solution.py:17
  31.4 1.5 %fusion.4 = bf16[384,384]{1,0:T(8,128)(2,1)S(1)} fusion(bf16[4,384,384]{2,1,0:T(8,128)(2,1)S(1)} %pad_maximum_fusion.1, bf16[4,384,384]{2,1,0:T(8,128)(2,1)S(1)} %pad_maximum_fusion, bf16[384,384,1]{1,0,2:T(8,128)(2,1)S(1)} %bitcast.105), kind=kOutput, calls=%fused_computation.6 | convolution fusion | flops 906706944 | bytes 2949120 | tf_op jit(solution)/shard_map/wac,wdc->ad/dot_general | solution.py:48
  32.8 10.6 %all_to_all.25 = bf16[6,64,384]{2,1,0:T(8,128)(2,1)S(1)} all-to-all(bf16[6,64,384]{2,1,0:T(8,128)(2,1)S(1)} %bitcast.107), channel_id=1, replica_groups=mesh['z_hi'=4,'x'=4,'y'=8,'z_lo'=3,'core'=2] {'z_lo','core'}, dimensions={0} | all-to-all | bytes 589824 | tf_op jit(solution)/shard_map/all_to_all | solution.py:17
  43.5 0.1 fusion.16
  43.7 0.7 collective-permute-start.4
  44.3 3.5 %collective-permute-start.5 = (bf16[2,64,384]{2,1,0:T(8,128)(2,1)S(1)}, bf16[2,64,384]{2,1,0:T(8,128)(2,1)S(1)}, u32[]{:S(2)}, u32[]{:S(2)}) collective-permute-start(bf16[2,64,384]{2,1,0:T(8,128)(2,1)S(1)} %convert_element_type.55), channel_id=1, source_target_pairs={{0,6},{6,0},{12,18},{18,12},{24,30},{30,24},{36,42},{42,36},{48,54... | collective-permute-start | bytes 294920 | tf_op jit(solution)/shard_map/ppermute | solution.py:33
  47.9 0.7 broadcast_in_dim.14
  48.5 19.4 %all-to-all-start.2 = ((f32[64,2,128]{2,1,0:T(2,128)}), f32[64,2,128]{2,1,0:T(2,128)S(1)}, u32[]{:S(2)}, u32[]{:S(2)}) async-start(f32[64,2,128]{2,1,0:T(2,128)} %broadcast_in_dim.14), calls=%async_computation.2 | async-start | bytes 131072 | tf_op jit(solution)/shard_map/all_to_all | solution.py:17
  68.1 1.0 fusion.7
  69.1 8.6 %all-to-all-done.2 = f32[64,2,128]{2,1,0:T(2,128)S(1)} async-done(((f32[64,2,128]{2,1,0:T(2,128)}), f32[64,2,128]{2,1,0:T(2,128)S(1)}, u32[]{:S(2)}, u32[]{:S(2)}) %all-to-all-start.2) | async-done | bytes 65568 | tf_op jit(solution)/shard_map/all_to_all | solution.py:17
  77.8 3.8 %all-to-all-start.3 = ((bf16[6,64,384]{2,1,0:T(8,128)(2,1)}), bf16[6,64,384]{2,1,0:T(8,128)(2,1)S(1)}, u32[]{:S(2)}, u32[]{:S(2)}) async-start(bf16[6,64,384]{2,1,0:T(8,128)(2,1)} %fusion.7), calls=%async_computation.3 | async-start | bytes 589824 | tf_op jit(solution)/shard_map/all_to_all | solution.py:17
  81.6 9.3 %collective-permute-start.6 = (f32[2,128]{1,0:T(2,128)S(1)}, f32[2,128]{1,0:T(2,128)S(1)}, u32[]{:S(2)}, u32[]{:S(2)}) collective-permute-start(f32[2,128]{1,0:T(2,128)S(1)} %reduce_sum.78), channel_id=1, source_target_pairs={{0,192},{192,384},{384,576},{576,0},{1,385},{193,577},{385,1},{577... | collective-permute-start | bytes 3080 | tf_op jit(solution)/shard_map/ppermute | solution.py:68
  91.0 0.7 collective-permute-start.7
  91.6 1.5 %fusion.5 = bf16[384,384]{1,0:T(8,128)(2,1)S(1)} fusion(bf16[4,384,384]{2,1,0:T(8,128)(2,1)S(1)} %pad_maximum_fusion.1, bf16[4,384,384]{2,1,0:T(8,128)(2,1)S(1)} %pad_maximum_fusion, bf16[384,384,1]{1,0,2:T(8,128)(2,1)S(1)} %bitcast.106), kind=kOutput, calls=%fused_computation.7 | convolution fusion | flops 906706944 | bytes 2949120 | tf_op jit(solution)/shard_map/wac,wdc->ad/dot_general | solution.py:48
  93.1 1.0 collective-permute-done.6
  94.3 16.2 %all_to_all.26 = bf16[6,72,384]{2,1,0:T(8,128)(2,1)S(1)} all-to-all(bf16[6,72,384]{2,1,0:T(8,128)(2,1)S(1)} %pad_maximum_fusion.2), channel_id=1, replica_groups=mesh['z_hi'=4,'x'=4,'y'=8,'z_lo'=3,'core'=2] {'z_lo','core'}, dimensions={0} | all-to-all | bytes 663552 | tf_op jit(solution)/shard_map/all_to_all | solution.py:17
  110.6 0.1 convert_reduce_fusion.2
  110.8 0.1 reduce_sum.82
  111.1 0.8 multiply_subtract_fusion
  (51 shorter events, 1.5 us)
Async XLA Ops:
  1.6 16.2 %collective-permute-start.2 = (bf16[2,64,384]{2,1,0:T(8,128)(2,1)S(1)}, bf16[2,64,384]{2,1,0:T(8,128)(2,1)S(1)}, u32[]{:S(2)}, u32[]{:S(2)}) collective-permute-start(bf16[2,64,384]{2,1,0:T(8,128)(2,1)S(1)} %fusion.19), channel_id=1, source_target_pairs={{6,12},{12,6},{18,24},{24,18},{30,36},{36,30},{42,48},{48,42},{54,... | collective-permute-start | bytes 294920 | tf_op jit(solution)/shard_map/ppermute | solution.py:32
  2.3 15.6 %collective-permute-start.3 = (bf16[2,64,384]{2,1,0:T(8,128)(2,1)S(1)}, bf16[2,64,384]{2,1,0:T(8,128)(2,1)S(1)}, u32[]{:S(2)}, u32[]{:S(2)}) collective-permute-start(bf16[2,64,384]{2,1,0:T(8,128)(2,1)S(1)} %fusion.19), channel_id=1, source_target_pairs={{0,6},{6,0},{12,18},{18,12},{24,30},{30,24},{36,42},{42,36},{48,54... | collective-permute-start | bytes 294920 | tf_op jit(solution)/shard_map/ppermute | solution.py:33
  8.9 17.2 %collective-permute-start.1 = (bf16[2,384,384]{2,1,0:T(8,128)(2,1)}, bf16[2,384,384]{2,1,0:T(8,128)(2,1)S(1)}, u32[]{:S(2)}, u32[]{:S(2)}) collective-permute-start(bf16[2,384,384]{2,1,0:T(8,128)(2,1)} %param.9), channel_id=1, source_target_pairs={{0,1},{1,0},{2,3},{3,2},{4,5},{5,4},{6,7},{7,6},{8,9},{9,8},{10,11... | collective-permute-start | bytes 1769480 | tf_op jit(solution)/shard_map/ppermute | solution.py:96
  18.1 5.8 %copy-start.1 = (bf16[2,2,384,384]{3,2,1,0:T(8,128)(2,1)S(1)}, bf16[2,2,384,384]{3,2,1,0:T(8,128)(2,1)}, u32[]{:S(2)}) copy-start(bf16[2,2,384,384]{3,2,1,0:T(8,128)(2,1)} %param.8) | copy-start | bytes 3538948
  19.1 12.3 %all-to-all-start = ((bf16[6,64,384]{2,1,0:T(8,128)(2,1)}), bf16[6,64,384]{2,1,0:T(8,128)(2,1)S(1)}, u32[]{:S(2)}, u32[]{:S(2)}) async-start(bf16[6,64,384]{2,1,0:T(8,128)(2,1)} %fusion.12), calls=%async_computation | async-start | bytes 589824 | tf_op jit(solution)/shard_map/all_to_all | solution.py:17
  23.9 2.3 %copy-start.2 = (bf16[2,384,384]{2,1,0:T(8,128)(2,1)S(1)}, bf16[2,384,384]{2,1,0:T(8,128)(2,1)}, u32[]{:S(2)}) copy-start(bf16[2,384,384]{2,1,0:T(8,128)(2,1)} %param.9) | copy-start | bytes 1769476
  24.0 4.0 %collective-permute-start = (bf16[2,384,384]{2,1,0:T(8,128)(2,1)S(1)}, bf16[2,384,384]{2,1,0:T(8,128)(2,1)S(1)}, u32[]{:S(2)}, u32[]{:S(2)}) collective-permute-start(bf16[2,384,384]{2,1,0:T(8,128)(2,1)S(1)} %get-tuple-element.22), channel_id=1, source_target_pairs={{0,1},{1,0},{2,3},{3,2},{4,5},{5,4},{6,7},{7,6},{8,9},{9,8},{10,11... | collective-permute-start | bytes 1769480 | tf_op jit(solution)/shard_map/ppermute | solution.py:95
  31.4 12.1 %copy-start.3 = (bf16[2,64,384]{2,1,0:T(8,128)(2,1)S(1)}, bf16[2,64,384]{2,1,0:T(8,128)(2,1)}, u32[]{:S(2)}) copy-start(bf16[2,64,384]{2,1,0:T(8,128)(2,1)} %param.5) | copy-start | bytes 294916
  31.4 12.1 %copy-start.4 = (s32[2]{0:T(128)S(1)}, s32[2]{0:T(128)}, u32[]{:S(2)}) copy-start(s32[2]{0:T(128)} %param.6) | copy-start | bytes 28
  43.6 67.4 %copy-start = (f32[2,64,384]{2,1,0:T(8,128)}, f32[2,64,384]{2,1,0:T(8,128)S(1)}, u32[]{:S(2)}) copy-start(f32[2,64,384]{2,1,0:T(8,128)S(1)} %get-tuple-element.20) | copy-start | bytes 589828
  43.7 24.3 %collective-permute-start.4 = (bf16[2,64,384]{2,1,0:T(8,128)(2,1)S(1)}, bf16[2,64,384]{2,1,0:T(8,128)(2,1)S(1)}, u32[]{:S(2)}, u32[]{:S(2)}) collective-permute-start(bf16[2,64,384]{2,1,0:T(8,128)(2,1)S(1)} %convert_element_type.55), channel_id=1, source_target_pairs={{6,12},{12,6},{18,24},{24,18},{30,36},{36,30},{42,48},{48,42},{54,... | collective-permute-start | bytes 294920 | tf_op jit(solution)/shard_map/ppermute | solution.py:32
  44.3 23.6 %collective-permute-start.5 = (bf16[2,64,384]{2,1,0:T(8,128)(2,1)S(1)}, bf16[2,64,384]{2,1,0:T(8,128)(2,1)S(1)}, u32[]{:S(2)}, u32[]{:S(2)}) collective-permute-start(bf16[2,64,384]{2,1,0:T(8,128)(2,1)S(1)} %convert_element_type.55), channel_id=1, source_target_pairs={{0,6},{6,0},{12,18},{18,12},{24,30},{30,24},{36,42},{42,36},{48,54... | collective-permute-start | bytes 294920 | tf_op jit(solution)/shard_map/ppermute | solution.py:33
  48.5 29.2 %all-to-all-start.2 = ((f32[64,2,128]{2,1,0:T(2,128)}), f32[64,2,128]{2,1,0:T(2,128)S(1)}, u32[]{:S(2)}, u32[]{:S(2)}) async-start(f32[64,2,128]{2,1,0:T(2,128)} %broadcast_in_dim.14), calls=%async_computation.2 | async-start | bytes 131072 | tf_op jit(solution)/shard_map/all_to_all | solution.py:17
  77.8 13.8 %all-to-all-start.3 = ((bf16[6,64,384]{2,1,0:T(8,128)(2,1)}), bf16[6,64,384]{2,1,0:T(8,128)(2,1)S(1)}, u32[]{:S(2)}, u32[]{:S(2)}) async-start(bf16[6,64,384]{2,1,0:T(8,128)(2,1)} %fusion.7), calls=%async_computation.3 | async-start | bytes 589824 | tf_op jit(solution)/shard_map/all_to_all | solution.py:17
  81.6 12.5 %collective-permute-start.6 = (f32[2,128]{1,0:T(2,128)S(1)}, f32[2,128]{1,0:T(2,128)S(1)}, u32[]{:S(2)}, u32[]{:S(2)}) collective-permute-start(f32[2,128]{1,0:T(2,128)S(1)} %reduce_sum.78), channel_id=1, source_target_pairs={{0,192},{192,384},{384,576},{576,0},{1,385},{193,577},{385,1},{577... | collective-permute-start | bytes 3080 | tf_op jit(solution)/shard_map/ppermute | solution.py:68
  91.0 3.2 %collective-permute-start.7 = (f32[2,128]{1,0:T(2,128)S(1)}, f32[2,128]{1,0:T(2,128)S(1)}, u32[]{:S(2)}, u32[]{:S(2)}) collective-permute-start(f32[2,128]{1,0:T(2,128)S(1)} %reduce_sum.78), channel_id=1, source_target_pairs={{0,576},{192,0},{384,192},{576,384},{2,578},{194,2},{386,194},{578... | collective-permute-start | bytes 3080 | tf_op jit(solution)/shard_map/ppermute | solution.py:69

commit v7 on v6

--- a/solution.py
+++ b/solution.py
@@ -1,6 +1,8 @@
 import jax
 import jax.numpy as jnp
 from jax import lax
+from jax.experimental import pallas as pl
+from jax.experimental.pallas import tpu as pltpu
 from jax.sharding import Mesh, PartitionSpec as P
 
 CORES = 2
@@ -10,6 +12,7 @@
 COL = ("z_lo", "core")
 NEAR = ("x", "y", "core")
 F32 = jnp.float32
+COST = 30_000_000_000
 BF16 = jnp.bfloat16
 
 
@@ -25,14 +28,17 @@
     return jnp.where((row < dims) & (column < dims), value, jnp.zeros_like(value))
 
 
-def combine(vector, coeff):
+def neighbours(vector):
     count = lax.axis_size(BLK)
     near = [(i, i ^ 1) for i in range(count)]
     across = [(i, i + 1 if i % 2 else i - 1) for i in range(1, count - 1)]
     other = lax.ppermute(vector, BLK, across)
     partner = lax.ppermute(vector, BLK, near)
     even = lax.rem(lax.axis_index(BLK), 2) == 0
-    low, high = jnp.where(even, other, partner), jnp.where(even, partner, other)
+    return jnp.where(even, other, partner), jnp.where(even, partner, other)
+
+
+def combine(low, vector, high, coeff):
     padded = jnp.concatenate([low, vector, high], axis=0).astype(F32)
     sectors, rows, width = vector.shape
     total = jnp.zeros(coeff.shape[:2] + (rows, width), F32)
@@ -55,9 +61,17 @@
     return jnp.sum(parts, axis=0) * scale
 
 
-def sum_by_exchange(values, axes):
-    copies = jnp.broadcast_to(values[None], (lax.axis_size(axes),) + values.shape)
-    return jnp.sum(exchange(copies, axes), axis=0)
+def add_up(received):
+    def kernel(received, total):
+        total[...] = jnp.sum(received[...], axis=0)
+
+    return pl.pallas_call(
+        kernel,
+        out_shape=jax.ShapeDtypeStruct(received.shape[1:], F32),
+        in_specs=[pl.BlockSpec(memory_space=pltpu.VMEM)],
+        out_specs=pl.BlockSpec(memory_space=pltpu.VMEM),
+        cost_estimate=pl.CostEstimate(flops=COST, bytes_accessed=0, transcendentals=0),
+    )(received)
 
 
 def own_share(values):
@@ -89,7 +103,8 @@
     coeff = lax.optimization_barrier(coeff)
 
     psi_m = masked(psi, dims)
-    outgoing = combine(psi_m, coeff)
+    low, high = neighbours(psi_m)
+    outgoing = combine(low, psi_m, high, coeff)
     left_mine = lax.dynamic_index_in_dim(left_env, core, 0, keepdims=False)
     left_sent = lax.dynamic_index_in_dim(left_env, 1 - core, 0, keepdims=False)
     left = jnp.concatenate([left_mine, lax.ppermute(left_sent, "core", swap)], axis=0)
@@ -99,9 +114,13 @@
     sigma = masked(reduced(parts, sectors, scale), dims)
     vector = psi_m.astype(F32)
     products = jnp.stack([jnp.sum(vector * sigma, axis=(0, 1)), jnp.sum(vector * vector, axis=(0, 1))])
-    sums = sum_by_exchange(jnp.sum(products.reshape(2, -1, LANES), axis=1), NEAR)
-    outgoing = combine(sigma.astype(BF16), coeff)
-    outgoing, sums = lax.optimization_barrier((outgoing, sums))
+    products = jnp.sum(products.reshape(2, -1, LANES), axis=1)
+    copies = jnp.broadcast_to(products[None], (lax.axis_size(NEAR),) + products.shape)
+    sums = add_up(exchange(copies, NEAR))
+    rounded = sigma.astype(BF16)
+    low, high = neighbours(rounded)
+    low, high, sums = lax.optimization_barrier((low, high, sums))
+    outgoing = combine(low, rounded, high, coeff)
     shares = own_share(sums)
     part = product(exchange(outgoing, COL), left, right)
     part, shares = lax.optimization_barrier((part, shares))

time: 113 us -> 116 us (1.027)
  Pallas kernels: 0 us -> 1.48 us
    pallas_call x0 -> x1, Pallas kernels: none -> 1.48 us  [add_up(): pl.pallas_call(kernel, out_shape=jax.ShapeDtypeStruct(received.shape[1:],...]
  transfers between devices with their start and end apart: 11 -> 11, of which waited for: 4 -> 4; matrix products, arithmetic and copies ran while one was open for 5% -> 4% of each run, Pallas kernels for 0% -> 0%
where the time goes in v7:
time: 116 us; the launch traced here: 115 us
  starting transfers between devices  59.3 us (51%)
  blocking collectives  26.8 us (23%)
  waiting for transfers between devices  15.7 us (14%)
  other arithmetic  5.48 us (5%)
  matrix products  2.94 us (3%)
  local copies, waits for them, and re-layouts  2.42 us (2%)
  Pallas kernels  1.48 us (1%)
    all_to_all x3, starting transfers between devices, exchange(): return lax.all_to_all(blocks, axes, 0, 0, tiled=True)  28 us
    all_to_all x2, blocking collectives, exchange(): return lax.all_to_all(blocks, axes, 0, 0, tiled=True)  26.8 us
    all_to_all x3, waiting for transfers between devices, exchange(): return lax.all_to_all(blocks, axes, 0, 0, tiled=True)  12.9 us
    ppermute x2, starting transfers between devices, neighbours(): partner = lax.ppermute(vector, BLK, near)  10 us
    ppermute x1, starting transfers between devices, own_share(): first = lax.ppermute(values, ('z_hi', 'core'), place[1] + place[2])  9.31 us
    ppermute x1, starting transfers between devices, body(): lax.ppermute(right_env, 'core', swap)  7.78 us
    dot_general x2, matrix products, product(): part = jnp.einsum('wac,wdc->ad', temp, right, preferred_element_type=F32)  2.94 us
  transfers between devices with their start and end apart: 11, of which 4 were waited for; matrix products, arithmetic and copies ran while one was open for 4% of the time, Pallas kernels for 0%

profile of v7, /device:TPU:1, one launch (start us, length us, event | category | flops | bytes accessed | tf_op | source)
XLA Modules:
  0.0 115.0 jit_solution(10921859712016046176)
XLA Ops:
  0.7 1.0 fusion.19
  1.6 0.7 collective-permute-start.2
  2.3 6.6 %collective-permute-start.3 = (bf16[2,64,384]{2,1,0:T(8,128)(2,1)S(1)}, bf16[2,64,384]{2,1,0:T(8,128)(2,1)S(1)}, u32[]{:S(2)}, u32[]{:S(2)}) collective-permute-start(bf16[2,64,384]{2,1,0:T(8,128)(2,1)S(1)} %fusion.19), channel_id=1, source_target_pairs={{0,6},{6,0},{12,18},{18,12},{24,30},{30,24},{36,42},{42,36},{48,54... | collective-permute-start | bytes 294920 | tf_op jit(solution)/shard_map/ppermute | solution.py:36
  8.9 7.8 %collective-permute-start.1 = (bf16[2,384,384]{2,1,0:T(8,128)(2,1)}, bf16[2,384,384]{2,1,0:T(8,128)(2,1)S(1)}, u32[]{:S(2)}, u32[]{:S(2)}) collective-permute-start(bf16[2,384,384]{2,1,0:T(8,128)(2,1)} %param.9), channel_id=1, source_target_pairs={{0,1},{1,0},{2,3},{3,2},{4,5},{5,4},{6,7},{7,6},{8,9},{9,8},{10,11... | collective-permute-start | bytes 1769480 | tf_op jit(solution)/shard_map/ppermute | solution.py:111
  16.7 0.7 convert_element_type.50
  18.1 1.0 fusion.12
  19.1 4.8 %all-to-all-start = ((bf16[6,64,384]{2,1,0:T(8,128)(2,1)}), bf16[6,64,384]{2,1,0:T(8,128)(2,1)S(1)}, u32[]{:S(2)}, u32[]{:S(2)}) async-start(bf16[6,64,384]{2,1,0:T(8,128)(2,1)} %fusion.12), calls=%async_computation | async-start | bytes 589824 | tf_op jit(solution)/shard_map/all_to_all | solution.py:20
  24.0 2.1 %collective-permute-start = (bf16[2,384,384]{2,1,0:T(8,128)(2,1)S(1)}, bf16[2,384,384]{2,1,0:T(8,128)(2,1)S(1)}, u32[]{:S(2)}, u32[]{:S(2)}) collective-permute-start(bf16[2,384,384]{2,1,0:T(8,128)(2,1)S(1)} %get-tuple-element.24), channel_id=1, source_target_pairs={{0,1},{1,0},{2,3},{3,2},{4,5},{5,4},{6,7},{7,6},{8,9},{9,8},{10,11... | collective-permute-start | bytes 1769480 | tf_op jit(solution)/shard_map/ppermute | solution.py:110
  26.2 0.1 pad_maximum_fusion.1
  26.3 1.7 %collective-permute-done = bf16[2,384,384]{2,1,0:T(8,128)(2,1)S(1)} collective-permute-done((bf16[2,384,384]{2,1,0:T(8,128)(2,1)S(1)}, bf16[2,384,384]{2,1,0:T(8,128)(2,1)S(1)}, u32[]{:S(2)}, u32[]{:S(2)}) %collective-permute-start) | collective-permute-done | bytes 589856 | tf_op jit(solution)/shard_map/ppermute | solution.py:110
  28.0 0.1 pad_maximum_fusion
  28.2 3.2 %all-to-all-done = bf16[6,64,384]{2,1,0:T(8,128)(2,1)S(1)} async-done(((bf16[6,64,384]{2,1,0:T(8,128)(2,1)}), bf16[6,64,384]{2,1,0:T(8,128)(2,1)S(1)}, u32[]{:S(2)}, u32[]{:S(2)}) %all-to-all-start) | async-done | bytes 294944 | tf_op jit(solution)/shard_map/all_to_all | solution.py:20
  31.4 1.5 %fusion.4 = bf16[384,384]{1,0:T(8,128)(2,1)S(1)} fusion(bf16[4,384,384]{2,1,0:T(8,128)(2,1)S(1)} %pad_maximum_fusion.1, bf16[4,384,384]{2,1,0:T(8,128)(2,1)S(1)} %pad_maximum_fusion, bf16[384,384,1]{1,0,2:T(8,128)(2,1)S(1)} %bitcast.105), kind=kOutput, calls=%fused_computation.6 | convolution fusion | flops 906706944 | bytes 2949120 | tf_op jit(solution)/shard_map/wac,wdc->ad/dot_general | solution.py:54
  32.8 10.6 %all_to_all.25 = bf16[6,64,384]{2,1,0:T(8,128)(2,1)S(1)} all-to-all(bf16[6,64,384]{2,1,0:T(8,128)(2,1)S(1)} %bitcast.107), channel_id=1, replica_groups=mesh['z_hi'=4,'x'=4,'y'=8,'z_lo'=3,'core'=2] {'z_lo','core'}, dimensions={0} | all-to-all | bytes 589824 | tf_op jit(solution)/shard_map/all_to_all | solution.py:20
  43.5 0.1 fusion.16
  43.7 0.7 collective-permute-start.4
  44.3 3.5 %collective-permute-start.5 = (bf16[2,64,384]{2,1,0:T(8,128)(2,1)S(1)}, bf16[2,64,384]{2,1,0:T(8,128)(2,1)S(1)}, u32[]{:S(2)}, u32[]{:S(2)}) collective-permute-start(bf16[2,64,384]{2,1,0:T(8,128)(2,1)S(1)} %convert_element_type.55), channel_id=1, source_target_pairs={{0,6},{6,0},{12,18},{18,12},{24,30},{30,24},{36,42},{42,36},{48,54... | collective-permute-start | bytes 294920 | tf_op jit(solution)/shard_map/ppermute | solution.py:36
  47.9 0.7 broadcast_in_dim.14
  48.5 19.4 %all-to-all-start.2 = ((f32[64,2,128]{2,1,0:T(2,128)}), f32[64,2,128]{2,1,0:T(2,128)S(1)}, u32[]{:S(2)}, u32[]{:S(2)}) async-start(f32[64,2,128]{2,1,0:T(2,128)} %broadcast_in_dim.14), calls=%async_computation.2 | async-start | bytes 131072 | tf_op jit(solution)/shard_map/all_to_all | solution.py:20
  68.0 9.7 %all-to-all-done.2.received = f32[64,2,128]{2,1,0:T(2,128)S(1)} async-done(((f32[64,2,128]{2,1,0:T(2,128)}), f32[64,2,128]{2,1,0:T(2,128)S(1)}, u32[]{:S(2)}, u32[]{:S(2)}) %all-to-all-start.2) | async-done | bytes 65568 | tf_op jit(solution)/shard_map/all_to_all | solution.py:20
  77.7 0.6 copy-done.4
  78.4 1.5 %shard_map.68 = f32[2,128]{1,0:T(2,128)} custom-call(f32[64,2,128]{2,1,0:T(2,128)} %copy-done.4), custom_call_target="tpu_custom_call" | custom-call | flops 30000001024 | tf_op jit(solution)/shard_map/pallas_call | solution.py:68
  80.0 1.0 fusion.7
  81.0 3.8 %all-to-all-start.3 = ((bf16[6,64,384]{2,1,0:T(8,128)(2,1)}), bf16[6,64,384]{2,1,0:T(8,128)(2,1)S(1)}, u32[]{:S(2)}, u32[]{:S(2)}) async-start(bf16[6,64,384]{2,1,0:T(8,128)(2,1)} %fusion.7), calls=%async_computation.3 | async-start | bytes 589824 | tf_op jit(solution)/shard_map/all_to_all | solution.py:20
  84.8 9.3 %collective-permute-start.6 = (f32[2,128]{1,0:T(2,128)S(1)}, f32[2,128]{1,0:T(2,128)S(1)}, u32[]{:S(2)}, u32[]{:S(2)}) collective-permute-start(f32[2,128]{1,0:T(2,128)S(1)} %copy-done.6), channel_id=1, source_target_pairs={{0,192},{192,384},{384,576},{576,0},{1,385},{193,577},{385,1},{577... | collective-permute-start | bytes 3080 | tf_op jit(solution)/shard_map/ppermute | solution.py:82
  94.1 0.7 collective-permute-start.7
  94.8 1.5 %fusion.5 = bf16[384,384]{1,0:T(8,128)(2,1)S(1)} fusion(bf16[4,384,384]{2,1,0:T(8,128)(2,1)S(1)} %pad_maximum_fusion.1, bf16[4,384,384]{2,1,0:T(8,128)(2,1)S(1)} %pad_maximum_fusion, bf16[384,384,1]{1,0,2:T(8,128)(2,1)S(1)} %bitcast.106), kind=kOutput, calls=%fused_computation.7 | convolution fusion | flops 906706944 | bytes 2949120 | tf_op jit(solution)/shard_map/wac,wdc->ad/dot_general | solution.py:54
  96.3 1.0 collective-permute-done.6
  97.5 16.2 %all_to_all.26 = bf16[6,72,384]{2,1,0:T(8,128)(2,1)S(1)} all-to-all(bf16[6,72,384]{2,1,0:T(8,128)(2,1)S(1)} %pad_maximum_fusion.2), channel_id=1, replica_groups=mesh['z_hi'=4,'x'=4,'y'=8,'z_lo'=3,'core'=2] {'z_lo','core'}, dimensions={0} | all-to-all | bytes 663552 | tf_op jit(solution)/shard_map/all_to_all | solution.py:20
  113.8 0.1 convert_reduce_fusion.2
  114.0 0.1 reduce_sum.72
  114.2 0.8 multiply_subtract_fusion
  (55 shorter events, 1.6 us)
Async XLA Ops:
  1.6 16.2 %collective-permute-start.2 = (bf16[2,64,384]{2,1,0:T(8,128)(2,1)S(1)}, bf16[2,64,384]{2,1,0:T(8,128)(2,1)S(1)}, u32[]{:S(2)}, u32[]{:S(2)}) collective-permute-start(bf16[2,64,384]{2,1,0:T(8,128)(2,1)S(1)} %fusion.19), channel_id=1, source_target_pairs={{6,12},{12,6},{18,24},{24,18},{30,36},{36,30},{42,48},{48,42},{54,... | collective-permute-start | bytes 294920 | tf_op jit(solution)/shard_map/ppermute | solution.py:35
  2.3 15.6 %collective-permute-start.3 = (bf16[2,64,384]{2,1,0:T(8,128)(2,1)S(1)}, bf16[2,64,384]{2,1,0:T(8,128)(2,1)S(1)}, u32[]{:S(2)}, u32[]{:S(2)}) collective-permute-start(bf16[2,64,384]{2,1,0:T(8,128)(2,1)S(1)} %fusion.19), channel_id=1, source_target_pairs={{0,6},{6,0},{12,18},{18,12},{24,30},{30,24},{36,42},{42,36},{48,54... | collective-permute-start | bytes 294920 | tf_op jit(solution)/shard_map/ppermute | solution.py:36
  8.9 17.3 %collective-permute-start.1 = (bf16[2,384,384]{2,1,0:T(8,128)(2,1)}, bf16[2,384,384]{2,1,0:T(8,128)(2,1)S(1)}, u32[]{:S(2)}, u32[]{:S(2)}) collective-permute-start(bf16[2,384,384]{2,1,0:T(8,128)(2,1)} %param.9), channel_id=1, source_target_pairs={{0,1},{1,0},{2,3},{3,2},{4,5},{5,4},{6,7},{7,6},{8,9},{9,8},{10,11... | collective-permute-start | bytes 1769480 | tf_op jit(solution)/shard_map/ppermute | solution.py:111
  18.1 5.8 %copy-start.1 = (bf16[2,2,384,384]{3,2,1,0:T(8,128)(2,1)S(1)}, bf16[2,2,384,384]{3,2,1,0:T(8,128)(2,1)}, u32[]{:S(2)}) copy-start(bf16[2,2,384,384]{3,2,1,0:T(8,128)(2,1)} %param.8) | copy-start | bytes 3538948
  19.1 12.3 %all-to-all-start = ((bf16[6,64,384]{2,1,0:T(8,128)(2,1)}), bf16[6,64,384]{2,1,0:T(8,128)(2,1)S(1)}, u32[]{:S(2)}, u32[]{:S(2)}) async-start(bf16[6,64,384]{2,1,0:T(8,128)(2,1)} %fusion.12), calls=%async_computation | async-start | bytes 589824 | tf_op jit(solution)/shard_map/all_to_all | solution.py:20
  23.9 2.3 %copy-start.2 = (bf16[2,384,384]{2,1,0:T(8,128)(2,1)S(1)}, bf16[2,384,384]{2,1,0:T(8,128)(2,1)}, u32[]{:S(2)}) copy-start(bf16[2,384,384]{2,1,0:T(8,128)(2,1)} %param.9) | copy-start | bytes 1769476
  24.0 4.0 %collective-permute-start = (bf16[2,384,384]{2,1,0:T(8,128)(2,1)S(1)}, bf16[2,384,384]{2,1,0:T(8,128)(2,1)S(1)}, u32[]{:S(2)}, u32[]{:S(2)}) collective-permute-start(bf16[2,384,384]{2,1,0:T(8,128)(2,1)S(1)} %get-tuple-element.24), channel_id=1, source_target_pairs={{0,1},{1,0},{2,3},{3,2},{4,5},{5,4},{6,7},{7,6},{8,9},{9,8},{10,11... | collective-permute-start | bytes 1769480 | tf_op jit(solution)/shard_map/ppermute | solution.py:110
  31.4 12.1 %copy-start.3 = (bf16[2,64,384]{2,1,0:T(8,128)(2,1)S(1)}, bf16[2,64,384]{2,1,0:T(8,128)(2,1)}, u32[]{:S(2)}) copy-start(bf16[2,64,384]{2,1,0:T(8,128)(2,1)} %param.5) | copy-start | bytes 294916
  31.4 12.1 %copy-start.5 = (s32[2]{0:T(128)S(1)}, s32[2]{0:T(128)}, u32[]{:S(2)}) copy-start(s32[2]{0:T(128)} %param.6) | copy-start | bytes 28
  43.6 70.6 %copy-start = (f32[2,64,384]{2,1,0:T(8,128)}, f32[2,64,384]{2,1,0:T(8,128)S(1)}, u32[]{:S(2)}) copy-start(f32[2,64,384]{2,1,0:T(8,128)S(1)} %get-tuple-element.22) | copy-start | bytes 589828
  43.7 24.3 %collective-permute-start.4 = (bf16[2,64,384]{2,1,0:T(8,128)(2,1)S(1)}, bf16[2,64,384]{2,1,0:T(8,128)(2,1)S(1)}, u32[]{:S(2)}, u32[]{:S(2)}) collective-permute-start(bf16[2,64,384]{2,1,0:T(8,128)(2,1)S(1)} %convert_element_type.55), channel_id=1, source_target_pairs={{6,12},{12,6},{18,24},{24,18},{30,36},{36,30},{42,48},{48,42},{54,... | collective-permute-start | bytes 294920 | tf_op jit(solution)/shard_map/ppermute | solution.py:35
  44.3 23.6 %collective-permute-start.5 = (bf16[2,64,384]{2,1,0:T(8,128)(2,1)S(1)}, bf16[2,64,384]{2,1,0:T(8,128)(2,1)S(1)}, u32[]{:S(2)}, u32[]{:S(2)}) collective-permute-start(bf16[2,64,384]{2,1,0:T(8,128)(2,1)S(1)} %convert_element_type.55), channel_id=1, source_target_pairs={{0,6},{6,0},{12,18},{18,12},{24,30},{30,24},{36,42},{42,36},{48,54... | collective-permute-start | bytes 294920 | tf_op jit(solution)/shard_map/ppermute | solution.py:36
  48.5 29.2 %all-to-all-start.2 = ((f32[64,2,128]{2,1,0:T(2,128)}), f32[64,2,128]{2,1,0:T(2,128)S(1)}, u32[]{:S(2)}, u32[]{:S(2)}) async-start(f32[64,2,128]{2,1,0:T(2,128)} %broadcast_in_dim.14), calls=%async_computation.2 | async-start | bytes 131072 | tf_op jit(solution)/shard_map/all_to_all | solution.py:20
  77.7 0.6 copy-start.4
  80.0 4.8 %copy-start.6 = (f32[2,128]{1,0:T(2,128)S(1)}, f32[2,128]{1,0:T(2,128)}, u32[]{:S(2)}) copy-start(f32[2,128]{1,0:T(2,128)} %shard_map.68) | copy-start | bytes 3076
  81.0 13.8 %all-to-all-start.3 = ((bf16[6,64,384]{2,1,0:T(8,128)(2,1)}), bf16[6,64,384]{2,1,0:T(8,128)(2,1)S(1)}, u32[]{:S(2)}, u32[]{:S(2)}) async-start(bf16[6,64,384]{2,1,0:T(8,128)(2,1)} %fusion.7), calls=%async_computation.3 | async-start | bytes 589824 | tf_op jit(solution)/shard_map/all_to_all | solution.py:20
  84.8 12.5 %collective-permute-start.6 = (f32[2,128]{1,0:T(2,128)S(1)}, f32[2,128]{1,0:T(2,128)S(1)}, u32[]{:S(2)}, u32[]{:S(2)}) collective-permute-start(f32[2,128]{1,0:T(2,128)S(1)} %copy-done.6), channel_id=1, source_target_pairs={{0,192},{192,384},{384,576},{576,0},{1,385},{193,577},{385,1},{577... | collective-permute-start | bytes 3080 | tf_op jit(solution)/shard_map/ppermute | solution.py:82
  94.1 3.2 %collective-permute-start.7 = (f32[2,128]{1,0:T(2,128)S(1)}, f32[2,128]{1,0:T(2,128)S(1)}, u32[]{:S(2)}, u32[]{:S(2)}) collective-permute-start(f32[2,128]{1,0:T(2,128)S(1)} %copy-done.6), channel_id=1, source_target_pairs={{0,576},{192,0},{384,192},{576,384},{2,578},{194,2},{386,194},{578... | collective-permute-start | bytes 3080 | tf_op jit(solution)/shard_map/ppermute | solution.py:83

commit v8 on v7

--- a/solution.py
+++ b/solution.py
@@ -34,11 +34,12 @@
     across = [(i, i + 1 if i % 2 else i - 1) for i in range(1, count - 1)]
     other = lax.ppermute(vector, BLK, across)
     partner = lax.ppermute(vector, BLK, near)
-    even = lax.rem(lax.axis_index(BLK), 2) == 0
-    return jnp.where(even, other, partner), jnp.where(even, partner, other)
+    return other, partner
 
 
-def combine(low, vector, high, coeff):
+def combine(other, vector, partner, coeff):
+    even = lax.rem(lax.axis_index(BLK), 2) == 0
+    low, high = jnp.where(even, other, partner), jnp.where(even, partner, other)
     padded = jnp.concatenate([low, vector, high], axis=0).astype(F32)
     sectors, rows, width = vector.shape
     total = jnp.zeros(coeff.shape[:2] + (rows, width), F32)
@@ -103,8 +104,8 @@
     coeff = lax.optimization_barrier(coeff)
 
     psi_m = masked(psi, dims)
-    low, high = neighbours(psi_m)
-    outgoing = combine(low, psi_m, high, coeff)
+    other, partner = neighbours(psi_m)
+    outgoing = combine(other, psi_m, partner, coeff)
     left_mine = lax.dynamic_index_in_dim(left_env, core, 0, keepdims=False)
     left_sent = lax.dynamic_index_in_dim(left_env, 1 - core, 0, keepdims=False)
     left = jnp.concatenate([left_mine, lax.ppermute(left_sent, "core", swap)], axis=0)
@@ -118,9 +119,9 @@
     copies = jnp.broadcast_to(products[None], (lax.axis_size(NEAR),) + products.shape)
     sums = add_up(exchange(copies, NEAR))
     rounded = sigma.astype(BF16)
-    low, high = neighbours(rounded)
-    low, high, sums = lax.optimization_barrier((low, high, sums))
-    outgoing = combine(low, rounded, high, coeff)
+    other, partner = neighbours(rounded)
+    other, partner, sums = lax.optimization_barrier((other, partner, sums))
+    outgoing = combine(other, rounded, partner, coeff)
     shares = own_share(sums)
     part = product(exchange(outgoing, COL), left, right)
     part, shares = lax.optimization_barrier((part, shares))

time: 116 us -> 112 us (0.966)
  waiting for transfers between devices: 15.7 us -> 9.34 us
  starting transfers between devices: 59.3 us -> 64.9 us
  blocking collectives: 26.8 us -> 24 us
    ppermute x1, starting transfers between devices: 9.31 us -> 19.7 us  [own_share(): first = lax.ppermute(values, ('z_hi', 'core'), place[1] + place[2])]
    all_to_all x3, starting transfers between devices: 28 us -> 20.9 us  [exchange(): return lax.all_to_all(blocks, axes, 0, 0, tiled=True)]
    all_to_all x3, waiting for transfers between devices: 12.9 us -> 6.55 us  [exchange(): return lax.all_to_all(blocks, axes, 0, 0, tiled=True)]
    all_to_all x2, blocking collectives: 26.8 us -> 24 us  [exchange(): return lax.all_to_all(blocks, axes, 0, 0, tiled=True)]
    ppermute x2, starting transfers between devices: 10 us -> 12.3 us  [neighbours(): partner = lax.ppermute(vector, BLK, near)]
  transfers between devices with their start and end apart: 11 -> 11, of which waited for: 4 -> 4; matrix products, arithmetic and copies ran while one was open for 4% -> 4% of each run, Pallas kernels for 0% -> 1%
where the time goes in v8:
time: 112 us; the launch traced here: 111 us
  starting transfers between devices  64.9 us (58%)
  blocking collectives  24 us (21%)
  waiting for transfers between devices  9.34 us (8%)
  other arithmetic  5.48 us (5%)
  matrix products  2.94 us (3%)
  local copies, waits for them, and re-layouts  2.44 us (2%)
  Pallas kernels  1.48 us (1%)
    all_to_all x2, blocking collectives, exchange(): return lax.all_to_all(blocks, axes, 0, 0, tiled=True)  24 us
    all_to_all x3, starting transfers between devices, exchange(): return lax.all_to_all(blocks, axes, 0, 0, tiled=True)  20.9 us
    ppermute x1, starting transfers between devices, own_share(): first = lax.ppermute(values, ('z_hi', 'core'), place[1] + place[2])  19.7 us
    ppermute x2, starting transfers between devices, neighbours(): partner = lax.ppermute(vector, BLK, near)  12.3 us
    ppermute x1, starting transfers between devices, body(): lax.ppermute(right_env, 'core', swap)  7.78 us
    all_to_all x3, waiting for transfers between devices, exchange(): return lax.all_to_all(blocks, axes, 0, 0, tiled=True)  6.55 us
    dot_general x2, matrix products, product(): part = jnp.einsum('wac,wdc->ad', temp, right, preferred_element_type=F32)  2.94 us
  transfers between devices with their start and end apart: 11, of which 4 were waited for; matrix products, arithmetic and copies ran while one was open for 4% of the time, Pallas kernels for 1%

profile of v8, /device:TPU:1, one launch (start us, length us, event | category | flops | bytes accessed | tf_op | source)
XLA Modules:
  0.0 111.5 jit_solution(2571453129555279244)
XLA Ops:
  0.7 1.0 fusion.19
  1.6 0.7 collective-permute-start.2
  2.3 6.6 %collective-permute-start.3 = (bf16[2,64,384]{2,1,0:T(8,128)(2,1)S(1)}, bf16[2,64,384]{2,1,0:T(8,128)(2,1)S(1)}, u32[]{:S(2)}, u32[]{:S(2)}) collective-permute-start(bf16[2,64,384]{2,1,0:T(8,128)(2,1)S(1)} %fusion.19), channel_id=1, source_target_pairs={{0,6},{6,0},{12,18},{18,12},{24,30},{30,24},{36,42},{42,36},{48,54... | collective-permute-start | bytes 294920 | tf_op jit(solution)/shard_map/ppermute | solution.py:36
  8.9 7.8 %collective-permute-start.1 = (bf16[2,384,384]{2,1,0:T(8,128)(2,1)}, bf16[2,384,384]{2,1,0:T(8,128)(2,1)S(1)}, u32[]{:S(2)}, u32[]{:S(2)}) collective-permute-start(bf16[2,384,384]{2,1,0:T(8,128)(2,1)} %param.9), channel_id=1, source_target_pairs={{0,1},{1,0},{2,3},{3,2},{4,5},{5,4},{6,7},{7,6},{8,9},{9,8},{10,11... | collective-permute-start | bytes 1769480 | tf_op jit(solution)/shard_map/ppermute | solution.py:112
  16.7 0.7 convert_element_type.50
  18.1 1.0 fusion.12
  19.1 4.8 %all-to-all-start = ((bf16[6,64,384]{2,1,0:T(8,128)(2,1)}), bf16[6,64,384]{2,1,0:T(8,128)(2,1)S(1)}, u32[]{:S(2)}, u32[]{:S(2)}) async-start(bf16[6,64,384]{2,1,0:T(8,128)(2,1)} %fusion.12), calls=%async_computation | async-start | bytes 589824 | tf_op jit(solution)/shard_map/all_to_all | solution.py:20
  24.0 2.1 %collective-permute-start = (bf16[2,384,384]{2,1,0:T(8,128)(2,1)S(1)}, bf16[2,384,384]{2,1,0:T(8,128)(2,1)S(1)}, u32[]{:S(2)}, u32[]{:S(2)}) collective-permute-start(bf16[2,384,384]{2,1,0:T(8,128)(2,1)S(1)} %get-tuple-element.24), channel_id=1, source_target_pairs={{0,1},{1,0},{2,3},{3,2},{4,5},{5,4},{6,7},{7,6},{8,9},{9,8},{10,11... | collective-permute-start | bytes 1769480 | tf_op jit(solution)/shard_map/ppermute | solution.py:111
  26.2 0.1 pad_maximum_fusion.1
  26.3 1.7 %collective-permute-done = bf16[2,384,384]{2,1,0:T(8,128)(2,1)S(1)} collective-permute-done((bf16[2,384,384]{2,1,0:T(8,128)(2,1)S(1)}, bf16[2,384,384]{2,1,0:T(8,128)(2,1)S(1)}, u32[]{:S(2)}, u32[]{:S(2)}) %collective-permute-start) | collective-permute-done | bytes 589856 | tf_op jit(solution)/shard_map/ppermute | solution.py:111
  28.0 0.1 pad_maximum_fusion
  28.2 3.2 %all-to-all-done = bf16[6,64,384]{2,1,0:T(8,128)(2,1)S(1)} async-done(((bf16[6,64,384]{2,1,0:T(8,128)(2,1)}), bf16[6,64,384]{2,1,0:T(8,128)(2,1)S(1)}, u32[]{:S(2)}, u32[]{:S(2)}) %all-to-all-start) | async-done | bytes 294944 | tf_op jit(solution)/shard_map/all_to_all | solution.py:20
  31.4 1.5 %fusion.4 = bf16[384,384]{1,0:T(8,128)(2,1)S(1)} fusion(bf16[4,384,384]{2,1,0:T(8,128)(2,1)S(1)} %pad_maximum_fusion.1, bf16[4,384,384]{2,1,0:T(8,128)(2,1)S(1)} %pad_maximum_fusion, bf16[384,384,1]{1,0,2:T(8,128)(2,1)S(1)} %bitcast.105), kind=kOutput, calls=%fused_computation.6 | convolution fusion | flops 906706944 | bytes 2949120 | tf_op jit(solution)/shard_map/wac,wdc->ad/dot_general | solution.py:55
  32.8 10.6 %all_to_all.25 = bf16[6,64,384]{2,1,0:T(8,128)(2,1)S(1)} all-to-all(bf16[6,64,384]{2,1,0:T(8,128)(2,1)S(1)} %bitcast.107), channel_id=1, replica_groups=mesh['z_hi'=4,'x'=4,'y'=8,'z_lo'=3,'core'=2] {'z_lo','core'}, dimensions={0} | all-to-all | bytes 589824 | tf_op jit(solution)/shard_map/all_to_all | solution.py:20
  43.5 0.1 fusion.16
  43.7 0.7 broadcast_in_dim.14
  44.4 12.4 %all-to-all-start.2 = ((f32[64,2,128]{2,1,0:T(2,128)}), f32[64,2,128]{2,1,0:T(2,128)S(1)}, u32[]{:S(2)}, u32[]{:S(2)}) async-start(f32[64,2,128]{2,1,0:T(2,128)} %broadcast_in_dim.14), calls=%async_computation.2 | async-start | bytes 131072 | tf_op jit(solution)/shard_map/all_to_all | solution.py:20
  56.7 0.7 collective-permute-start.4
  57.4 5.7 %collective-permute-start.5 = (bf16[2,64,384]{2,1,0:T(8,128)(2,1)S(1)}, bf16[2,64,384]{2,1,0:T(8,128)(2,1)S(1)}, u32[]{:S(2)}, u32[]{:S(2)}) collective-permute-start(bf16[2,64,384]{2,1,0:T(8,128)(2,1)S(1)} %convert_element_type.55), channel_id=1, source_target_pairs={{0,6},{6,0},{12,18},{18,12},{24,30},{30,24},{36,42},{42,36},{48,54... | collective-permute-start | bytes 294920 | tf_op jit(solution)/shard_map/ppermute | solution.py:36
  63.1 3.4 %all-to-all-done.2.received = f32[64,2,128]{2,1,0:T(2,128)S(1)} async-done(((f32[64,2,128]{2,1,0:T(2,128)}), f32[64,2,128]{2,1,0:T(2,128)S(1)}, u32[]{:S(2)}, u32[]{:S(2)}) %all-to-all-start.2) | async-done | bytes 65568 | tf_op jit(solution)/shard_map/all_to_all | solution.py:20
  66.5 0.6 copy-done.4
  67.1 1.5 %shard_map.68 = f32[2,128]{1,0:T(2,128)} custom-call(f32[64,2,128]{2,1,0:T(2,128)} %copy-done.4), custom_call_target="tpu_custom_call" | custom-call | flops 30000001024 | tf_op jit(solution)/shard_map/pallas_call | solution.py:69
  68.8 1.0 fusion.7
  69.8 3.8 %all-to-all-start.3 = ((bf16[6,64,384]{2,1,0:T(8,128)(2,1)}), bf16[6,64,384]{2,1,0:T(8,128)(2,1)S(1)}, u32[]{:S(2)}, u32[]{:S(2)}) async-start(bf16[6,64,384]{2,1,0:T(8,128)(2,1)} %fusion.7), calls=%async_computation.3 | async-start | bytes 589824 | tf_op jit(solution)/shard_map/all_to_all | solution.py:20
  73.6 19.7 %collective-permute-start.6 = (f32[2,128]{1,0:T(2,128)S(1)}, f32[2,128]{1,0:T(2,128)S(1)}, u32[]{:S(2)}, u32[]{:S(2)}) collective-permute-start(f32[2,128]{1,0:T(2,128)S(1)} %copy-done.6), channel_id=1, source_target_pairs={{0,192},{192,384},{384,576},{576,0},{1,385},{193,577},{385,1},{577... | collective-permute-start | bytes 3080 | tf_op jit(solution)/shard_map/ppermute | solution.py:83
  93.4 0.7 collective-permute-start.7
  94.1 1.5 %fusion.5 = bf16[384,384]{1,0:T(8,128)(2,1)S(1)} fusion(bf16[4,384,384]{2,1,0:T(8,128)(2,1)S(1)} %pad_maximum_fusion.1, bf16[4,384,384]{2,1,0:T(8,128)(2,1)S(1)} %pad_maximum_fusion, bf16[384,384,1]{1,0,2:T(8,128)(2,1)S(1)} %bitcast.106), kind=kOutput, calls=%fused_computation.7 | convolution fusion | flops 906706944 | bytes 2949120 | tf_op jit(solution)/shard_map/wac,wdc->ad/dot_general | solution.py:55
  95.6 1.0 collective-permute-done.6
  96.8 13.4 %all_to_all.26 = bf16[6,72,384]{2,1,0:T(8,128)(2,1)S(1)} all-to-all(bf16[6,72,384]{2,1,0:T(8,128)(2,1)S(1)} %pad_maximum_fusion.2), channel_id=1, replica_groups=mesh['z_hi'=4,'x'=4,'y'=8,'z_lo'=3,'core'=2] {'z_lo','core'}, dimensions={0} | all-to-all | bytes 663552 | tf_op jit(solution)/shard_map/all_to_all | solution.py:20
  110.2 0.1 convert_reduce_fusion.2
  110.5 0.1 reduce_sum.72
  110.7 0.8 multiply_subtract_fusion
  (55 shorter events, 1.6 us)
Async XLA Ops:
  1.6 16.2 %collective-permute-start.2 = (bf16[2,64,384]{2,1,0:T(8,128)(2,1)S(1)}, bf16[2,64,384]{2,1,0:T(8,128)(2,1)S(1)}, u32[]{:S(2)}, u32[]{:S(2)}) collective-permute-start(bf16[2,64,384]{2,1,0:T(8,128)(2,1)S(1)} %fusion.19), channel_id=1, source_target_pairs={{6,12},{12,6},{18,24},{24,18},{30,36},{36,30},{42,48},{48,42},{54,... | collective-permute-start | bytes 294920 | tf_op jit(solution)/shard_map/ppermute | solution.py:35
  2.3 15.6 %collective-permute-start.3 = (bf16[2,64,384]{2,1,0:T(8,128)(2,1)S(1)}, bf16[2,64,384]{2,1,0:T(8,128)(2,1)S(1)}, u32[]{:S(2)}, u32[]{:S(2)}) collective-permute-start(bf16[2,64,384]{2,1,0:T(8,128)(2,1)S(1)} %fusion.19), channel_id=1, source_target_pairs={{0,6},{6,0},{12,18},{18,12},{24,30},{30,24},{36,42},{42,36},{48,54... | collective-permute-start | bytes 294920 | tf_op jit(solution)/shard_map/ppermute | solution.py:36
  8.9 17.3 %collective-permute-start.1 = (bf16[2,384,384]{2,1,0:T(8,128)(2,1)}, bf16[2,384,384]{2,1,0:T(8,128)(2,1)S(1)}, u32[]{:S(2)}, u32[]{:S(2)}) collective-permute-start(bf16[2,384,384]{2,1,0:T(8,128)(2,1)} %param.9), channel_id=1, source_target_pairs={{0,1},{1,0},{2,3},{3,2},{4,5},{5,4},{6,7},{7,6},{8,9},{9,8},{10,11... | collective-permute-start | bytes 1769480 | tf_op jit(solution)/shard_map/ppermute | solution.py:112
  18.1 5.8 %copy-start.1 = (bf16[2,2,384,384]{3,2,1,0:T(8,128)(2,1)S(1)}, bf16[2,2,384,384]{3,2,1,0:T(8,128)(2,1)}, u32[]{:S(2)}) copy-start(bf16[2,2,384,384]{3,2,1,0:T(8,128)(2,1)} %param.8) | copy-start | bytes 3538948
  19.1 12.3 %all-to-all-start = ((bf16[6,64,384]{2,1,0:T(8,128)(2,1)}), bf16[6,64,384]{2,1,0:T(8,128)(2,1)S(1)}, u32[]{:S(2)}, u32[]{:S(2)}) async-start(bf16[6,64,384]{2,1,0:T(8,128)(2,1)} %fusion.12), calls=%async_computation | async-start | bytes 589824 | tf_op jit(solution)/shard_map/all_to_all | solution.py:20
  23.9 2.3 %copy-start.2 = (bf16[2,384,384]{2,1,0:T(8,128)(2,1)S(1)}, bf16[2,384,384]{2,1,0:T(8,128)(2,1)}, u32[]{:S(2)}) copy-start(bf16[2,384,384]{2,1,0:T(8,128)(2,1)} %param.9) | copy-start | bytes 1769476
  24.0 4.0 %collective-permute-start = (bf16[2,384,384]{2,1,0:T(8,128)(2,1)S(1)}, bf16[2,384,384]{2,1,0:T(8,128)(2,1)S(1)}, u32[]{:S(2)}, u32[]{:S(2)}) collective-permute-start(bf16[2,384,384]{2,1,0:T(8,128)(2,1)S(1)} %get-tuple-element.24), channel_id=1, source_target_pairs={{0,1},{1,0},{2,3},{3,2},{4,5},{5,4},{6,7},{7,6},{8,9},{9,8},{10,11... | collective-permute-start | bytes 1769480 | tf_op jit(solution)/shard_map/ppermute | solution.py:111
  31.4 12.1 %copy-start.3 = (bf16[2,64,384]{2,1,0:T(8,128)(2,1)S(1)}, bf16[2,64,384]{2,1,0:T(8,128)(2,1)}, u32[]{:S(2)}) copy-start(bf16[2,64,384]{2,1,0:T(8,128)(2,1)} %param.5) | copy-start | bytes 294916
  31.4 12.1 %copy-start.5 = (s32[2]{0:T(128)S(1)}, s32[2]{0:T(128)}, u32[]{:S(2)}) copy-start(s32[2]{0:T(128)} %param.6) | copy-start | bytes 28
  43.6 67.1 %copy-start = (f32[2,64,384]{2,1,0:T(8,128)}, f32[2,64,384]{2,1,0:T(8,128)S(1)}, u32[]{:S(2)}) copy-start(f32[2,64,384]{2,1,0:T(8,128)S(1)} %get-tuple-element.22) | copy-start | bytes 589828
  44.4 22.2 %all-to-all-start.2 = ((f32[64,2,128]{2,1,0:T(2,128)}), f32[64,2,128]{2,1,0:T(2,128)S(1)}, u32[]{:S(2)}, u32[]{:S(2)}) async-start(f32[64,2,128]{2,1,0:T(2,128)} %broadcast_in_dim.14), calls=%async_computation.2 | async-start | bytes 131072 | tf_op jit(solution)/shard_map/all_to_all | solution.py:20
  56.7 11.9 %collective-permute-start.4 = (bf16[2,64,384]{2,1,0:T(8,128)(2,1)S(1)}, bf16[2,64,384]{2,1,0:T(8,128)(2,1)S(1)}, u32[]{:S(2)}, u32[]{:S(2)}) collective-permute-start(bf16[2,64,384]{2,1,0:T(8,128)(2,1)S(1)} %convert_element_type.55), channel_id=1, source_target_pairs={{6,12},{12,6},{18,24},{24,18},{30,36},{36,30},{42,48},{48,42},{54,... | collective-permute-start | bytes 294920 | tf_op jit(solution)/shard_map/ppermute | solution.py:35
  57.4 11.2 %collective-permute-start.5 = (bf16[2,64,384]{2,1,0:T(8,128)(2,1)S(1)}, bf16[2,64,384]{2,1,0:T(8,128)(2,1)S(1)}, u32[]{:S(2)}, u32[]{:S(2)}) collective-permute-start(bf16[2,64,384]{2,1,0:T(8,128)(2,1)S(1)} %convert_element_type.55), channel_id=1, source_target_pairs={{0,6},{6,0},{12,18},{18,12},{24,30},{30,24},{36,42},{42,36},{48,54... | collective-permute-start | bytes 294920 | tf_op jit(solution)/shard_map/ppermute | solution.py:36
  66.5 0.6 copy-start.4
  68.8 4.8 %copy-start.6 = (f32[2,128]{1,0:T(2,128)S(1)}, f32[2,128]{1,0:T(2,128)}, u32[]{:S(2)}) copy-start(f32[2,128]{1,0:T(2,128)} %shard_map.68) | copy-start | bytes 3076
  69.8 24.3 %all-to-all-start.3 = ((bf16[6,64,384]{2,1,0:T(8,128)(2,1)}), bf16[6,64,384]{2,1,0:T(8,128)(2,1)S(1)}, u32[]{:S(2)}, u32[]{:S(2)}) async-start(bf16[6,64,384]{2,1,0:T(8,128)(2,1)} %fusion.7), calls=%async_computation.3 | async-start | bytes 589824 | tf_op jit(solution)/shard_map/all_to_all | solution.py:20
  73.6 23.0 %collective-permute-start.6 = (f32[2,128]{1,0:T(2,128)S(1)}, f32[2,128]{1,0:T(2,128)S(1)}, u32[]{:S(2)}, u32[]{:S(2)}) collective-permute-start(f32[2,128]{1,0:T(2,128)S(1)} %copy-done.6), channel_id=1, source_target_pairs={{0,192},{192,384},{384,576},{576,0},{1,385},{193,577},{385,1},{577... | collective-permute-start | bytes 3080 | tf_op jit(solution)/shard_map/ppermute | solution.py:83
  93.4 3.2 %collective-permute-start.7 = (f32[2,128]{1,0:T(2,128)S(1)}, f32[2,128]{1,0:T(2,128)S(1)}, u32[]{:S(2)}, u32[]{:S(2)}) collective-permute-start(f32[2,128]{1,0:T(2,128)S(1)} %copy-done.6), channel_id=1, source_target_pairs={{0,576},{192,0},{384,192},{576,384},{2,578},{194,2},{386,194},{578... | collective-permute-start | bytes 3080 | tf_op jit(solution)/shard_map/ppermute | solution.py:84

commit v9 on v8

--- a/solution.py
+++ b/solution.py
@@ -76,12 +76,24 @@
 
 
 def own_share(values):
-    count = lax.axis_size("z_hi")
-    steps = [(h, (h + d) % count) for d in (1, 2, 3) for h in range(count)]
-    place = {d: [(CORES * h, CORES * t) for h, t in steps if (t - h) % count == d] for d in (1, 3)}
-    place[2] = [(CORES * h + 1, CORES * t + 1) for h, t in steps if (t - h) % count == 2]
-    first = lax.ppermute(values, ("z_hi", "core"), place[1] + place[2])
-    last = lax.ppermute(values, ("z_hi", "core"), place[3])
+    planes = lax.axis_size("z_hi")
+    places = lax.axis_size(("x", "y"))
+    edge = lax.axis_size("y") - 1
+    source = {0: edge, edge: places - 1, places - 1: 0}
+
+    def pairs(distance, core):
+        return [
+            (
+                (plane * places + source.get(place, place)) * CORES + core,
+                ((plane + distance) % planes * places + place) * CORES + core,
+            )
+            for plane in range(planes)
+            for place in range(places)
+        ]
+
+    axes = ("z_hi", "x", "y", "core")
+    first = lax.ppermute(values, axes, pairs(1, 0) + pairs(2, 1))
+    last = lax.ppermute(values, axes, pairs(3, 0))
     own = jnp.where(lax.axis_index("core") == 0, values, jnp.zeros_like(values))
     return own, first, last
 

time: 112 us -> 119 us (1.062)
  the two profiles are of different devices: /device:TPU:1 before, /device:TPU:192 now
where the time goes in v9:
time: 119 us
  starting transfers between devices  58.1 us (49%)
  blocking collectives  27.2 us (23%)
  waiting for transfers between devices  20 us (17%)
  other arithmetic  5.48 us (5%)
  matrix products  2.94 us (2%)
  local copies, waits for them, and re-layouts  2.45 us (2%)
  Pallas kernels  1.48 us (1%)
    all_to_all x2, blocking collectives, exchange(): return lax.all_to_all(blocks, axes, 0, 0, tiled=True)  27.2 us
    all_to_all x3, starting transfers between devices, exchange(): return lax.all_to_all(blocks, axes, 0, 0, tiled=True)  24.1 us
    ppermute x1, starting transfers between devices, own_share(): first = lax.ppermute(values, axes, pairs(1, 0) + pairs(2, 1))  13.8 us
    ppermute x2, starting transfers between devices, neighbours(): other = lax.ppermute(vector, BLK, across)  8.56 us
    all_to_all x3, waiting for transfers between devices, exchange(): return lax.all_to_all(blocks, axes, 0, 0, tiled=True)  7.96 us
    ppermute x1, waiting for transfers between devices, own_share(): last = lax.ppermute(values, axes, pairs(3, 0))  7.14 us
    ppermute x2, starting transfers between devices, neighbours(): partner = lax.ppermute(vector, BLK, near)  5.26 us
    ppermute x2, waiting for transfers between devices, neighbours(): other = lax.ppermute(vector, BLK, across)  3.42 us
  transfers between devices with their start and end apart: 11, of which 6 were waited for; matrix products, arithmetic and copies ran while one was open for 4% of the time, Pallas kernels for 1%

profile of v9, /device:TPU:192, one launch (start us, length us, event | category | flops | bytes accessed | tf_op | source)
XLA Modules:
  0.0 118.5 jit_solution(1849471039659810114)
XLA Ops:
  0.7 1.0 fusion.19
  1.6 4.8 %collective-permute-start.2 = (bf16[2,64,384]{2,1,0:T(8,128)(2,1)S(1)}, bf16[2,64,384]{2,1,0:T(8,128)(2,1)S(1)}, u32[]{:S(2)}, u32[]{:S(2)}) collective-permute-start(bf16[2,64,384]{2,1,0:T(8,128)(2,1)S(1)} %fusion.19), channel_id=1, source_target_pairs={{6,12},{12,6},{18,24},{24,18},{30,36},{36,30},{42,48},{48,42},{54,... | collective-permute-start | bytes 294920 | tf_op jit(solution)/shard_map/ppermute | solution.py:35
  6.5 2.1 %collective-permute-start.3 = (bf16[2,64,384]{2,1,0:T(8,128)(2,1)S(1)}, bf16[2,64,384]{2,1,0:T(8,128)(2,1)S(1)}, u32[]{:S(2)}, u32[]{:S(2)}) collective-permute-start(bf16[2,64,384]{2,1,0:T(8,128)(2,1)S(1)} %fusion.19), channel_id=1, source_target_pairs={{0,6},{6,0},{12,18},{18,12},{24,30},{30,24},{36,42},{42,36},{48,54... | collective-permute-start | bytes 294920 | tf_op jit(solution)/shard_map/ppermute | solution.py:36
  8.6 1.9 %collective-permute-start.1 = (bf16[2,384,384]{2,1,0:T(8,128)(2,1)}, bf16[2,384,384]{2,1,0:T(8,128)(2,1)S(1)}, u32[]{:S(2)}, u32[]{:S(2)}) collective-permute-start(bf16[2,384,384]{2,1,0:T(8,128)(2,1)} %param.9), channel_id=1, source_target_pairs={{0,1},{1,0},{2,3},{3,2},{4,5},{5,4},{6,7},{7,6},{8,9},{9,8},{10,11... | collective-permute-start | bytes 1769480 | tf_op jit(solution)/shard_map/ppermute | solution.py:124
  10.6 0.7 convert_element_type.50
  11.8 2.4 %collective-permute-done.2 = bf16[2,64,384]{2,1,0:T(8,128)(2,1)S(1)} collective-permute-done((bf16[2,64,384]{2,1,0:T(8,128)(2,1)S(1)}, bf16[2,64,384]{2,1,0:T(8,128)(2,1)S(1)}, u32[]{:S(2)}, u32[]{:S(2)}) %collective-permute-start.2) | collective-permute-done | bytes 98336 | tf_op jit(solution)/shard_map/ppermute | solution.py:35
  14.4 1.0 fusion.12
  15.3 9.3 %all-to-all-start = ((bf16[6,64,384]{2,1,0:T(8,128)(2,1)}), bf16[6,64,384]{2,1,0:T(8,128)(2,1)S(1)}, u32[]{:S(2)}, u32[]{:S(2)}) async-start(bf16[6,64,384]{2,1,0:T(8,128)(2,1)} %fusion.12), calls=%async_computation | async-start | bytes 589824 | tf_op jit(solution)/shard_map/all_to_all | solution.py:20
  24.7 2.5 %collective-permute-start = (bf16[2,384,384]{2,1,0:T(8,128)(2,1)S(1)}, bf16[2,384,384]{2,1,0:T(8,128)(2,1)S(1)}, u32[]{:S(2)}, u32[]{:S(2)}) collective-permute-start(bf16[2,384,384]{2,1,0:T(8,128)(2,1)S(1)} %get-tuple-element.24), channel_id=1, source_target_pairs={{0,1},{1,0},{2,3},{3,2},{4,5},{5,4},{6,7},{7,6},{8,9},{9,8},{10,11... | collective-permute-start | bytes 1769480 | tf_op jit(solution)/shard_map/ppermute | solution.py:123
  27.3 0.1 pad_maximum_fusion.1
  27.4 1.4 %collective-permute-done = bf16[2,384,384]{2,1,0:T(8,128)(2,1)S(1)} collective-permute-done((bf16[2,384,384]{2,1,0:T(8,128)(2,1)S(1)}, bf16[2,384,384]{2,1,0:T(8,128)(2,1)S(1)}, u32[]{:S(2)}, u32[]{:S(2)}) %collective-permute-start) | collective-permute-done | bytes 589856 | tf_op jit(solution)/shard_map/ppermute | solution.py:123
  28.9 0.1 pad_maximum_fusion
  29.0 5.1 %all-to-all-done = bf16[6,64,384]{2,1,0:T(8,128)(2,1)S(1)} async-done(((bf16[6,64,384]{2,1,0:T(8,128)(2,1)}), bf16[6,64,384]{2,1,0:T(8,128)(2,1)S(1)}, u32[]{:S(2)}, u32[]{:S(2)}) %all-to-all-start) | async-done | bytes 294944 | tf_op jit(solution)/shard_map/all_to_all | solution.py:20
  34.2 1.5 %fusion.4 = bf16[384,384]{1,0:T(8,128)(2,1)S(1)} fusion(bf16[4,384,384]{2,1,0:T(8,128)(2,1)S(1)} %pad_maximum_fusion.1, bf16[4,384,384]{2,1,0:T(8,128)(2,1)S(1)} %pad_maximum_fusion, bf16[384,384,1]{1,0,2:T(8,128)(2,1)S(1)} %bitcast.105), kind=kOutput, calls=%fused_computation.6 | convolution fusion | flops 906706944 | bytes 2949120 | tf_op jit(solution)/shard_map/wac,wdc->ad/dot_general | solution.py:55
  35.6 12.0 %all_to_all.25 = bf16[6,64,384]{2,1,0:T(8,128)(2,1)S(1)} all-to-all(bf16[6,64,384]{2,1,0:T(8,128)(2,1)S(1)} %bitcast.107), channel_id=1, replica_groups=mesh['z_hi'=4,'x'=4,'y'=8,'z_lo'=3,'core'=2] {'z_lo','core'}, dimensions={0} | all-to-all | bytes 589824 | tf_op jit(solution)/shard_map/all_to_all | solution.py:20
  47.6 0.1 fusion.16
  47.9 0.7 broadcast_in_dim.14
  48.5 7.8 %all-to-all-start.2 = ((f32[64,2,128]{2,1,0:T(2,128)}), f32[64,2,128]{2,1,0:T(2,128)S(1)}, u32[]{:S(2)}, u32[]{:S(2)}) async-start(f32[64,2,128]{2,1,0:T(2,128)} %broadcast_in_dim.14), calls=%async_computation.2 | async-start | bytes 131072 | tf_op jit(solution)/shard_map/all_to_all | solution.py:20
  56.4 3.7 %collective-permute-start.4 = (bf16[2,64,384]{2,1,0:T(8,128)(2,1)S(1)}, bf16[2,64,384]{2,1,0:T(8,128)(2,1)S(1)}, u32[]{:S(2)}, u32[]{:S(2)}) collective-permute-start(bf16[2,64,384]{2,1,0:T(8,128)(2,1)S(1)} %convert_element_type.55), channel_id=1, source_target_pairs={{6,12},{12,6},{18,24},{24,18},{30,36},{36,30},{42,48},{48,42},{54,... | collective-permute-start | bytes 294920 | tf_op jit(solution)/shard_map/ppermute | solution.py:35
  60.1 3.1 %collective-permute-start.5 = (bf16[2,64,384]{2,1,0:T(8,128)(2,1)S(1)}, bf16[2,64,384]{2,1,0:T(8,128)(2,1)S(1)}, u32[]{:S(2)}, u32[]{:S(2)}) collective-permute-start(bf16[2,64,384]{2,1,0:T(8,128)(2,1)S(1)} %convert_element_type.55), channel_id=1, source_target_pairs={{0,6},{6,0},{12,18},{18,12},{24,30},{30,24},{36,42},{42,36},{48,54... | collective-permute-start | bytes 294920 | tf_op jit(solution)/shard_map/ppermute | solution.py:36
  63.2 2.8 %all-to-all-done.2.received = f32[64,2,128]{2,1,0:T(2,128)S(1)} async-done(((f32[64,2,128]{2,1,0:T(2,128)}), f32[64,2,128]{2,1,0:T(2,128)S(1)}, u32[]{:S(2)}, u32[]{:S(2)}) %all-to-all-start.2) | async-done | bytes 65568 | tf_op jit(solution)/shard_map/all_to_all | solution.py:20
  66.1 0.6 copy-done.4
  66.7 1.5 %shard_map.68 = f32[2,128]{1,0:T(2,128)} custom-call(f32[64,2,128]{2,1,0:T(2,128)} %copy-done.4), custom_call_target="tpu_custom_call" | custom-call | flops 30000001024 | tf_op jit(solution)/shard_map/pallas_call | solution.py:69
  68.2 1.0 collective-permute-done.4
  69.4 1.0 fusion.7
  70.3 7.1 %all-to-all-start.3 = ((bf16[6,64,384]{2,1,0:T(8,128)(2,1)}), bf16[6,64,384]{2,1,0:T(8,128)(2,1)S(1)}, u32[]{:S(2)}, u32[]{:S(2)}) async-start(bf16[6,64,384]{2,1,0:T(8,128)(2,1)} %fusion.7), calls=%async_computation.3 | async-start | bytes 589824 | tf_op jit(solution)/shard_map/all_to_all | solution.py:20
  77.5 13.8 %collective-permute-start.6 = (f32[2,128]{1,0:T(2,128)S(1)}, f32[2,128]{1,0:T(2,128)S(1)}, u32[]{:S(2)}, u32[]{:S(2)}) collective-permute-start(f32[2,128]{1,0:T(2,128)S(1)} %copy-done.6), channel_id=1, source_target_pairs={{42,192},{6,198},{12,204},{18,210},{24,216},{30,222},{36,228},{186... | collective-permute-start | bytes 3080 | tf_op jit(solution)/shard_map/ppermute | solution.py:95
  91.2 1.9 %collective-permute-start.7 = (f32[2,128]{1,0:T(2,128)S(1)}, f32[2,128]{1,0:T(2,128)S(1)}, u32[]{:S(2)}, u32[]{:S(2)}) collective-permute-start(f32[2,128]{1,0:T(2,128)S(1)} %copy-done.6), channel_id=1, source_target_pairs={{42,576},{6,582},{12,588},{18,594},{24,600},{30,606},{36,612},{186... | collective-permute-start | bytes 3080 | tf_op jit(solution)/shard_map/ppermute | solution.py:96
  93.2 1.5 %fusion.5 = bf16[384,384]{1,0:T(8,128)(2,1)S(1)} fusion(bf16[4,384,384]{2,1,0:T(8,128)(2,1)S(1)} %pad_maximum_fusion.1, bf16[4,384,384]{2,1,0:T(8,128)(2,1)S(1)} %pad_maximum_fusion, bf16[384,384,1]{1,0,2:T(8,128)(2,1)S(1)} %bitcast.106), kind=kOutput, calls=%fused_computation.7 | convolution fusion | flops 906706944 | bytes 2949120 | tf_op jit(solution)/shard_map/wac,wdc->ad/dot_general | solution.py:55
  94.7 7.1 %collective-permute-done.7 = f32[2,128]{1,0:T(2,128)S(1)} collective-permute-done((f32[2,128]{1,0:T(2,128)S(1)}, f32[2,128]{1,0:T(2,128)S(1)}, u32[]{:S(2)}, u32[]{:S(2)}) %collective-permute-start.7) | collective-permute-done | bytes 1056 | tf_op jit(solution)/shard_map/ppermute | solution.py:96
  102.0 15.2 %all_to_all.26 = bf16[6,72,384]{2,1,0:T(8,128)(2,1)S(1)} all-to-all(bf16[6,72,384]{2,1,0:T(8,128)(2,1)S(1)} %pad_maximum_fusion.2), channel_id=1, replica_groups=mesh['z_hi'=4,'x'=4,'y'=8,'z_lo'=3,'core'=2] {'z_lo','core'}, dimensions={0} | all-to-all | bytes 663552 | tf_op jit(solution)/shard_map/all_to_all | solution.py:20
  117.7 0.8 multiply_subtract_fusion
  (55 shorter events, 1.8 us)
Async XLA Ops:
  1.6 12.5 %collective-permute-start.2 = (bf16[2,64,384]{2,1,0:T(8,128)(2,1)S(1)}, bf16[2,64,384]{2,1,0:T(8,128)(2,1)S(1)}, u32[]{:S(2)}, u32[]{:S(2)}) collective-permute-start(bf16[2,64,384]{2,1,0:T(8,128)(2,1)S(1)} %fusion.19), channel_id=1, source_target_pairs={{6,12},{12,6},{18,24},{24,18},{30,36},{36,30},{42,48},{48,42},{54,... | collective-permute-start | bytes 294920 | tf_op jit(solution)/shard_map/ppermute | solution.py:35
  6.5 7.7 %collective-permute-start.3 = (bf16[2,64,384]{2,1,0:T(8,128)(2,1)S(1)}, bf16[2,64,384]{2,1,0:T(8,128)(2,1)S(1)}, u32[]{:S(2)}, u32[]{:S(2)}) collective-permute-start(bf16[2,64,384]{2,1,0:T(8,128)(2,1)S(1)} %fusion.19), channel_id=1, source_target_pairs={{0,6},{6,0},{12,18},{18,12},{24,30},{30,24},{36,42},{42,36},{48,54... | collective-permute-start | bytes 294920 | tf_op jit(solution)/shard_map/ppermute | solution.py:36
  8.6 18.6 %collective-permute-start.1 = (bf16[2,384,384]{2,1,0:T(8,128)(2,1)}, bf16[2,384,384]{2,1,0:T(8,128)(2,1)S(1)}, u32[]{:S(2)}, u32[]{:S(2)}) collective-permute-start(bf16[2,384,384]{2,1,0:T(8,128)(2,1)} %param.9), channel_id=1, source_target_pairs={{0,1},{1,0},{2,3},{3,2},{4,5},{5,4},{6,7},{7,6},{8,9},{9,8},{10,11... | collective-permute-start | bytes 1769480 | tf_op jit(solution)/shard_map/ppermute | solution.py:124
  14.4 10.2 %copy-start.1 = (bf16[2,2,384,384]{3,2,1,0:T(8,128)(2,1)S(1)}, bf16[2,2,384,384]{3,2,1,0:T(8,128)(2,1)}, u32[]{:S(2)}) copy-start(bf16[2,2,384,384]{3,2,1,0:T(8,128)(2,1)} %param.8) | copy-start | bytes 3538948
  15.3 18.8 %all-to-all-start = ((bf16[6,64,384]{2,1,0:T(8,128)(2,1)}), bf16[6,64,384]{2,1,0:T(8,128)(2,1)S(1)}, u32[]{:S(2)}, u32[]{:S(2)}) async-start(bf16[6,64,384]{2,1,0:T(8,128)(2,1)} %fusion.12), calls=%async_computation | async-start | bytes 589824 | tf_op jit(solution)/shard_map/all_to_all | solution.py:20
  24.6 2.7 %copy-start.2 = (bf16[2,384,384]{2,1,0:T(8,128)(2,1)S(1)}, bf16[2,384,384]{2,1,0:T(8,128)(2,1)}, u32[]{:S(2)}) copy-start(bf16[2,384,384]{2,1,0:T(8,128)(2,1)} %param.9) | copy-start | bytes 1769476
  24.7 4.1 %collective-permute-start = (bf16[2,384,384]{2,1,0:T(8,128)(2,1)S(1)}, bf16[2,384,384]{2,1,0:T(8,128)(2,1)S(1)}, u32[]{:S(2)}, u32[]{:S(2)}) collective-permute-start(bf16[2,384,384]{2,1,0:T(8,128)(2,1)S(1)} %get-tuple-element.24), channel_id=1, source_target_pairs={{0,1},{1,0},{2,3},{3,2},{4,5},{5,4},{6,7},{7,6},{8,9},{9,8},{10,11... | collective-permute-start | bytes 1769480 | tf_op jit(solution)/shard_map/ppermute | solution.py:123
  34.1 13.5 %copy-start.3 = (bf16[2,64,384]{2,1,0:T(8,128)(2,1)S(1)}, bf16[2,64,384]{2,1,0:T(8,128)(2,1)}, u32[]{:S(2)}) copy-start(bf16[2,64,384]{2,1,0:T(8,128)(2,1)} %param.5) | copy-start | bytes 294916
  34.1 13.5 %copy-start.5 = (s32[2]{0:T(128)S(1)}, s32[2]{0:T(128)}, u32[]{:S(2)}) copy-start(s32[2]{0:T(128)} %param.6) | copy-start | bytes 28
  47.8 70.0 %copy-start = (f32[2,64,384]{2,1,0:T(8,128)}, f32[2,64,384]{2,1,0:T(8,128)S(1)}, u32[]{:S(2)}) copy-start(f32[2,64,384]{2,1,0:T(8,128)S(1)} %get-tuple-element.22) | copy-start | bytes 589828
  48.5 17.5 %all-to-all-start.2 = ((f32[64,2,128]{2,1,0:T(2,128)}), f32[64,2,128]{2,1,0:T(2,128)S(1)}, u32[]{:S(2)}, u32[]{:S(2)}) async-start(f32[64,2,128]{2,1,0:T(2,128)} %broadcast_in_dim.14), calls=%async_computation.2 | async-start | bytes 131072 | tf_op jit(solution)/shard_map/all_to_all | solution.py:20
  56.4 12.8 %collective-permute-start.4 = (bf16[2,64,384]{2,1,0:T(8,128)(2,1)S(1)}, bf16[2,64,384]{2,1,0:T(8,128)(2,1)S(1)}, u32[]{:S(2)}, u32[]{:S(2)}) collective-permute-start(bf16[2,64,384]{2,1,0:T(8,128)(2,1)S(1)} %convert_element_type.55), channel_id=1, source_target_pairs={{6,12},{12,6},{18,24},{24,18},{30,36},{36,30},{42,48},{48,42},{54,... | collective-permute-start | bytes 294920 | tf_op jit(solution)/shard_map/ppermute | solution.py:35
  60.1 9.1 %collective-permute-start.5 = (bf16[2,64,384]{2,1,0:T(8,128)(2,1)S(1)}, bf16[2,64,384]{2,1,0:T(8,128)(2,1)S(1)}, u32[]{:S(2)}, u32[]{:S(2)}) collective-permute-start(bf16[2,64,384]{2,1,0:T(8,128)(2,1)S(1)} %convert_element_type.55), channel_id=1, source_target_pairs={{0,6},{6,0},{12,18},{18,12},{24,30},{30,24},{36,42},{42,36},{48,54... | collective-permute-start | bytes 294920 | tf_op jit(solution)/shard_map/ppermute | solution.py:36
  66.1 0.6 copy-start.4
  69.4 8.1 %copy-start.6 = (f32[2,128]{1,0:T(2,128)S(1)}, f32[2,128]{1,0:T(2,128)}, u32[]{:S(2)}) copy-start(f32[2,128]{1,0:T(2,128)} %shard_map.68) | copy-start | bytes 3076
  70.3 22.8 %all-to-all-start.3 = ((bf16[6,64,384]{2,1,0:T(8,128)(2,1)}), bf16[6,64,384]{2,1,0:T(8,128)(2,1)S(1)}, u32[]{:S(2)}, u32[]{:S(2)}) async-start(bf16[6,64,384]{2,1,0:T(8,128)(2,1)} %fusion.7), calls=%async_computation.3 | async-start | bytes 589824 | tf_op jit(solution)/shard_map/all_to_all | solution.py:20
  77.5 17.2 %collective-permute-start.6 = (f32[2,128]{1,0:T(2,128)S(1)}, f32[2,128]{1,0:T(2,128)S(1)}, u32[]{:S(2)}, u32[]{:S(2)}) collective-permute-start(f32[2,128]{1,0:T(2,128)S(1)} %copy-done.6), channel_id=1, source_target_pairs={{42,192},{6,198},{12,204},{18,210},{24,216},{30,222},{36,228},{186... | collective-permute-start | bytes 3080 | tf_op jit(solution)/shard_map/ppermute | solution.py:95
  91.2 10.6 %collective-permute-start.7 = (f32[2,128]{1,0:T(2,128)S(1)}, f32[2,128]{1,0:T(2,128)S(1)}, u32[]{:S(2)}, u32[]{:S(2)}) collective-permute-start(f32[2,128]{1,0:T(2,128)S(1)} %copy-done.6), channel_id=1, source_target_pairs={{42,576},{6,582},{12,588},{18,594},{24,600},{30,606},{36,612},{186... | collective-permute-start | bytes 3080 | tf_op jit(solution)/shard_map/ppermute | solution.py:96

commit v10 on v8

--- a/solution.py
+++ b/solution.py
@@ -120,7 +120,7 @@
     sums = add_up(exchange(copies, NEAR))
     rounded = sigma.astype(BF16)
     other, partner = neighbours(rounded)
-    other, partner, sums = lax.optimization_barrier((other, partner, sums))
+    partner, other, sums = lax.optimization_barrier((partner, other, sums))
     outgoing = combine(other, rounded, partner, coeff)
     shares = own_share(sums)
     part = product(exchange(outgoing, COL), left, right)

time: 112 us -> 115 us (1.027)
  waiting for transfers between devices: 9.34 us -> 11.8 us
    ppermute x1, starting transfers between devices: 19.7 us -> 23 us  [own_share(): first = lax.ppermute(values, ('z_hi', 'core'), place[1] + place[2])]
    ppermute x2, starting transfers between devices: 12.3 us -> 9.87 us  [neighbours(): partner = lax.ppermute(vector, BLK, near)]
    all_to_all x3, waiting for transfers between devices: 6.55 us -> 8.98 us  [exchange(): return lax.all_to_all(blocks, axes, 0, 0, tiled=True)]
where the time goes in v10:
time: 115 us
  starting transfers between devices  65.8 us (57%)
  blocking collectives  24 us (21%)
  waiting for transfers between devices  11.8 us (10%)
  other arithmetic  5.48 us (5%)
  matrix products  2.94 us (3%)
  local copies, waits for them, and re-layouts  2.44 us (2%)
  Pallas kernels  1.48 us (1%)
    all_to_all x2, blocking collectives, exchange(): return lax.all_to_all(blocks, axes, 0, 0, tiled=True)  24 us
    ppermute x1, starting transfers between devices, own_share(): first = lax.ppermute(values, ('z_hi', 'core'), place[1] + place[2])  23 us
    all_to_all x3, starting transfers between devices, exchange(): return lax.all_to_all(blocks, axes, 0, 0, tiled=True)  20.9 us
    ppermute x2, starting transfers between devices, neighbours(): partner = lax.ppermute(vector, BLK, near)  9.87 us
    all_to_all x3, waiting for transfers between devices, exchange(): return lax.all_to_all(blocks, axes, 0, 0, tiled=True)  8.98 us
    ppermute x1, starting transfers between devices, body(): lax.ppermute(right_env, 'core', swap)  7.78 us
    dot_general x2, matrix products, product(): part = jnp.einsum('wac,wdc->ad', temp, right, preferred_element_type=F32)  2.94 us
  transfers between devices with their start and end apart: 11, of which 4 were waited for; matrix products, arithmetic and copies ran while one was open for 4% of the time, Pallas kernels for 1%

profile of v10, /device:TPU:1, one launch (start us, length us, event | category | flops | bytes accessed | tf_op | source)
XLA Modules:
  0.0 114.8 jit_solution(15705267298144612830)
XLA Ops:
  0.7 1.0 fusion.19
  1.6 0.7 collective-permute-start.2
  2.3 6.6 %collective-permute-start.3 = (bf16[2,64,384]{2,1,0:T(8,128)(2,1)S(1)}, bf16[2,64,384]{2,1,0:T(8,128)(2,1)S(1)}, u32[]{:S(2)}, u32[]{:S(2)}) collective-permute-start(bf16[2,64,384]{2,1,0:T(8,128)(2,1)S(1)} %fusion.19), channel_id=1, source_target_pairs={{0,6},{6,0},{12,18},{18,12},{24,30},{30,24},{36,42},{42,36},{48,54... | collective-permute-start | bytes 294920 | tf_op jit(solution)/shard_map/ppermute | solution.py:36
  8.9 7.8 %collective-permute-start.1 = (bf16[2,384,384]{2,1,0:T(8,128)(2,1)}, bf16[2,384,384]{2,1,0:T(8,128)(2,1)S(1)}, u32[]{:S(2)}, u32[]{:S(2)}) collective-permute-start(bf16[2,384,384]{2,1,0:T(8,128)(2,1)} %param.9), channel_id=1, source_target_pairs={{0,1},{1,0},{2,3},{3,2},{4,5},{5,4},{6,7},{7,6},{8,9},{9,8},{10,11... | collective-permute-start | bytes 1769480 | tf_op jit(solution)/shard_map/ppermute | solution.py:112
  16.7 0.7 convert_element_type.50
  18.1 1.0 fusion.12
  19.1 4.8 %all-to-all-start = ((bf16[6,64,384]{2,1,0:T(8,128)(2,1)}), bf16[6,64,384]{2,1,0:T(8,128)(2,1)S(1)}, u32[]{:S(2)}, u32[]{:S(2)}) async-start(bf16[6,64,384]{2,1,0:T(8,128)(2,1)} %fusion.12), calls=%async_computation | async-start | bytes 589824 | tf_op jit(solution)/shard_map/all_to_all | solution.py:20
  24.0 2.1 %collective-permute-start = (bf16[2,384,384]{2,1,0:T(8,128)(2,1)S(1)}, bf16[2,384,384]{2,1,0:T(8,128)(2,1)S(1)}, u32[]{:S(2)}, u32[]{:S(2)}) collective-permute-start(bf16[2,384,384]{2,1,0:T(8,128)(2,1)S(1)} %get-tuple-element.24), channel_id=1, source_target_pairs={{0,1},{1,0},{2,3},{3,2},{4,5},{5,4},{6,7},{7,6},{8,9},{9,8},{10,11... | collective-permute-start | bytes 1769480 | tf_op jit(solution)/shard_map/ppermute | solution.py:111
  26.2 0.1 pad_maximum_fusion.1
  26.3 1.7 %collective-permute-done = bf16[2,384,384]{2,1,0:T(8,128)(2,1)S(1)} collective-permute-done((bf16[2,384,384]{2,1,0:T(8,128)(2,1)S(1)}, bf16[2,384,384]{2,1,0:T(8,128)(2,1)S(1)}, u32[]{:S(2)}, u32[]{:S(2)}) %collective-permute-start) | collective-permute-done | bytes 589856 | tf_op jit(solution)/shard_map/ppermute | solution.py:111
  28.0 0.1 pad_maximum_fusion
  28.2 3.2 %all-to-all-done = bf16[6,64,384]{2,1,0:T(8,128)(2,1)S(1)} async-done(((bf16[6,64,384]{2,1,0:T(8,128)(2,1)}), bf16[6,64,384]{2,1,0:T(8,128)(2,1)S(1)}, u32[]{:S(2)}, u32[]{:S(2)}) %all-to-all-start) | async-done | bytes 294944 | tf_op jit(solution)/shard_map/all_to_all | solution.py:20
  31.4 1.5 %fusion.4 = bf16[384,384]{1,0:T(8,128)(2,1)S(1)} fusion(bf16[4,384,384]{2,1,0:T(8,128)(2,1)S(1)} %pad_maximum_fusion.1, bf16[4,384,384]{2,1,0:T(8,128)(2,1)S(1)} %pad_maximum_fusion, bf16[384,384,1]{1,0,2:T(8,128)(2,1)S(1)} %bitcast.105), kind=kOutput, calls=%fused_computation.6 | convolution fusion | flops 906706944 | bytes 2949120 | tf_op jit(solution)/shard_map/wac,wdc->ad/dot_general | solution.py:55
  32.8 10.6 %all_to_all.25 = bf16[6,64,384]{2,1,0:T(8,128)(2,1)S(1)} all-to-all(bf16[6,64,384]{2,1,0:T(8,128)(2,1)S(1)} %bitcast.107), channel_id=1, replica_groups=mesh['z_hi'=4,'x'=4,'y'=8,'z_lo'=3,'core'=2] {'z_lo','core'}, dimensions={0} | all-to-all | bytes 589824 | tf_op jit(solution)/shard_map/all_to_all | solution.py:20
  43.5 0.1 fusion.16
  43.7 0.7 broadcast_in_dim.14
  44.4 12.4 %all-to-all-start.2 = ((f32[64,2,128]{2,1,0:T(2,128)}), f32[64,2,128]{2,1,0:T(2,128)S(1)}, u32[]{:S(2)}, u32[]{:S(2)}) async-start(f32[64,2,128]{2,1,0:T(2,128)} %broadcast_in_dim.14), calls=%async_computation.2 | async-start | bytes 131072 | tf_op jit(solution)/shard_map/all_to_all | solution.py:20
  56.7 3.3 %collective-permute-start.4 = (bf16[2,64,384]{2,1,0:T(8,128)(2,1)S(1)}, bf16[2,64,384]{2,1,0:T(8,128)(2,1)S(1)}, u32[]{:S(2)}, u32[]{:S(2)}) collective-permute-start(bf16[2,64,384]{2,1,0:T(8,128)(2,1)S(1)} %convert_element_type.55), channel_id=1, source_target_pairs={{0,6},{6,0},{12,18},{18,12},{24,30},{30,24},{36,42},{42,36},{48,54... | collective-permute-start | bytes 294920 | tf_op jit(solution)/shard_map/ppermute | solution.py:36
  60.0 0.7 collective-permute-start.5
  60.7 5.8 %all-to-all-done.2.received = f32[64,2,128]{2,1,0:T(2,128)S(1)} async-done(((f32[64,2,128]{2,1,0:T(2,128)}), f32[64,2,128]{2,1,0:T(2,128)S(1)}, u32[]{:S(2)}, u32[]{:S(2)}) %all-to-all-start.2) | async-done | bytes 65568 | tf_op jit(solution)/shard_map/all_to_all | solution.py:20
  66.5 0.6 copy-done.4
  67.1 1.5 %shard_map.68 = f32[2,128]{1,0:T(2,128)} custom-call(f32[64,2,128]{2,1,0:T(2,128)} %copy-done.4), custom_call_target="tpu_custom_call" | custom-call | flops 30000001024 | tf_op jit(solution)/shard_map/pallas_call | solution.py:69
  68.8 1.0 fusion.7
  69.8 3.8 %all-to-all-start.3 = ((bf16[6,64,384]{2,1,0:T(8,128)(2,1)}), bf16[6,64,384]{2,1,0:T(8,128)(2,1)S(1)}, u32[]{:S(2)}, u32[]{:S(2)}) async-start(bf16[6,64,384]{2,1,0:T(8,128)(2,1)} %fusion.7), calls=%async_computation.3 | async-start | bytes 589824 | tf_op jit(solution)/shard_map/all_to_all | solution.py:20
  73.6 23.0 %collective-permute-start.6 = (f32[2,128]{1,0:T(2,128)S(1)}, f32[2,128]{1,0:T(2,128)S(1)}, u32[]{:S(2)}, u32[]{:S(2)}) collective-permute-start(f32[2,128]{1,0:T(2,128)S(1)} %copy-done.6), channel_id=1, source_target_pairs={{0,192},{192,384},{384,576},{576,0},{1,385},{193,577},{385,1},{577... | collective-permute-start | bytes 3080 | tf_op jit(solution)/shard_map/ppermute | solution.py:83
  96.7 0.7 collective-permute-start.7
  97.4 1.5 %fusion.5 = bf16[384,384]{1,0:T(8,128)(2,1)S(1)} fusion(bf16[4,384,384]{2,1,0:T(8,128)(2,1)S(1)} %pad_maximum_fusion.1, bf16[4,384,384]{2,1,0:T(8,128)(2,1)S(1)} %pad_maximum_fusion, bf16[384,384,1]{1,0,2:T(8,128)(2,1)S(1)} %bitcast.106), kind=kOutput, calls=%fused_computation.7 | convolution fusion | flops 906706944 | bytes 2949120 | tf_op jit(solution)/shard_map/wac,wdc->ad/dot_general | solution.py:55
  98.9 1.0 collective-permute-done.6
  100.1 13.4 %all_to_all.26 = bf16[6,72,384]{2,1,0:T(8,128)(2,1)S(1)} all-to-all(bf16[6,72,384]{2,1,0:T(8,128)(2,1)S(1)} %pad_maximum_fusion.2), channel_id=1, replica_groups=mesh['z_hi'=4,'x'=4,'y'=8,'z_lo'=3,'core'=2] {'z_lo','core'}, dimensions={0} | all-to-all | bytes 663552 | tf_op jit(solution)/shard_map/all_to_all | solution.py:20
  113.5 0.1 convert_reduce_fusion.2
  113.8 0.1 reduce_sum.72
  114.0 0.8 multiply_subtract_fusion
  (55 shorter events, 1.6 us)
Async XLA Ops:
  1.6 16.2 %collective-permute-start.2 = (bf16[2,64,384]{2,1,0:T(8,128)(2,1)S(1)}, bf16[2,64,384]{2,1,0:T(8,128)(2,1)S(1)}, u32[]{:S(2)}, u32[]{:S(2)}) collective-permute-start(bf16[2,64,384]{2,1,0:T(8,128)(2,1)S(1)} %fusion.19), channel_id=1, source_target_pairs={{6,12},{12,6},{18,24},{24,18},{30,36},{36,30},{42,48},{48,42},{54,... | collective-permute-start | bytes 294920 | tf_op jit(solution)/shard_map/ppermute | solution.py:35
  2.3 15.6 %collective-permute-start.3 = (bf16[2,64,384]{2,1,0:T(8,128)(2,1)S(1)}, bf16[2,64,384]{2,1,0:T(8,128)(2,1)S(1)}, u32[]{:S(2)}, u32[]{:S(2)}) collective-permute-start(bf16[2,64,384]{2,1,0:T(8,128)(2,1)S(1)} %fusion.19), channel_id=1, source_target_pairs={{0,6},{6,0},{12,18},{18,12},{24,30},{30,24},{36,42},{42,36},{48,54... | collective-permute-start | bytes 294920 | tf_op jit(solution)/shard_map/ppermute | solution.py:36
  8.9 17.3 %collective-permute-start.1 = (bf16[2,384,384]{2,1,0:T(8,128)(2,1)}, bf16[2,384,384]{2,1,0:T(8,128)(2,1)S(1)}, u32[]{:S(2)}, u32[]{:S(2)}) collective-permute-start(bf16[2,384,384]{2,1,0:T(8,128)(2,1)} %param.9), channel_id=1, source_target_pairs={{0,1},{1,0},{2,3},{3,2},{4,5},{5,4},{6,7},{7,6},{8,9},{9,8},{10,11... | collective-permute-start | bytes 1769480 | tf_op jit(solution)/shard_map/ppermute | solution.py:112
  18.1 5.8 %copy-start.1 = (bf16[2,2,384,384]{3,2,1,0:T(8,128)(2,1)S(1)}, bf16[2,2,384,384]{3,2,1,0:T(8,128)(2,1)}, u32[]{:S(2)}) copy-start(bf16[2,2,384,384]{3,2,1,0:T(8,128)(2,1)} %param.8) | copy-start | bytes 3538948
  19.1 12.3 %all-to-all-start = ((bf16[6,64,384]{2,1,0:T(8,128)(2,1)}), bf16[6,64,384]{2,1,0:T(8,128)(2,1)S(1)}, u32[]{:S(2)}, u32[]{:S(2)}) async-start(bf16[6,64,384]{2,1,0:T(8,128)(2,1)} %fusion.12), calls=%async_computation | async-start | bytes 589824 | tf_op jit(solution)/shard_map/all_to_all | solution.py:20
  23.9 2.3 %copy-start.2 = (bf16[2,384,384]{2,1,0:T(8,128)(2,1)S(1)}, bf16[2,384,384]{2,1,0:T(8,128)(2,1)}, u32[]{:S(2)}) copy-start(bf16[2,384,384]{2,1,0:T(8,128)(2,1)} %param.9) | copy-start | bytes 1769476
  24.0 4.0 %collective-permute-start = (bf16[2,384,384]{2,1,0:T(8,128)(2,1)S(1)}, bf16[2,384,384]{2,1,0:T(8,128)(2,1)S(1)}, u32[]{:S(2)}, u32[]{:S(2)}) collective-permute-start(bf16[2,384,384]{2,1,0:T(8,128)(2,1)S(1)} %get-tuple-element.24), channel_id=1, source_target_pairs={{0,1},{1,0},{2,3},{3,2},{4,5},{5,4},{6,7},{7,6},{8,9},{9,8},{10,11... | collective-permute-start | bytes 1769480 | tf_op jit(solution)/shard_map/ppermute | solution.py:111
  31.4 12.1 %copy-start.3 = (bf16[2,64,384]{2,1,0:T(8,128)(2,1)S(1)}, bf16[2,64,384]{2,1,0:T(8,128)(2,1)}, u32[]{:S(2)}) copy-start(bf16[2,64,384]{2,1,0:T(8,128)(2,1)} %param.5) | copy-start | bytes 294916
  31.4 12.1 %copy-start.5 = (s32[2]{0:T(128)S(1)}, s32[2]{0:T(128)}, u32[]{:S(2)}) copy-start(s32[2]{0:T(128)} %param.6) | copy-start | bytes 28
  43.6 70.4 %copy-start = (f32[2,64,384]{2,1,0:T(8,128)}, f32[2,64,384]{2,1,0:T(8,128)S(1)}, u32[]{:S(2)}) copy-start(f32[2,64,384]{2,1,0:T(8,128)S(1)} %get-tuple-element.22) | copy-start | bytes 589828
  44.4 22.2 %all-to-all-start.2 = ((f32[64,2,128]{2,1,0:T(2,128)}), f32[64,2,128]{2,1,0:T(2,128)S(1)}, u32[]{:S(2)}, u32[]{:S(2)}) async-start(f32[64,2,128]{2,1,0:T(2,128)} %broadcast_in_dim.14), calls=%async_computation.2 | async-start | bytes 131072 | tf_op jit(solution)/shard_map/all_to_all | solution.py:20
  56.7 11.9 %collective-permute-start.4 = (bf16[2,64,384]{2,1,0:T(8,128)(2,1)S(1)}, bf16[2,64,384]{2,1,0:T(8,128)(2,1)S(1)}, u32[]{:S(2)}, u32[]{:S(2)}) collective-permute-start(bf16[2,64,384]{2,1,0:T(8,128)(2,1)S(1)} %convert_element_type.55), channel_id=1, source_target_pairs={{0,6},{6,0},{12,18},{18,12},{24,30},{30,24},{36,42},{42,36},{48,54... | collective-permute-start | bytes 294920 | tf_op jit(solution)/shard_map/ppermute | solution.py:36
  60.0 8.6 %collective-permute-start.5 = (bf16[2,64,384]{2,1,0:T(8,128)(2,1)S(1)}, bf16[2,64,384]{2,1,0:T(8,128)(2,1)S(1)}, u32[]{:S(2)}, u32[]{:S(2)}) collective-permute-start(bf16[2,64,384]{2,1,0:T(8,128)(2,1)S(1)} %convert_element_type.55), channel_id=1, source_target_pairs={{6,12},{12,6},{18,24},{24,18},{30,36},{36,30},{42,48},{48,42},{54,... | collective-permute-start | bytes 294920 | tf_op jit(solution)/shard_map/ppermute | solution.py:35
  66.5 0.6 copy-start.4
  68.8 4.8 %copy-start.6 = (f32[2,128]{1,0:T(2,128)S(1)}, f32[2,128]{1,0:T(2,128)}, u32[]{:S(2)}) copy-start(f32[2,128]{1,0:T(2,128)} %shard_map.68) | copy-start | bytes 3076
  69.8 27.6 %all-to-all-start.3 = ((bf16[6,64,384]{2,1,0:T(8,128)(2,1)}), bf16[6,64,384]{2,1,0:T(8,128)(2,1)S(1)}, u32[]{:S(2)}, u32[]{:S(2)}) async-start(bf16[6,64,384]{2,1,0:T(8,128)(2,1)} %fusion.7), calls=%async_computation.3 | async-start | bytes 589824 | tf_op jit(solution)/shard_map/all_to_all | solution.py:20
  73.6 26.3 %collective-permute-start.6 = (f32[2,128]{1,0:T(2,128)S(1)}, f32[2,128]{1,0:T(2,128)S(1)}, u32[]{:S(2)}, u32[]{:S(2)}) collective-permute-start(f32[2,128]{1,0:T(2,128)S(1)} %copy-done.6), channel_id=1, source_target_pairs={{0,192},{192,384},{384,576},{576,0},{1,385},{193,577},{385,1},{577... | collective-permute-start | bytes 3080 | tf_op jit(solution)/shard_map/ppermute | solution.py:83
  96.7 3.2 %collective-permute-start.7 = (f32[2,128]{1,0:T(2,128)S(1)}, f32[2,128]{1,0:T(2,128)S(1)}, u32[]{:S(2)}, u32[]{:S(2)}) collective-permute-start(f32[2,128]{1,0:T(2,128)S(1)} %copy-done.6), channel_id=1, source_target_pairs={{0,576},{192,0},{384,192},{576,384},{2,578},{194,2},{386,194},{578... | collective-permute-start | bytes 3080 | tf_op jit(solution)/shard_map/ppermute | solution.py:84
